TPU v7x, 128 devices: a whole 4x4x4 slice. The times are simulated.
128 devices in a mesh: shard: 16 (over x_hi, y, core), replica: 8 (over x_lo, z).
Axes of the slice: x: 4 (x_hi: 2, x_lo: 2; x = x_hi * 2 + x_lo), y: 4, z: 4, core: 2. Of those that a mesh axis runs over, the one named last changes fastest.
Arguments:
- tokens: bfloat16 [24576, 1024], P(('shard', 'replica')), may hold values from -6 to 6
- seq_lengths: int32 [128, 2], P(('shard', 'replica')), may hold values from 32 to 160, as said below
- routes: int32 [24576, 8], P(('shard', 'replica')), may hold values from 0 to 15, all different within a row; in each aligned block of 192 rows (0 to 191, 192 to 383, ...) at most 120 rows name the same one
- attn_gain: bfloat16 [1024], replicated, may hold values from 0.5 to 1.5
- ffn_gain: bfloat16 [1024], replicated, may hold values from 0.5 to 1.5
- w_query: bfloat16 [1024, 1024], P('shard'), may hold values from -0.1875 to 0.1875
- key_projection: bfloat16 [1024, 512], P('shard'), may hold values from -0.1875 to 0.1875
- value_projection: bfloat16 [1024, 512], P('shard'), may hold values from -0.1875 to 0.1875
- w_output: bfloat16 [1024, 1024], P('shard'), may hold values from -1.5 to 1.5
- w_router: bfloat16 [1024, 16], P('shard'), may hold values from -0.09375 to 0.09375
- w_in: bfloat16 [16, 1024, 1024], P('shard'), may hold values from -0.1875 to 0.1875
- w_out: bfloat16 [16, 512, 1024], P('shard'), may hold values from -1 to 1
- cotangent: bfloat16 [24576, 1024], P(('shard', 'replica')), may hold values from -6 to 6
Outputs:
- output: bfloat16 [24576, 1024], P(('shard', 'replica'))
- d_tokens: float32 [24576, 1024], P(('shard', 'replica'))
- d_attn_gain: float32 [1024], replicated
- d_ffn_gain: float32 [1024], replicated
- d_query: float32 [1024, 1024], P('shard')
- d_key: float32 [1024, 512], P('shard')
- d_value: float32 [1024, 512], P('shard')
- d_output: float32 [1024, 1024], P('shard')
- d_router: float32 [1024, 16], P('shard')
- d_in: float32 [16, 1024, 1024], P('shard')
- d_out: float32 [16, 512, 1024], P('shard')
Inputs may be any that keep to these rules, and one draw needn't show every extreme that they name: `seq_lengths`: row b holds the lengths of the 2 sequences dealt to block b, laid end to end from its first row; they sum to at most 192, the rest of the block is padding, and some block is full. `routes`: each row names 8 different experts; in each aligned block of 192 rows no expert is named by more than 120 rows.
All inputs are finite; a program needn't handle non-finite values.
Results may differ from a plain program's by a relative error of at most 0.023.
Values may be sent and summed in bfloat16 or wider, within the bound.
A program may use at most 128 MiB of HBM per device.

v0:
```python
import math

import jax
import jax.numpy as jnp
from jax import lax
from jax.sharding import PartitionSpec as P

QUERY_HEADS = 16
KEY_VALUE_HEADS = 8
HEAD_SIZE = 64
TOP = 8
E = 16
CAP = 120


EPS = 1e-06
ROPE_BASE = 10000.0
NEGATIVE = -1e30


def norm_apply(value_rows, gain_vec):
    return (
        value_rows
        * lax.rsqrt(jnp.mean(value_rows * value_rows, axis=1, keepdims=True) + EPS)
        * gain_vec
    )


def layout(lengths, count_of_rows):
    row_index = jnp.arange(count_of_rows, dtype=jnp.int32)
    first_len = lengths[0]
    total_len = lengths[0] + lengths[1]
    doc_index = jnp.where(row_index < first_len, 0, jnp.where(row_index < total_len, 1, 2)).astype(
        jnp.int32
    )
    doc_start = jnp.where(
        row_index < first_len, 0, jnp.where(row_index < total_len, first_len, total_len)
    )
    allowed = (doc_index[:, None] == doc_index[None, :]) & (
        row_index[None, :] <= row_index[:, None]
    )
    return (row_index - doc_start, row_index < total_len, allowed)


def tables(position, head_dim):
    half_dim = head_dim // 2
    frequency = jnp.exp(
        jnp.arange(half_dim, dtype=jnp.float32) * (-2.0 * math.log(ROPE_BASE) / head_dim)
    )
    angles = position.astype(jnp.float32)[:, None] * frequency[None, :]
    return (jnp.cos(angles), jnp.sin(angles))


def rotary_apply(value_rows, cosine_table, sine_lookup, head_count, head_dim):
    count_of_rows = value_rows.shape[0]
    halves = value_rows.reshape(count_of_rows, head_count, 2, head_dim // 2)
    first_half = halves[:, :, 0]
    second = halves[:, :, 1]
    cos_rows = cosine_table[:, None, :]
    sin_rows = sine_lookup[:, None, :]
    turned = jnp.stack(
        [first_half * cos_rows - second * sin_rows, second * cos_rows + first_half * sin_rows],
        axis=2,
    )
    return turned.reshape(count_of_rows, head_count * head_dim)


def smooth_gate(value_rows):
    return value_rows * jax.nn.sigmoid(value_rows)


def gated(gate_part, up_part):
    return smooth_gate(gate_part) * up_part


def softmax_last(score_matrix):
    largest = jnp.max(score_matrix, axis=-1, keepdims=True)
    shifted = jnp.exp(score_matrix - largest)
    return shifted / jnp.sum(shifted, axis=-1, keepdims=True)


def slots(routes, experts, capacity):
    flat_routes = routes.reshape(-1)
    onehot = (flat_routes[:, None] == jnp.arange(experts, dtype=jnp.int32)[None, :]).astype(
        jnp.int32
    )
    route_rank = jnp.sum((jnp.cumsum(onehot, axis=0) - 1) * onehot, axis=1)
    slot_index = flat_routes * capacity + route_rank
    source = (
        jnp.zeros((experts * capacity,), jnp.int32)
        .at[slot_index]
        .set(jnp.arange(flat_routes.shape[0], dtype=jnp.int32))
    )
    filled = jnp.zeros((experts * capacity,), jnp.int32).at[slot_index].set(1)
    return (slot_index, source, filled)


def scores_of(heads_of_query, heads_of_key, allowed, scale):
    raw_scores = (
        jnp.einsum(
            "ehla,jha->hlej", heads_of_query, heads_of_key, preferred_element_type=jnp.float32
        )
        * scale
    )
    return jnp.where(allowed, raw_scores, NEGATIVE)


def local(
    tokens,
    seq_lengths,
    routes,
    attn_gain,
    ffn_gain,
    w_query,
    key_projection,
    value_projection,
    w_output,
    w_router,
    w_in,
    w_out,
    cotangent,
):
    count_of_rows = tokens.shape[0]
    width = tokens.shape[1]
    groups = lax.axis_size("shard")
    owned = w_in.shape[0]
    hidden_units = w_out.shape[1]
    replica_group_size = QUERY_HEADS // KEY_VALUE_HEADS
    scale = HEAD_SIZE ** (-0.5)
    position, live_rows, allowed = layout(seq_lengths[0], count_of_rows)
    live_mask = live_rows.astype(jnp.float32)[:, None]
    cosine_table, sine_lookup = tables(position, HEAD_SIZE)
    gain_first = attn_gain.astype(jnp.float32)
    gain_second = ffn_gain.astype(jnp.float32)
    inputs = tokens.astype(jnp.float32)
    first_normalized = norm_apply(inputs, gain_first).astype(jnp.bfloat16)
    full_query, full_key, full_value, full_output, full_router = (
        lax.all_gather(w_query, "shard", axis=0, tiled=True),
        lax.all_gather(key_projection, "shard", axis=0, tiled=True),
        lax.all_gather(value_projection, "shard", axis=0, tiled=True),
        lax.all_gather(w_output, "shard", axis=0, tiled=True),
        lax.all_gather(w_router, "shard", axis=0, tiled=True),
    )
    query_matrix = rotary_apply(
        jnp.dot(first_normalized, full_query, preferred_element_type=jnp.float32),
        cosine_table,
        sine_lookup,
        QUERY_HEADS,
        HEAD_SIZE,
    ).astype(jnp.bfloat16)
    key_rows = rotary_apply(
        jnp.dot(first_normalized, full_key, preferred_element_type=jnp.float32),
        cosine_table,
        sine_lookup,
        KEY_VALUE_HEADS,
        HEAD_SIZE,
    ).astype(jnp.bfloat16)
    value_rows = jnp.dot(first_normalized, full_value, preferred_element_type=jnp.float32).astype(
        jnp.bfloat16
    )
    heads_of_query = query_matrix.reshape(
        count_of_rows, KEY_VALUE_HEADS, replica_group_size, HEAD_SIZE
    )
    heads_of_key = key_rows.reshape(count_of_rows, KEY_VALUE_HEADS, HEAD_SIZE)
    heads_of_value = value_rows.reshape(count_of_rows, KEY_VALUE_HEADS, HEAD_SIZE)
    score_matrix = scores_of(heads_of_query, heads_of_key, allowed, scale)
    largest = jnp.max(score_matrix, axis=-1, keepdims=True)
    log_total = largest + jnp.log(jnp.sum(jnp.exp(score_matrix - largest), axis=-1, keepdims=True))
    attention_probability = jnp.exp(score_matrix - log_total).astype(jnp.bfloat16)
    mixture_heads = (
        jnp.einsum(
            "pjwi,ipx->wpjx",
            attention_probability,
            heads_of_value,
            preferred_element_type=jnp.float32,
        )
        .reshape(count_of_rows, QUERY_HEADS * HEAD_SIZE)
        .astype(jnp.bfloat16)
    )
    attn_out = jnp.dot(mixture_heads, full_output, preferred_element_type=jnp.float32)
    hidden_one = inputs + live_mask * attn_out
    normed_second = norm_apply(hidden_one, gain_second).astype(jnp.bfloat16)
    logits = jnp.dot(normed_second, full_router, preferred_element_type=jnp.float32)
    route_pick = (routes[:, :, None] == jnp.arange(E, dtype=jnp.int32)[None, None, :]).astype(
        jnp.float32
    )
    chosen = jnp.sum(route_pick * logits[:, None, :], axis=2)
    gate_values = softmax_last(chosen)
    slot_index, source, filled = slots(routes, E, CAP)
    fill_mask = filled.astype(jnp.bfloat16)[:, None]
    expert_rows = (normed_second[source // TOP] * fill_mask).reshape(groups, owned, CAP, width)
    arrived = lax.all_to_all(expert_rows, "shard", split_axis=0, concat_axis=0, tiled=True)
    pre_act = jnp.einsum("sekd,edf->sekf", arrived, w_in, preferred_element_type=jnp.float32)
    activation = gated(pre_act[..., :hidden_units], pre_act[..., hidden_units:]).astype(
        jnp.bfloat16
    )
    result = jnp.einsum(
        "sekh,ehd->sekd", activation, w_out, preferred_element_type=jnp.float32
    ).astype(jnp.bfloat16)
    returned = lax.all_to_all(result, "shard", split_axis=0, concat_axis=0, tiled=True)
    per_route = (
        returned.reshape(E * CAP, width)[slot_index]
        .reshape(count_of_rows, TOP, width)
        .astype(jnp.float32)
    )
    expert_mix = jnp.sum(gate_values[:, :, None] * per_route, axis=1)
    output = (hidden_one + live_mask * expert_mix).astype(jnp.bfloat16)
    upstream = cotangent.astype(jnp.float32)
    back_query, back_key, back_value, back_output, back_router = (
        lax.all_gather(w_query, "shard", axis=0, tiled=True),
        lax.all_gather(key_projection, "shard", axis=0, tiled=True),
        lax.all_gather(value_projection, "shard", axis=0, tiled=True),
        lax.all_gather(w_output, "shard", axis=0, tiled=True),
        lax.all_gather(w_router, "shard", axis=0, tiled=True),
    )
    mix_grad = live_mask * upstream
    gate_grad = jnp.sum(per_route * mix_grad[:, None, :], axis=2)
    chosen_grad = gate_values * (
        gate_grad - jnp.sum(gate_values * gate_grad, axis=1, keepdims=True)
    )
    logit_grad = jnp.sum(route_pick * chosen_grad[:, :, None], axis=1).astype(jnp.bfloat16)
    route_grad = (
        (gate_values[:, :, None] * mix_grad[:, None, :])
        .astype(jnp.bfloat16)
        .reshape(count_of_rows * TOP, width)
    )
    slot_grad = (route_grad[source] * fill_mask).reshape(groups, owned, CAP, width)
    arrived_grad = lax.all_to_all(slot_grad, "shard", split_axis=0, concat_axis=0, tiled=True)
    pre_again = jnp.einsum("sekd,edf->sekf", arrived, w_in, preferred_element_type=jnp.float32)
    activation_full, gate_back = jax.vjp(
        gated, pre_again[..., :hidden_units], pre_again[..., hidden_units:]
    )
    activation = activation_full.astype(jnp.bfloat16)
    activation_grad = jnp.einsum(
        "sekd,ehd->sekh", arrived_grad, w_out, preferred_element_type=jnp.float32
    )
    gate_part_grad, up_part_grad = gate_back(activation_grad)
    pre_grad = jnp.concatenate([gate_part_grad, up_part_grad], axis=-1).astype(jnp.bfloat16)
    grad_in = jnp.einsum("sekd,sekf->edf", arrived, pre_grad, preferred_element_type=jnp.float32)
    grad_out = jnp.einsum(
        "sekh,sekd->ehd", activation, arrived_grad, preferred_element_type=jnp.float32
    )
    row_grad = jnp.einsum(
        "sekf,edf->sekd", pre_grad, w_in, preferred_element_type=jnp.float32
    ).astype(jnp.bfloat16)
    back_rows = lax.all_to_all(row_grad, "shard", split_axis=0, concat_axis=0, tiled=True)
    normed_second_grad = jnp.sum(
        back_rows.reshape(E * CAP, width)[slot_index]
        .reshape(count_of_rows, TOP, width)
        .astype(jnp.float32),
        axis=1,
    )
    normed_second_grad = normed_second_grad + jnp.einsum(
        "te,de->td", logit_grad, back_router, preferred_element_type=jnp.float32
    )
    router_grad = jnp.einsum(
        "td,te->de", normed_second, logit_grad, preferred_element_type=jnp.float32
    )
    norm_second_value, norm_second_back = jax.vjp(norm_apply, hidden_one, gain_second)
    hidden_norm_grad, second_gain_grad = norm_second_back(normed_second_grad)
    hidden_grad = upstream + hidden_norm_grad
    attn_grad = (live_mask * hidden_grad).astype(jnp.bfloat16)
    mixture_gradient = jnp.einsum(
        "td,cd->tc", attn_grad, back_output, preferred_element_type=jnp.float32
    ).astype(jnp.bfloat16)
    output_grad = jnp.einsum(
        "tc,td->cd", mixture_heads, attn_grad, preferred_element_type=jnp.float32
    )
    mixture_gradient_heads = mixture_gradient.reshape(
        count_of_rows, KEY_VALUE_HEADS, replica_group_size, HEAD_SIZE
    )
    scores_again = scores_of(heads_of_query, heads_of_key, allowed, scale)
    attn_soft = jnp.exp(scores_again - log_total)
    probability_recomputed = attn_soft.astype(jnp.bfloat16)
    prob_grad = jnp.einsum(
        "ehla,jha->hlej", mixture_gradient_heads, heads_of_value, preferred_element_type=jnp.float32
    )
    value_grad = (
        jnp.einsum(
            "uqeh,euqz->huz",
            probability_recomputed,
            mixture_gradient_heads,
            preferred_element_type=jnp.float32,
        )
        .reshape(count_of_rows, KEY_VALUE_HEADS * HEAD_SIZE)
        .astype(jnp.bfloat16)
    )
    row_dot = jnp.sum(attn_soft * prob_grad, axis=-1, keepdims=True)
    score_gradient = (attn_soft * (prob_grad - row_dot)).astype(jnp.bfloat16)
    query_turned = (
        jnp.einsum(
            "pjwi,ipx->wpjx", score_gradient, heads_of_key, preferred_element_type=jnp.float32
        ).reshape(count_of_rows, QUERY_HEADS * HEAD_SIZE)
        * scale
    )
    query_grad = rotary_apply(
        query_turned, cosine_table, -sine_lookup, QUERY_HEADS, HEAD_SIZE
    ).astype(jnp.bfloat16)
    key_rotated = (
        jnp.einsum(
            "uqeh,euqz->huz", score_gradient, heads_of_query, preferred_element_type=jnp.float32
        ).reshape(count_of_rows, KEY_VALUE_HEADS * HEAD_SIZE)
        * scale
    )
    key_gradient = rotary_apply(
        key_rotated, cosine_table, -sine_lookup, KEY_VALUE_HEADS, HEAD_SIZE
    ).astype(jnp.bfloat16)
    normed_first_grad = jnp.einsum(
        "tc,dc->td", query_grad, back_query, preferred_element_type=jnp.float32
    )
    normed_first_grad = normed_first_grad + jnp.einsum(
        "tc,dc->td", key_gradient, back_key, preferred_element_type=jnp.float32
    )
    normed_first_grad = normed_first_grad + jnp.einsum(
        "tc,dc->td", value_grad, back_value, preferred_element_type=jnp.float32
    )
    query_weight_grad = jnp.einsum(
        "td,tc->dc", first_normalized, query_grad, preferred_element_type=jnp.float32
    )
    key_weight_grad = jnp.einsum(
        "td,tc->dc", first_normalized, key_gradient, preferred_element_type=jnp.float32
    )
    value_weight_grad = jnp.einsum(
        "td,tc->dc", first_normalized, value_grad, preferred_element_type=jnp.float32
    )
    norm_first_value, norm_first_back = jax.vjp(norm_apply, inputs, gain_first)
    input_norm_grad, first_gain_grad = norm_first_back(normed_first_grad)
    input_grad = hidden_grad + input_norm_grad
    part_query, part_key, part_value, part_output, part_router = (
        lax.psum_scatter(
            query_weight_grad.astype(jnp.bfloat16), "shard", scatter_dimension=0, tiled=True
        ).astype(jnp.float32),
        lax.psum_scatter(
            key_weight_grad.astype(jnp.bfloat16), "shard", scatter_dimension=0, tiled=True
        ).astype(jnp.float32),
        lax.psum_scatter(
            value_weight_grad.astype(jnp.bfloat16), "shard", scatter_dimension=0, tiled=True
        ).astype(jnp.float32),
        lax.psum_scatter(
            output_grad.astype(jnp.bfloat16), "shard", scatter_dimension=0, tiled=True
        ).astype(jnp.float32),
        lax.psum_scatter(
            router_grad.astype(jnp.bfloat16), "shard", scatter_dimension=0, tiled=True
        ).astype(jnp.float32),
    )
    total_query, total_key, total_value, total_output, total_router, total_in, total_out = (
        lax.psum(part_query.astype(jnp.bfloat16), "replica").astype(jnp.float32),
        lax.psum(part_key.astype(jnp.bfloat16), "replica").astype(jnp.float32),
        lax.psum(part_value.astype(jnp.bfloat16), "replica").astype(jnp.float32),
        lax.psum(part_output.astype(jnp.bfloat16), "replica").astype(jnp.float32),
        lax.psum(part_router.astype(jnp.bfloat16), "replica").astype(jnp.float32),
        lax.psum(grad_in.astype(jnp.bfloat16), "replica").astype(jnp.float32),
        lax.psum(grad_out.astype(jnp.bfloat16), "replica").astype(jnp.float32),
    )
    first_gain_total, second_gain_total = lax.psum(
        (first_gain_grad, second_gain_grad), ("shard", "replica")
    )
    return (
        output,
        input_grad,
        first_gain_total,
        second_gain_total,
        total_query,
        total_key,
        total_value,
        total_output,
        total_router,
        total_in,
        total_out,
    )


def solution(mesh):
    return jax.shard_map(
        local,
        mesh=mesh,
        in_specs=(
            P(("shard", "replica"), None),
            P(("shard", "replica"), None),
            P(("shard", "replica"), None),
            P(),
            P(),
            P("shard", None),
            P("shard", None),
            P("shard", None),
            P("shard", None),
            P("shard", None),
            P("shard", None, None),
            P("shard", None, None),
            P(("shard", "replica"), None),
        ),
        out_specs=(
            P(("shard", "replica"), None),
            P(("shard", "replica"), None),
            P(),
            P(),
            P("shard", None),
            P("shard", None),
            P("shard", None),
            P("shard", None),
            P("shard", None),
            P("shard", None, None),
            P("shard", None, None),
        ),
        check_vma=False,
    )
```

profile of v0, /device:TPU:8, one launch (start us, length us, event | category | flops | bytes accessed | tf_op | source)
XLA Modules:
  0.0 997.0 jit_solution(768086674232008244)
XLA Ops:
  10.0 1.3 fusion.78
  15.3 4.5 reduce-window.6
  20.7 6.2 scatter_custom_fusion
  28.3 20.3 %all-gather = bf16[16,64,16]{1,2,0:T(8,128)(2,1)S(1)} all-gather(bf16[1,64,16]{1,2,0:T(8,128)(2,1)} %bitcast.246), channel_id=1, replica_groups=mesh['shard'=16,'replica'=8] {'shard'}, dimensions={0}, use_global_device_ids=true | all-gather | bytes 34816 | tf_op jit(solution)/shard_map/all_gather | solution.py:142
  48.7 6.4 scatter_custom_fusion.1
  56.4 1.2 fusion.45
  59.2 1.0 convert_multiply_fusion.6
  60.2 1.6 convolution_convert_fusion.6
  62.0 41.3 %all-gather.8.cloned.1.call-done = bf16[1024,512]{1,0:T(8,128)(2,1)} async-done(((bf16[64,512]{1,0:T(8,128)(2,1)}), bf16[1024,512]{1,0:T(8,128)(2,1)}) %all-gather.8.cloned.1.call-update) | async-done | bytes 1048592 | tf_op jit(solution)/shard_map/all_gather | solution.py:139
  103.3 1.8 fusion.75
  106.0 46.1 %all-gather.10.cloned.1.call-done = bf16[1024,1024]{1,0:T(8,128)(2,1)} async-done(((bf16[64,1024]{1,0:T(8,128)(2,1)}), bf16[1024,1024]{1,0:T(8,128)(2,1)}) %all-gather.10.cloned.1.call-update) | async-done | bytes 2097168 | tf_op jit(solution)/shard_map/all_gather | solution.py:138
  152.1 2.6 fusion.73
  156.3 1.1 copy-done.2
  157.4 1.4 convolution_convert_fusion.4
  158.9 41.8 %all-gather.12.cloned.1.call-done = bf16[1024,1024]{1,0:T(8,128)(2,1)} async-done(((bf16[64,1024]{1,0:T(8,128)(2,1)}), bf16[1024,1024]{1,0:T(8,128)(2,1)}) %all-gather.12.cloned.1.call-update) | async-done | bytes 2097168 | tf_op jit(solution)/shard_map/all_gather | solution.py:141
  200.7 2.5 multiply_reduce_fusion.2
  207.8 7.4 gather_fusion
  215.2 3.2 fusion.2
  218.5 12.3 %gather_fusion.2 = bf16[1920,1024]{1,0:T(8,128)(2,1)} fusion(bf16[1536,1024]{1,0:T(8,128)(2,1)} %fusion.2, s32[2048]{0:T(1024)} %get-tuple-element.57), kind=kCustom, calls=%fused_computation.2 | custom fusion | bytes 7872000 | tf_op jit(solution)/shard_map/gather | solution.py:227
  230.7 4.9 broadcast_multiply_fusion
  235.7 50.7 %all_to_all.20 = bf16[16,1,120,1024]{3,2,1,0:T(8,128)(2,1)} all-to-all(bf16[16,1,120,1024]{3,2,1,0:T(8,128)(2,1)S(1)} %get-tuple-element.41), channel_id=1, replica_groups=mesh['shard'=16,'replica'=8] {'shard'}, dimensions={0} | all-to-all | bytes 7864320 | tf_op jit(solution)/shard_map/all_to_all | solution.py:192
  286.4 7.4 all-to-all-start.2
  293.7 8.5 fusion.19
  302.2 46.1 %all-to-all-done.2 = bf16[16,1,120,1024]{3,2,1,0:T(8,128)(2,1)} async-done(((bf16[16,1,120,1024]{3,2,1,0:T(8,128)(2,1)}), bf16[16,1,120,1024]{3,2,1,0:T(8,128)(2,1)}, u32[]{:S(2)}, u32[]{:S(2)}) %all-to-all-start.2) | async-done | bytes 3932192 | tf_op jit(solution)/shard_map/all_to_all | solution.py:228
  348.4 10.0 fusion.28
  358.3 1.3 copy-done.49
  360.3 6.0 convert_bitcast_fusion
  366.3 8.7 all-to-all-start.3
  374.9 5.6 convert_bitcast_fusion.1
  380.6 49.6 %all-to-all-done.3 = bf16[16,1,120,1024]{3,2,1,0:T(8,128)(2,1)} async-done(((bf16[16,1,120,1024]{3,2,1,0:T(8,128)(2,1)}), bf16[16,1,120,1024]{3,2,1,0:T(8,128)(2,1)}, u32[]{:S(2)}, u32[]{:S(2)}) %all-to-all-start.3) | async-done | bytes 3932192 | tf_op jit(solution)/shard_map/all_to_all | solution.py:246
  430.2 8.5 all-to-all-start.1
  439.3 10.4 %gather_fusion.3 = bf16[1536,1024]{1,0:T(8,128)(2,1)} fusion(bf16[1920,1024]{1,0:T(8,128)(2,1)} %bitcast.50, s32[2048]{0:T(1024)S(1)} %pad_clamp_fusion.1), kind=kCustom, calls=%fused_computation.3 | custom fusion | bytes 6297600 | tf_op jit(solution)/shard_map/gather | solution.py:248
  449.7 5.3 convert_reduce_fusion
  454.9 39.1 %all-to-all-done.1 = bf16[16,1,120,1024]{3,2,1,0:T(8,128)(2,1)} async-done(((bf16[16,1,120,1024]{3,2,1,0:T(8,128)(2,1)}), bf16[16,1,120,1024]{3,2,1,0:T(8,128)(2,1)}, u32[]{:S(2)}, u32[]{:S(2)}) %all-to-all-start.1) | async-done | bytes 3932192 | tf_op jit(solution)/shard_map/all_to_all | solution.py:200
  494.0 10.5 %gather_fusion.1 = bf16[1536,1024]{1,0:T(8,128)(2,1)} fusion(bf16[1920,1024]{1,0:T(8,128)(2,1)} %bitcast.33, s32[2048]{0:T(1024)S(1)} %pad_clamp_fusion.1), kind=kCustom, calls=%fused_computation.1 | custom fusion | bytes 6297600 | tf_op jit(solution)/shard_map/gather | solution.py:202
  504.5 5.3 fusion.1
  512.1 1.8 multiply_reduce_fusion
  514.5 2.2 convert_add_fusion.1
  516.8 0.9 convolution_convert_fusion.5
  517.9 2.6 fusion.37
  520.5 1.6 convolution_convert_fusion.2
  522.3 2.9 fusion.16
  527.5 1.6 convolution_convert_fusion.3
  529.2 3.2 convolution_convert_fusion
  533.2 2.2 convolution_convert_fusion.1
  535.5 9.4 fusion.23
  545.1 0.8 copy.120
  546.0 5.5 fusion.33
  551.5 39.9 %reduce-scatter.12.cloned.1.call-done = bf16[64,512]{1,0:T(8,128)(2,1)} async-done(((bf16[1024,512]{1,0:T(8,128)(2,1)}), bf16[64,512]{1,0:T(8,128)(2,1)}) %reduce-scatter.12.cloned.1.call-update) | async-done | bytes 65552 | tf_op jit(solution)/shard_map/reduce_scatter | solution.py:336
  591.3 70.0 %reduce-scatter.10.cloned.1.call-done = bf16[64,512]{1,0:T(8,128)(2,1)} async-done(((bf16[1024,512]{1,0:T(8,128)(2,1)}), bf16[64,512]{1,0:T(8,128)(2,1)}) %reduce-scatter.10.cloned.1.call-update) | async-done | bytes 65552 | tf_op jit(solution)/shard_map/reduce_scatter | solution.py:333
  661.3 74.5 %reduce-scatter.14.cloned.1.call-done = bf16[64,1024]{1,0:T(8,128)(2,1)} async-done(((bf16[1024,1024]{1,0:T(8,128)(2,1)}), bf16[64,1024]{1,0:T(8,128)(2,1)}) %reduce-scatter.14.cloned.1.call-update) | async-done | bytes 131088 | tf_op jit(solution)/shard_map/reduce_scatter | solution.py:339
  735.8 74.9 %reduce-scatter.8.cloned.1.call-done = bf16[64,1024]{1,0:T(8,128)(2,1)} async-done(((bf16[1024,1024]{1,0:T(8,128)(2,1)}), bf16[64,1024]{1,0:T(8,128)(2,1)}) %reduce-scatter.8.cloned.1.call-update) | async-done | bytes 131088 | tf_op jit(solution)/shard_map/reduce_scatter | solution.py:330
  810.8 0.9 fusion.85
  813.3 63.1 %all-reduce = (f32[1024]{0:T(1024)}, f32[1024]{0:T(1024)}) all-reduce(f32[1024]{0:T(1024)S(1)} %get-tuple-element.15, f32[1024]{0:T(1024)S(1)} %get-tuple-element.13), channel_id=1, replica_groups=mesh['shard'=16,'replica'=8] {'shard','replica'}, use_global_device_ids=true, to_apply=%region_21.22 | all-reduce | flops 2048 | bytes 16384 | tf_op jit(solution)/shard_map/psum | solution.py:355
  876.4 1.1 fusion.44
  877.5 1.6 reduce-scatter.16.cloned.1.call-done
  879.9 19.1 %psum.69 = bf16[64,16]{0,1:T(8,128)(2,1)S(1)} all-reduce(bf16[64,16]{0,1:T(8,128)(2,1)S(1)} %copy.121), channel_id=1, replica_groups=mesh['shard'=16,'replica'=8] {'replica'}, use_global_device_ids=true, to_apply=%region_33.34 | all-reduce | flops 1024 | bytes 4096 | tf_op jit(solution)/shard_map/psum | solution.py:351
  899.5 78.8 %all-reduce.4.cloned.1.call-done = (bf16[64,1024]{1,0:T(8,128)(2,1)}, bf16[64,512]{1,0:T(8,128)(2,1)}, bf16[64,512]{1,0:T(8,128)(2,1)}, bf16[64,1024]{1,0:T(8,12...) async-done(((bf16[64,1024]{1,0:T(8,128)(2,1)}, bf16[64,512]{1,0:T(8,128)(2,1)}, bf16[64,512]{1,0:T(8,128)(2,1)}, bf16[64,1024]{1,0:T(8,128)(2,1)}, ...) | async-done | bytes 3538960 | tf_op jit(solution)/shard_map/psum | solution.py:347
  978.3 1.8 convert_element_type.252
  980.0 1.5 convert_element_type.254
  981.6 1.5 convert_element_type.256
  983.1 1.6 convert_element_type.258
  984.7 2.8 convert_element_type.266
  987.5 2.5 convert_element_type.263
  (186 shorter events, 28.4 us)
Async XLA Ops:
  7.2 286.6 %copy-start = (bf16[1,1024,1024]{2,1,0:T(8,128)(2,1)S(1)}, bf16[1,1024,1024]{2,1,0:T(8,128)(2,1)}, u32[]{:S(2)}) copy-start(bf16[1,1024,1024]{2,1,0:T(8,128)(2,1)} %param.23) | copy-start | bytes 6291460
  7.2 53.0 %copy-start.4 = (bf16[192,1024]{1,0:T(8,128)(2,1)S(1)}, bf16[192,1024]{1,0:T(8,128)(2,1)}, u32[]{:S(2)}) copy-start(bf16[192,1024]{1,0:T(8,128)(2,1)} %param.13) | copy-start | bytes 1179652
  7.2 52.0 %copy-start.23 = (bf16[192,1024]{1,0:T(8,128)(2,1)S(1)}, bf16[192,1024]{1,0:T(8,128)(2,1)}, u32[]{:S(2)}) copy-start(bf16[192,1024]{1,0:T(8,128)(2,1)} %param.25) | copy-start | bytes 1179652
  7.2 52.9 %all-gather.6.cloned.1.call-start = ((), (), s32[]{:S(2)}) async-start(), calls=%async_computation.9 | async-start | bytes 1114112 | tf_op jit(solution)/shard_map/all_gather | solution.py:140
  8.0 95.4 %all-gather.8.cloned.1.call-start = ((), (), s32[]{:S(2)}) async-start(), calls=%async_computation.10 | async-start | bytes 1114112 | tf_op jit(solution)/shard_map/all_gather | solution.py:139
  8.7 143.4 %all-gather.10.cloned.1.call-start = ((), (), s32[]{:S(2)}) async-start(), calls=%async_computation.11 | async-start | bytes 2228224 | tf_op jit(solution)/shard_map/all_gather | solution.py:138
  9.4 191.3 %all-gather.12.cloned.1.call-start = ((), (), s32[]{:S(2)}) async-start(), calls=%async_computation.12 | async-start | bytes 2228224 | tf_op jit(solution)/shard_map/all_gather | solution.py:141
  12.6 188.1 %copy-start.37 = (f32[192]{0:T(256)}, f32[192]{0:T(256)S(1)}, u32[]{:S(2)}) copy-start(f32[192]{0:T(256)S(1)} %fusion.65) | copy-start | bytes 2308
  20.6 37.7 %copy-start.39 = (s32[1536]{0:T(1024)}, s32[1536]{0:T(1024)S(1)}, u32[]{:S(2)}) copy-start(s32[1536]{0:T(1024)S(1)} %fusion.58) | copy-start | bytes 18436
  27.6 124.5 %copy-start.30 = (f32[1024]{0:T(1024)}, f32[1024]{0:T(1024)S(1)}, u32[]{:S(2)}) copy-start(f32[1024]{0:T(1024)S(1)} %convert_element_type.212) | copy-start | bytes 12292
  28.3 175.0 %copy-start.36 = (f32[1024]{0:T(1024)}, f32[1024]{0:T(1024)S(1)}, u32[]{:S(2)}) copy-start(f32[1024]{0:T(1024)S(1)} %convert_element_type.222) | copy-start | bytes 12292
  48.7 155.5 %copy-start.26 = (bf16[1024,16]{0,1:T(8,128)(2,1)}, bf16[1024,16]{0,1:T(8,128)(2,1)S(1)}, u32[]{:S(2)}) copy-start(bf16[1024,16]{0,1:T(8,128)(2,1)S(1)} %reshape.535) | copy-start | bytes 98308
  57.6 0.7 copy-start.44
  57.6 94.5 %copy-start.34 = (f32[192]{0:T(256)}, f32[192]{0:T(256)S(1)}, u32[]{:S(2)}) copy-start(f32[192]{0:T(256)S(1)} %fusion.66) | copy-start | bytes 2308
  62.0 94.3 %copy-start.14 = (bf16[192,512]{0,1:T(8,128)(2,1)}, bf16[192,512]{0,1:T(8,128)(2,1)S(1)}, u32[]{:S(2)}) copy-start(bf16[192,512]{0,1:T(8,128)(2,1)S(1)} %copy.90) | copy-start | bytes 589828
  106.0 49.0 %copy-start.32 = (pred[192,192]{0,1:T(8,128)(4,1)S(1)}, pred[192,192]{0,1:T(8,128)(4,1)}, u32[]{:S(2)}) copy-start(pred[192,192]{0,1:T(8,128)(4,1)} %fusion.49) | copy-start | bytes 110596
  152.1 2.9 copy-start.18
  155.7 1.7 copy-start.2
  158.9 45.6 %copy-start.33 = (s32[192,8]{0,1:T(8,128)S(1)}, s32[192,8]{0,1:T(8,128)}, u32[]{:S(2)}) copy-start(s32[192,8]{0,1:T(8,128)} %param.15) | copy-start | bytes 18436
  203.2 0.9 copy-start.5
  203.2 1.4 copy-start.46
  203.2 1.3 copy-start.43
  204.5 0.6 copy-start.28
  204.5 0.6 copy-start.41
  205.1 0.6 copy-start.42
  286.4 62.0 %all-to-all-start.2 = ((bf16[16,1,120,1024]{3,2,1,0:T(8,128)(2,1)}), bf16[16,1,120,1024]{3,2,1,0:T(8,128)(2,1)}, u32[]{:S(2)}, u32[]{:S(2)}) async-start(bf16[16,1,120,1024]{3,2,1,0:T(8,128)(2,1)} %get-tuple-element.40), calls=%async_computation.2 | async-start | bytes 7864320 | tf_op jit(solution)/shard_map/all_to_all | solution.py:228
  358.3 1.3 copy-start.49
  358.3 1.9 copy-start.50
  366.3 8.7 copy-start.47
  366.3 63.9 %all-to-all-start.3 = ((bf16[16,1,120,1024]{3,2,1,0:T(8,128)(2,1)}), bf16[16,1,120,1024]{3,2,1,0:T(8,128)(2,1)}, u32[]{:S(2)}, u32[]{:S(2)}) async-start(bf16[16,1,120,1024]{3,2,1,0:T(8,128)(2,1)} %convert_bitcast_fusion), calls=%async_computation.3 | async-start | bytes 7864320 | tf_op jit(solution)/shard_map/all_to_all | solution.py:246
  380.6 58.7 %copy-start.40 = (s32[1536]{0:T(1024)S(1)}, s32[1536]{0:T(1024)}, u32[]{:S(2)}) copy-start(s32[1536]{0:T(1024)} %copy-done.39) | copy-start | bytes 18436
  430.2 63.8 %all-to-all-start.1 = ((bf16[16,1,120,1024]{3,2,1,0:T(8,128)(2,1)}), bf16[16,1,120,1024]{3,2,1,0:T(8,128)(2,1)}, u32[]{:S(2)}, u32[]{:S(2)}) async-start(bf16[16,1,120,1024]{3,2,1,0:T(8,128)(2,1)} %convert_bitcast_fusion.1), calls=%async_computation.1 | async-start | bytes 7864320 | tf_op jit(solution)/shard_map/all_to_all | solution.py:200
  438.7 152.6 %reduce-scatter.12.cloned.1.call-start = ((), (), s32[]{:S(2)}) async-start(), calls=%async_computation.15 | async-start | bytes 1114112 | tf_op jit(solution)/shard_map/reduce_scatter | solution.py:336
  494.0 10.5 %copy-start.11 = (f32[192,1024]{1,0:T(8,128)S(1)}, f32[192,1024]{1,0:T(8,128)}, u32[]{:S(2)}) copy-start(f32[192,1024]{1,0:T(8,128)} %convert_multiply_fusion.6) | copy-start | bytes 2359300
  504.4 7.6 copy-start.6
  504.5 7.6 copy-start.27
  504.5 10.1 %copy-start.24 = (bf16[192,1024]{1,0:T(8,128)(2,1)S(1)}, bf16[192,1024]{1,0:T(8,128)(2,1)}, u32[]{:S(2)}) copy-start(bf16[192,1024]{1,0:T(8,128)(2,1)} %param.25) | copy-start | bytes 1179652
  512.1 4.7 copy-start.9
  512.1 4.7 copy-start.38
  516.8 3.7 copy-start.7
  517.6 2.8 copy-start.31
  517.6 2.8 copy-start.35
  517.9 4.5 copy-start.15
  520.5 4.8 copy-start.20
  522.1 139.2 %reduce-scatter.10.cloned.1.call-start = ((), (), s32[]{:S(2)}) async-start(), calls=%async_computation.14 | async-start | bytes 1114112 | tf_op jit(solution)/shard_map/reduce_scatter | solution.py:333
  522.3 2.9 copy-start.3
  525.3 1.4 copy-start.29
  526.1 3.1 copy-start.12
  526.8 0.7 copy-start.16
  529.1 3.4 copy-start.19
  529.1 206.7 %reduce-scatter.14.cloned.1.call-start = ((), (), s32[]{:S(2)}) async-start(), calls=%async_computation.16 | async-start | bytes 2228224 | tf_op jit(solution)/shard_map/reduce_scatter | solution.py:339
  532.4 278.2 %reduce-scatter.8.cloned.1.call-start = ((), (), s32[]{:S(2)}) async-start(), calls=%async_computation.13 | async-start | bytes 2228224 | tf_op jit(solution)/shard_map/reduce_scatter | solution.py:330
  535.4 10.6 %copy-start.48 = (bf16[16,120,512]{2,1,0:T(8,128)(2,1)S(1)}, bf16[16,120,512]{2,1,0:T(8,128)(2,1)}, u32[]{:S(2)}) copy-start(bf16[16,120,512]{2,1,0:T(8,128)(2,1)} %get-tuple-element.27) | copy-start | bytes 5898244
  535.4 343.7 %reduce-scatter.16.cloned.1.call-start = ((), (), s32[]{:S(2)}) async-start(), calls=%async_computation.17 | async-start | bytes 278528
  545.9 432.3 %all-reduce.4.cloned.1.call-start = ((), (), s32[]{:S(2)}) async-start(), calls=%async_computation.18 | async-start | bytes 7077888 | tf_op jit(solution)/shard_map/psum | solution.py:347
  551.5 259.3 %copy-start.10 = (bf16[1024,1024]{1,0:T(8,128)(2,1)S(1)}, bf16[1024,1024]{1,0:T(8,128)(2,1)}, u32[]{:S(2)}) copy-start(bf16[1024,1024]{1,0:T(8,128)(2,1)} %all-gather.10.cloned.1.call-done) | copy-start | bytes 6291460
  810.7 0.9 copy-start.17
  810.7 1.3 copy-start.13
  810.7 1.8 copy-start.21
  810.7 1.8 copy-start.25
  812.0 64.4 %copy-start.45 = (f32[192]{0:T(256)S(1)}, f32[192]{0:T(256)}, u32[]{:S(2)}) copy-start(f32[192]{0:T(256)} %copy-done.44) | copy-start | bytes 2308
  812.0 64.4 %copy-start.8 = (f32[192,1024]{1,0:T(8,128)S(1)}, f32[192,1024]{1,0:T(8,128)}, u32[]{:S(2)}) copy-start(f32[192,1024]{1,0:T(8,128)} %copy-done.7) | copy-start | bytes 2359300
  978.3 9.2 copy-start.22
  987.5 2.5 copy-start.1
Sparse Core Ops, SparseCore 0:
  10.5 46.6 all-gather.5
  59.7 43.5 all-gather.7
  105.8 46.2 all-gather.9
  154.4 46.2 all-gather.11
  522.2 69.0 reduce-scatter.11
  595.4 65.8 reduce-scatter.9
  665.8 69.9 reduce-scatter.13
  740.8 69.8 reduce-scatter.7
  814.9 64.0 reduce-scatter.15
  881.9 96.2 all-reduce.3
where the time goes:
time: 1000 us; the launch traced here: 997 us
  waiting for transfers between devices  606 us (61%)
  blocking collectives  153 us (15%)
  matrix products  75.9 us (8%)
  local copies, waits for them, and re-layouts  66.8 us (7%)
  other arithmetic  52.8 us (5%)
  starting transfers between devices  25.6 us (3%)
  between operations  16.5 us (2%)
    psum x1, waiting for transfers between devices, local(): lax.psum(part_query.astype(jnp.bfloat16), 'replica').astype(jnp.float32)  78.8 us
    reduce_scatter x1, waiting for transfers between devices, local(): lax.psum_scatter(query_weight_grad.astype(jnp.bfloat16), 'shard', scatter...  74.9 us
    reduce_scatter x1, waiting for transfers between devices, local(): lax.psum_scatter(output_grad.astype(jnp.bfloat16), 'shard', scatter_dimen...  74.5 us
    reduce_scatter x1, waiting for transfers between devices, local(): lax.psum_scatter(key_weight_grad.astype(jnp.bfloat16), 'shard', scatter_d...  70 us
    psum x1, blocking collectives, local(): lax.psum((first_gain_grad, second_gain_grad), ('shard', 'replica'))  63.1 us
    all_to_all x1, blocking collectives, local(): lax.all_to_all(expert_rows, 'shard', split_axis=0, concat_axis=0, tiled=T...  50.7 us
    all_to_all x1, waiting for transfers between devices, local(): lax.all_to_all(row_grad, 'shard', split_axis=0, concat_axis=0, tiled=True)  49.6 us
    all_to_all x1, waiting for transfers between devices, local(): lax.all_to_all(slot_grad, 'shard', split_axis=0, concat_axis=0, tiled=True)  46.1 us
  transfers between devices with their start and end apart: 13, of which 12 were waited for; matrix products, arithmetic and copies ran while one was open for 10% of the time, Pallas kernels for 0%

commit v1 on v0

v1 whole, which is shorter than its diff:
```python
import functools
import math

import jax
import jax.numpy as jnp
from jax import lax
from jax.experimental import pallas as pl
from jax.experimental.pallas import tpu as pltpu
from jax.sharding import PartitionSpec as P

QUERY_HEADS = 16
KEY_VALUE_HEADS = 8
HEAD_SIZE = 64
H = 512
E = 16
CAP = 120
PACKED = 3328

EPS = 1e-06
ROPE_BASE = 10000.0
NEGATIVE = -1e30

MESH = pl.DeviceIdType.MESH


def place():
    me = lax.axis_index("shard")
    rep = lax.axis_index("replica")
    core = lax.rem(me, 2)
    y = lax.rem(me // 2, 4)
    high = me // 8
    return me, rep, core, y, high


def index_of(high, y, core):
    return (high * 4 + lax.rem(y, 4)) * 2 + core


def greet(targets):
    barrier = pltpu.get_barrier_semaphore()
    for target in targets:
        pl.semaphore_signal(barrier, inc=1, device_id=target, device_id_type=MESH)
    pl.semaphore_wait(barrier, len(targets))


def gather_kernel(cut, block_ref, out_ref, local_sem, send_sem, recv_sem):
    me, rep, core, y, high = place()
    rows = block_ref.shape[0]
    mate = (index_of(high, y, 1 - core), rep)
    up = (index_of(high, y + 1, core), rep)
    down = (index_of(high, y + 3, core), rep)
    across = (index_of(1 - high, y, core), rep)
    greet([mate, up, down, across])
    top, low = pl.ds(0, cut), pl.ds(cut, rows - cut)

    def remote(number, source, slot, span, target):
        return pltpu.make_async_remote_copy(
            src_ref=source,
            dst_ref=out_ref.at[slot, span],
            send_sem=send_sem.at[number],
            recv_sem=recv_sem.at[number],
            device_id=target,
            device_id_type=MESH,
        )

    whole = pl.ds(0, rows)
    other = index_of(1 - high, y, core)
    from_down = index_of(high, y + 3, core)
    from_up = index_of(high, y + 1, core)
    far = index_of(high, y + 2, core)
    other_down = index_of(1 - high, y + 3, core)
    other_up = index_of(1 - high, y + 1, core)
    other_far = index_of(1 - high, y + 2, core)
    own_across = remote(0, block_ref, me, whole, across)
    own_up = remote(1, block_ref, me, whole, up)
    own_down = remote(2, block_ref, me, whole, down)
    own_mate = remote(3, block_ref, me, whole, mate)
    copies = [own_across, own_up, own_down, own_mate]
    for copy in copies:
        copy.start()
    local = pltpu.make_async_copy(block_ref, out_ref.at[me], local_sem)
    local.start()

    def onward(number, slot, span, target):
        copy = remote(number, out_ref.at[slot, span], slot, span, target)
        copy.start()
        copies.append(copy)
        return copy

    own_up.wait_recv()
    far_up = onward(4, from_down, top, up)
    own_down.wait_recv()
    far_down = onward(5, from_up, low, down)
    own_across.wait_recv()
    other_to_up = onward(6, other, whole, up)
    other_to_down = onward(7, other, whole, down)
    mates = [own_mate]
    mates.append(onward(8, from_down, whole, mate))
    mates.append(onward(9, from_up, whole, mate))
    mates.append(onward(10, other, whole, mate))
    other_to_up.wait_recv()
    other_far_up = onward(11, other_down, top, up)
    other_to_down.wait_recv()
    other_far_down = onward(12, other_up, low, down)
    mates.append(onward(13, other_down, whole, mate))
    mates.append(onward(14, other_up, whole, mate))
    far_up.wait_recv()
    mates.append(onward(15, far, top, mate))
    far_down.wait_recv()
    mates.append(onward(16, far, low, mate))
    other_far_up.wait_recv()
    mates.append(onward(17, other_far, top, mate))
    other_far_down.wait_recv()
    mates.append(onward(18, other_far, low, mate))
    for copy in mates:
        copy.wait_recv()
    for copy in copies:
        copy.wait_send()
    local.wait()


def gather_rows(block, collective_id):
    rows, width = block.shape
    cut = (rows // 16 + 1) // 2 * 16
    return pl.pallas_call(
        functools.partial(gather_kernel, cut),
        out_shape=jax.ShapeDtypeStruct((16, rows, width), block.dtype),
        in_specs=[pl.BlockSpec(memory_space=pl.ANY)],
        out_specs=pl.BlockSpec(memory_space=pl.ANY),
        scratch_shapes=[
            pltpu.SemaphoreType.DMA,
            pltpu.SemaphoreType.DMA((19,)),
            pltpu.SemaphoreType.DMA((19,)),
        ],
        compiler_params=pltpu.CompilerParams(collective_id=collective_id, has_side_effects=True),
        cost_estimate=pl.CostEstimate(
            flops=0, bytes_accessed=16 * rows * width * 2 * 8, transcendentals=0
        ),
    )(block)


def add_rows(target, source, start, count):
    def body(step, carry):
        at = pl.ds(pl.multiple_of(start + step * 16, 16), 16)
        here = pl.ds(pl.multiple_of(step * 16, 16), 16)
        target[at, :] = (
            target[at, :].astype(jnp.float32) + source[here, :].astype(jnp.float32)
        ).astype(target.dtype)
        return carry

    lax.fori_loop(0, count // 16, body, 0)


def scatter_kernel(
    cut, blocks_ref, out_ref, sums, mates, near_up, near_down, far_up, far_down, cross,
    local_sem, send_sem, recv_sem,
):
    me, rep, core, y, high = place()
    rows = out_ref.shape[0]
    mate = (index_of(high, y, 1 - core), rep)
    up = (index_of(high, y + 1, core), rep)
    down = (index_of(high, y + 3, core), rep)
    across = (index_of(1 - high, y, core), rep)
    greet([mate, up, down, across])

    def remote(number, source, target_ref, target):
        return pltpu.make_async_remote_copy(
            src_ref=source,
            dst_ref=target_ref,
            send_sem=send_sem.at[number],
            recv_sem=recv_sem.at[number],
            device_id=target,
            device_id_type=MESH,
        )

    order = [4, 5, 2, 3, 6, 7, 0, 1]
    locals_, swaps, sends = {}, {}, []
    for slot in order:
        d, o = slot // 2, slot % 2
        side = 1 - high if o == 0 else high
        swap = remote(slot, blocks_ref.at[index_of(side, y + d, 1 - core)], mates.at[slot], mate)
        swap.start()
        swaps[slot] = swap
        sends.append(swap)
        local = pltpu.make_async_copy(
            blocks_ref.at[index_of(side, y + d, core)], sums.at[slot], local_sem.at[slot]
        )
        local.start()
        locals_[slot] = local

    def settle(slot):
        locals_[slot].wait()
        swaps[slot].wait_recv()
        add_rows(sums.at[slot], mates.at[slot], 0, rows)

    top, low = pl.ds(0, cut), pl.ds(cut, rows - cut)
    firsts = []
    for o in range(2):
        settle(4 + o)
        one = remote(8 + o, sums.at[4 + o, top], far_up.at[o], up)
        two = remote(10 + o, sums.at[4 + o, low], far_down.at[o], down)
        one.start()
        two.start()
        firsts.append((one, two))
        sends += [one, two]
    seconds = []
    for o in range(2):
        settle(2 + o)
        settle(6 + o)
        one, two = firsts[o]
        one.wait_recv()
        add_rows(sums.at[2 + o], far_up.at[o], 0, cut)
        one = remote(12 + o, sums.at[2 + o], near_up.at[o], up)
        one.start()
        two.wait_recv()
        add_rows(sums.at[6 + o], far_down.at[o], cut, rows - cut)
        two = remote(14 + o, sums.at[6 + o], near_down.at[o], down)
        two.start()
        seconds.append((one, two))
        sends += [one, two]
    for o in range(2):
        settle(o)
        one, two = seconds[o]
        one.wait_recv()
        add_rows(sums.at[o], near_up.at[o], 0, rows)
        two.wait_recv()
        add_rows(sums.at[o], near_down.at[o], 0, rows)
        if o == 0:
            last = remote(16, sums.at[0], cross, across)
            last.start()
            sends.append(last)
    last.wait_recv()

    def body(step, carry):
        at = pl.ds(pl.multiple_of(step * 16, 16), 16)
        out_ref[at, :] = (
            sums[1, at, :].astype(jnp.float32) + cross[at, :].astype(jnp.float32)
        ).astype(out_ref.dtype)
        return carry

    lax.fori_loop(0, rows // 16, body, 0)
    for copy in sends:
        copy.wait_send()


def scatter_rows(blocks, collective_id, out_type):
    count, rows, width = blocks.shape
    cut = (rows // 16 + 1) // 2 * 16
    kind = blocks.dtype
    return pl.pallas_call(
        functools.partial(scatter_kernel, cut),
        out_shape=jax.ShapeDtypeStruct((rows, width), out_type),
        in_specs=[pl.BlockSpec(memory_space=pl.ANY)],
        out_specs=pl.BlockSpec(memory_space=pltpu.VMEM),
        scratch_shapes=[
            pltpu.VMEM((8, rows, width), kind),
            pltpu.VMEM((8, rows, width), kind),
            pltpu.VMEM((2, rows, width), kind),
            pltpu.VMEM((2, rows, width), kind),
            pltpu.VMEM((2, cut, width), kind),
            pltpu.VMEM((2, rows - cut, width), kind),
            pltpu.VMEM((rows, width), kind),
            pltpu.SemaphoreType.DMA((8,)),
            pltpu.SemaphoreType.DMA((17,)),
            pltpu.SemaphoreType.DMA((17,)),
        ],
        compiler_params=pltpu.CompilerParams(
            collective_id=collective_id, has_side_effects=True, vmem_limit_bytes=40 * 1024 * 1024
        ),
        cost_estimate=pl.CostEstimate(
            flops=0, bytes_accessed=16 * rows * width * 2 * 8, transcendentals=0
        ),
    )(blocks)


def total_kernel(part_ref, out_ref, pieces, send_sem, recv_sem, send_back, recv_back):
    shard = lax.axis_index("shard")
    me = lax.axis_index("replica")
    rows, width = part_ref.shape
    others = [(shard, lax.rem(me + step, 8)) for step in range(1, 8)]
    greet(others)

    def piece(ref, which):
        half = width // 2
        return ref.at[
            pl.ds(pl.multiple_of((which // 2) * 16, 16), 16),
            pl.ds(pl.multiple_of(lax.rem(which, 2) * half, 128), half),
        ]

    firsts = []
    for step in range(1, 8):
        target = lax.rem(me + step, 8)
        copy = pltpu.make_async_remote_copy(
            src_ref=piece(part_ref, target),
            dst_ref=pieces.at[step - 1],
            send_sem=send_sem.at[step - 1],
            recv_sem=recv_sem.at[step - 1],
            device_id=(shard, target),
            device_id_type=MESH,
        )
        copy.start()
        firsts.append(copy)
    total = piece(part_ref, me)[...].astype(jnp.float32)
    for step in range(1, 8):
        firsts[step - 1].wait_recv()
        total = total + pieces[step - 1].astype(jnp.float32)
    piece(out_ref, me)[...] = total.astype(out_ref.dtype)
    seconds = []
    for step in range(1, 8):
        target = lax.rem(me + step, 8)
        copy = pltpu.make_async_remote_copy(
            src_ref=piece(out_ref, me),
            dst_ref=piece(out_ref, me),
            send_sem=send_back.at[step - 1],
            recv_sem=recv_back.at[step - 1],
            device_id=(shard, target),
            device_id_type=MESH,
        )
        copy.start()
        seconds.append(copy)
    for copy in seconds:
        copy.wait_recv()
    for copy in firsts + seconds:
        copy.wait_send()


def total_rows(part, collective_id):
    rows, width = part.shape
    return pl.pallas_call(
        total_kernel,
        out_shape=jax.ShapeDtypeStruct((rows, width), part.dtype),
        in_specs=[pl.BlockSpec(memory_space=pltpu.VMEM)],
        out_specs=pl.BlockSpec(memory_space=pltpu.VMEM),
        scratch_shapes=[
            pltpu.VMEM((7, 16, width // 2), part.dtype),
            pltpu.SemaphoreType.DMA((7,)),
            pltpu.SemaphoreType.DMA((7,)),
            pltpu.SemaphoreType.DMA((7,)),
            pltpu.SemaphoreType.DMA((7,)),
        ],
        compiler_params=pltpu.CompilerParams(collective_id=collective_id, has_side_effects=True),
    )(part)


def heads_first(rows, width):
    return rows.reshape(rows.shape[0], -1, width)


def rotate(value_rows, cosine_table, sine_table):
    count = value_rows.shape[0]
    halves = value_rows.reshape(count, -1, 2, HEAD_SIZE // 2)
    first, second = halves[:, :, 0], halves[:, :, 1]
    cos_rows, sin_rows = cosine_table[:, None, :], sine_table[:, None, :]
    turned = jnp.stack(
        [first * cos_rows - second * sin_rows, second * cos_rows + first * sin_rows], axis=2
    )
    return turned.reshape(count, -1)


def dot(a, b):
    return jnp.dot(a, b, preferred_element_type=jnp.float32)


def einsum(form, a, b):
    return jnp.einsum(form, a, b, preferred_element_type=jnp.float32)


def split_two(values):
    upper = values.astype(jnp.bfloat16)
    return upper, (values - upper.astype(jnp.float32)).astype(jnp.bfloat16)


def local(
    tokens,
    seq_lengths,
    routes,
    attn_gain,
    ffn_gain,
    w_query,
    key_projection,
    value_projection,
    w_output,
    w_router,
    w_in,
    w_out,
    cotangent,
):
    rows, width = tokens.shape
    group = QUERY_HEADS // KEY_VALUE_HEADS
    scale = HEAD_SIZE ** (-0.5)
    expert = lax.axis_index("shard")
    w_in, w_out = w_in[0], w_out[0]
    bf16, f32 = jnp.bfloat16, jnp.float32

    lengths = seq_lengths[0]
    row_index = jnp.arange(rows, dtype=jnp.int32)
    first_len, total_len = lengths[0], lengths[0] + lengths[1]
    doc = jnp.where(row_index < first_len, 0, jnp.where(row_index < total_len, 1, 2))
    start = jnp.where(
        row_index < first_len, 0, jnp.where(row_index < total_len, first_len, total_len)
    )
    allowed = (doc[:, None] == doc[None, :]) & (row_index[None, :] <= row_index[:, None])
    live = (row_index < total_len).astype(f32)[:, None]
    frequency = jnp.exp(
        jnp.arange(HEAD_SIZE // 2, dtype=f32) * (-2.0 * math.log(ROPE_BASE) / HEAD_SIZE)
    )
    angles = (row_index - start).astype(f32)[:, None] * frequency[None, :]
    cosine_table, sine_table = jnp.cos(angles), jnp.sin(angles)
    gain_first, gain_second = attn_gain.astype(f32), ffn_gain.astype(f32)

    packed = jnp.concatenate(
        [
            w_query,
            key_projection,
            value_projection,
            w_output,
            w_router,
            jnp.zeros((w_query.shape[0], PACKED - 3072 - E), bf16),
        ],
        axis=1,
    )
    weights = gather_rows(packed, 1).reshape(-1, PACKED)
    upstream = cotangent.astype(f32)
    mix_grad = (cotangent * live.astype(bf16)).astype(bf16)
    all_mix_grad = lax.all_gather(mix_grad, "shard", axis=0)

    inputs = tokens.astype(f32)
    scale_first = lax.rsqrt(jnp.mean(inputs * inputs, axis=1, keepdims=True) + EPS)
    normed_first = (inputs * scale_first * gain_first).astype(bf16)
    w_qkv, full_output, full_router = (
        weights[:, :2048],
        weights[:, 2048:3072],
        weights[:, 3072 : 3072 + E],
    )
    qkv = dot(normed_first, w_qkv)
    turned = rotate(qkv[:, :1536], cosine_table, sine_table).astype(bf16)
    query = turned[:, :1024].reshape(rows, KEY_VALUE_HEADS, group, HEAD_SIZE)
    key = turned[:, 1024:].reshape(rows, KEY_VALUE_HEADS, HEAD_SIZE)
    value = qkv[:, 1536:].astype(bf16).reshape(rows, KEY_VALUE_HEADS, HEAD_SIZE)
    scores = jnp.where(allowed, einsum("ehla,jha->hlej", query, key) * scale, NEGATIVE)
    largest = jnp.max(scores, axis=-1, keepdims=True)
    raised = jnp.exp(scores - largest)
    attn_prob = raised / jnp.sum(raised, axis=-1, keepdims=True)
    attn_prob_b = attn_prob.astype(bf16)
    mixed = einsum("pjwi,ipx->wpjx", attn_prob_b, value).reshape(rows, -1).astype(bf16)
    hidden_one = inputs + live * dot(mixed, full_output)
    scale_second = lax.rsqrt(jnp.mean(hidden_one * hidden_one, axis=1, keepdims=True) + EPS)
    normed_second = (hidden_one * scale_second * gain_second).astype(bf16)
    logits = dot(normed_second, full_router)
    named = jnp.any(routes[:, :, None] == jnp.arange(E, dtype=jnp.int32), axis=1)
    logits = jnp.where(named, logits, NEGATIVE)
    raised = jnp.exp(logits - jnp.max(logits, axis=1, keepdims=True))
    gates = raised / jnp.sum(raised, axis=1, keepdims=True)

    def side_rows(table):
        upper, lower = split_two(table)
        return jnp.concatenate(
            [jnp.pad(upper, ((0, 0), (0, 64))), jnp.pad(lower, ((0, 0), (0, 1024 - 448)))], axis=1
        )

    payload = jnp.concatenate([normed_second, side_rows(gates.T)], axis=0)
    arrived = gather_rows(payload, 2)
    own = lax.dynamic_slice(arrived, (0, rows + expert, 0), (16, 1, 448))[:, 0].astype(f32)
    own_gates = own[:, :rows] + own[:, 256 : 256 + rows]
    member = own_gates > 0
    earlier = (row_index[:, None] < row_index[None, :]).astype(bf16)
    rank = dot(member.astype(bf16), earlier).astype(jnp.int32)
    slot_of = jnp.where(member, rank, -1)
    pick = slot_of[:, None, :] == jnp.arange(CAP, dtype=jnp.int32)[None, :, None]
    pick_b = pick.astype(bf16)
    slot_gates = jnp.sum(jnp.where(pick, own_gates[:, None, :], 0.0), axis=2)[:, :, None]

    expert_rows = einsum("srt,std->srd", pick_b, arrived[:, :rows]).astype(bf16)
    mix_rows = einsum("srt,std->srd", pick_b, all_mix_grad).astype(bf16)
    expert_rows = expert_rows.reshape(16 * CAP, width)
    pre_act = dot(expert_rows, w_in)
    gate, up = pre_act[:, :H], pre_act[:, H:]
    sig = jax.nn.sigmoid(gate)
    silu = gate * sig
    activation = (silu * up).astype(bf16)
    expert_out = dot(activation, w_out).astype(bf16).astype(f32).reshape(16, CAP, width)
    mix_rows = mix_rows.astype(f32)
    slot_gate_grad = jnp.sum(expert_out * mix_rows, axis=2, keepdims=True)
    weighted = (slot_gates * expert_out).astype(bf16)
    route_grad = (slot_gates * mix_rows).astype(bf16).reshape(16 * CAP, width)
    activation_grad = einsum("rd,hd->rh", route_grad, w_out)
    pre_grad = jnp.concatenate(
        [activation_grad * up * sig * (1 + gate * (1 - sig)), activation_grad * silu], axis=1
    ).astype(bf16)
    grad_in = einsum("rd,rf->df", expert_rows, pre_grad)
    grad_out = einsum("rh,rd->hd", activation, route_grad)
    expert_grads = lax.psum(jnp.concatenate([grad_in, grad_out], axis=0).astype(bf16), "replica")
    row_grad = einsum("rf,df->rd", pre_grad, w_in).astype(bf16).reshape(16, CAP, width)
    returned = einsum(
        "srt,srd->std", pick_b, jnp.concatenate([weighted, row_grad], axis=2)
    ).astype(bf16)
    token_gate_grad = jnp.sum(jnp.where(pick, slot_gate_grad, 0.0), axis=1)
    upper, lower = split_two(token_gate_grad)
    side = jnp.concatenate(
        [jnp.pad(upper, ((0, 0), (0, 64))), jnp.pad(lower, ((0, 0), (0, 2048 - 448)))], axis=1
    )
    mine = (jnp.arange(E) == expert)[None, :, None]
    side = jnp.where(mine, side[:, None, :], 0).astype(bf16)
    back = scatter_rows(jnp.concatenate([returned, side], axis=1), 3, f32)

    output = (hidden_one + live * back[:rows, :width]).astype(bf16)
    gate_grad = (back[rows:, :rows] + back[rows:, 256 : 256 + rows]).T
    logit_grad = (gates * (gate_grad - jnp.sum(gates * gate_grad, axis=1, keepdims=True))).astype(
        bf16
    )
    normed_second_grad = back[:rows, width:] + einsum("te,de->td", logit_grad, full_router)
    d_router = einsum("td,te->de", normed_second, logit_grad)
    d_ffn_gain = jnp.sum(normed_second_grad * hidden_one * scale_second, axis=0)
    gained = normed_second_grad * gain_second
    hidden_grad = (
        upstream
        + scale_second * gained
        - hidden_one
        * scale_second**3
        * jnp.mean(gained * hidden_one, axis=1, keepdims=True)
    )
    attn_grad = (live * hidden_grad).astype(bf16)
    mixed_grad = einsum("td,cd->tc", attn_grad, full_output).astype(bf16)
    d_output = einsum("tc,td->cd", mixed, attn_grad).astype(bf16)
    mixed_grad = mixed_grad.reshape(rows, KEY_VALUE_HEADS, group, HEAD_SIZE)
    prob_grad = einsum("ehla,jha->hlej", mixed_grad, value)
    value_grad = einsum("uqeh,euqz->huz", attn_prob_b, mixed_grad).reshape(rows, -1).astype(bf16)
    row_dot = jnp.sum(attn_prob * prob_grad, axis=-1, keepdims=True)
    score_grad = (attn_prob * (prob_grad - row_dot)).astype(bf16)
    query_turned = einsum("pjwi,ipx->wpjx", score_grad, key).reshape(rows, -1) * scale
    key_turned = einsum("uqeh,euqz->huz", score_grad, query).reshape(rows, -1) * scale
    turned_back = rotate(
        jnp.concatenate([query_turned, key_turned], axis=1), cosine_table, -sine_table
    ).astype(bf16)
    qkv_grad = jnp.concatenate([turned_back, value_grad], axis=1)
    normed_first_grad = einsum("tc,dc->td", qkv_grad, w_qkv)
    d_qkv = einsum("td,tc->dc", normed_first, qkv_grad).astype(bf16)
    d_attn_gain = jnp.sum(normed_first_grad * inputs * scale_first, axis=0)
    gained = normed_first_grad * gain_first
    d_tokens = (
        hidden_grad
        + scale_first * gained
        - inputs * scale_first**3 * jnp.mean(gained * inputs, axis=1, keepdims=True)
    )
    share = w_query.shape[0]
    gains = jnp.concatenate([d_attn_gain, d_ffn_gain]).astype(bf16).reshape(share, -1)
    lanes = gains.shape[1]
    grads = jnp.concatenate(
        [
            d_qkv,
            d_output,
            d_router.astype(bf16),
            jnp.tile(gains, (16, 1)),
            jnp.zeros((1024, PACKED - 3072 - E - lanes), bf16),
        ],
        axis=1,
    )
    part = scatter_rows(grads.reshape(16, share, PACKED), 4, bf16)
    total = total_rows(part, 5).astype(f32)
    gains = total[:, 3072 + E : 3072 + E + lanes].reshape(2, width)
    expert_grads = expert_grads.astype(f32)
    return (
        output,
        d_tokens,
        gains[0],
        gains[1],
        total[:, :1024],
        total[:, 1024:1536],
        total[:, 1536:2048],
        total[:, 2048:3072],
        total[:, 3072 : 3072 + E],
        expert_grads[None, :width],
        expert_grads[None, width:],
    )


def solution(mesh):
    return jax.shard_map(
        local,
        mesh=mesh,
        in_specs=(
            P(("shard", "replica"), None),
            P(("shard", "replica"), None),
            P(("shard", "replica"), None),
            P(),
            P(),
            P("shard", None),
            P("shard", None),
            P("shard", None),
            P("shard", None),
            P("shard", None),
            P("shard", None, None),
            P("shard", None, None),
            P(("shard", "replica"), None),
        ),
        out_specs=(
            P(("shard", "replica"), None),
            P(("shard", "replica"), None),
            P(),
            P(),
            P("shard", None),
            P("shard", None),
            P("shard", None),
            P("shard", None),
            P("shard", None),
            P("shard", None, None),
            P("shard", None, None),
        ),
        check_vma=False,
    )
```

time: 1000 us -> 422 us (0.42)
  waiting for transfers between devices: 606 us -> 0.04 us
  Pallas kernels: 0 us -> 231 us
  blocking collectives: 153 us -> 0 us
  starting transfers between devices: 25.6 us -> 0.08 us
  other arithmetic: 52.8 us -> 36.3 us
  local copies, waits for them, and re-layouts: 66.8 us -> 50.4 us
    reduce_scatter x4 -> x0, waiting for transfers between devices: 259 us -> none  [the longest x1 74.9 us: local(): lax.psum_scatter(query_weight_grad.astype(jnp.bfloat16), 'shard', scatter...]
    pallas_call x0 -> x5, Pallas kernels: none -> 231 us  [the longest x2 111 us: scatter_rows(): pl.pallas_call(functools.partial(scatter_kernel, cut), out_shape=jax.Shap...]
    all_to_all x3 -> x0, waiting for transfers between devices: 135 us -> none  [the longest x1 49.6 us: local(): lax.all_to_all(row_grad, 'shard', split_axis=0, concat_axis=0, tiled=True)]
    all_gather x4 -> x1, waiting for transfers between devices: 129 us -> 0.01 us  [local(): all_mix_grad = lax.all_gather(mix_grad, 'shard', axis=0)]
    psum x2 -> x0, blocking collectives: 82.2 us -> none  [the longest x1 63.1 us: local(): lax.psum((first_gain_grad, second_gain_grad), ('shard', 'replica'))]
    psum x1, waiting for transfers between devices: 78.8 us -> 0.01 us  [local(): lax.psum(jnp.concatenate([grad_in, grad_out], axis=0).astype(bf16), 'repl...]
    all_to_all x1 -> x0, blocking collectives: 50.7 us -> none  [local(): lax.all_to_all(expert_rows, 'shard', split_axis=0, concat_axis=0, tiled=T...]
    gather x4 -> x0, local copies, waits for them, and re-layouts: 40.5 us -> none  [the longest x1 12.3 us: local(): route_grad[source] * fill_mask]
  transfers between devices with their start and end apart: 13 -> 2, of which waited for: 12 -> 0; matrix products, arithmetic and copies ran while one was open for 10% -> 19% of each run, Pallas kernels for 0% -> 40%
where the time goes in v1:
time: 422 us; the launch traced here: 415 us
  Pallas kernels  231 us (55%)
  matrix products  80.6 us (19%)
  local copies, waits for them, and re-layouts  50.4 us (12%)
  other arithmetic  36.3 us (9%)
  between operations  16.6 us (4%)
    pallas_call x2, Pallas kernels, scatter_rows(): pl.pallas_call(functools.partial(scatter_kernel, cut), out_shape=jax.Shap...  111 us
    pallas_call x2, Pallas kernels, gather_rows(): pl.pallas_call(functools.partial(gather_kernel, cut), out_shape=jax.Shape...  83.8 us
    dot_general x18, matrix products, einsum(): return jnp.einsum(form, a, b, preferred_element_type=jnp.float32)  60.3 us
    pallas_call x1, Pallas kernels, total_rows(): pl.pallas_call(total_kernel, out_shape=jax.ShapeDtypeStruct((rows, width)...  36.7 us
    dot_general x6, matrix products, dot(): return jnp.dot(a, b, preferred_element_type=jnp.float32)  16.1 us
    unnamed x135, local copies, waits for them, and re-layouts  15.9 us
    concatenate x1, local copies, waits for them, and re-layouts, local(): jnp.concatenate([d_qkv, d_output, d_router.astype(bf16), jnp.tile(gains,...  10.5 us
    concatenate x1, other arithmetic, local(): back = scatter_rows(jnp.concatenate([returned, side], axis=1), 3, f32)  8.59 us
  transfers between devices with their start and end apart: 2, of which 0 were waited for; matrix products, arithmetic and copies ran while one was open for 19% of the time, Pallas kernels for 40%

profile of v1, /device:TPU:8, one launch (start us, length us, event | category | flops | bytes accessed | tf_op | source)
XLA Modules:
  0.0 415.3 jit_solution(6635211546225562329)
XLA Ops:
  7.2 1.4 fusion.105
  9.9 1.8 broadcast_multiply_fusion
  11.9 0.8 copy.51
  12.7 1.9 concatenate.53.block_ref
  14.6 47.0 %shard_map.212 = bf16[16,64,3328]{2,1,0:T(8,128)(2,1)} custom-call(bf16[64,3328]{1,0:T(8,128)(2,1)} %concatenate.53.block_ref), custom_call_target="tpu_custom_call" | custom-call | bytes 54525952 | tf_op jit(solution)/shard_map/pallas_call | solution.py:125
  62.4 3.3 fusion.16
  65.7 1.1 copy-done.22
  66.8 1.1 slice.135
  67.9 2.9 copy.53
  71.5 0.8 fusion.90
  72.4 1.7 subtract_convert_fusion.1
  74.2 0.8 slice.139
  75.1 1.0 slice.212
  78.3 4.1 fusion.106
  82.4 2.3 convolution_convert_fusion.6
  84.7 2.5 multiply_reduce_fusion.2
  88.6 1.2 fusion.107
  90.4 0.8 fusion.71.block_ref
  91.2 36.8 %shard_map.213 = bf16[16,208,1024]{2,1,0:T(8,128)(2,1)} custom-call(bf16[208,1024]{1,0:T(8,128)(2,1)} %fusion.71.block_ref), custom_call_target="tpu_custom_call" | custom-call | bytes 54525952 | tf_op jit(solution)/shard_map/pallas_call | solution.py:125
  128.0 0.9 dynamic-slice_convert_fusion
  130.3 4.7 %fusion.21 = bf16[16,120,1024]{2,1,0:T(8,128)(2,1)S(1)} fusion(bf16[16,208,1024]{2,1,0:T(8,128)(2,1)} %shard_map.213, s32[16,192]{1,0:T(8,128)S(1)} %fusion.47), kind=kOutput, calls=%fused_computation.37 | convolution fusion | flops 757309440 | bytes 10235904 | tf_op jit(solution)/shard_map/srt,std->srd/dot_general | solution.py:365
  135.0 4.9 %fusion.27 = f32[1920,1024]{0,1:T(8,128)S(1)} fusion(bf16[1920,1024]{1,0:T(8,128)(2,1)S(1)} %bitcast.134, bf16[1,1024,1024]{2,1,0:T(8,128)(2,1)S(1)} %copy-done), kind=kOutput, calls=%fused_computation.43 | convolution fusion | flops 4026531840 | bytes 13893632 | tf_op jit(solution)/shard_map/dot_general | solution.py:361
  139.9 1.2 multiply_convert_fusion.2
  141.1 1.9 copy-done.7
  142.9 1.3 copy-done.19
  144.2 4.2 %convolution_convert_fusion = bf16[1920,1024]{1,0:T(8,128)(2,1)} fusion(bf16[1920,512]{0,1:T(8,128)(2,1)S(1)} %multiply_convert_fusion.2, bf16[1,512,1024]{2,1,0:T(8,128)(2,1)S(1)} %copy-done.62), kind=kOutput, calls=%fused_computation.22 | convolution fusion | flops 2015232000 | bytes 6946816 | tf_op jit(solution)/shard_map/dot_general | solution.py:361
  148.4 6.3 %fusion.3 = (f32[16,120]{1,0:T(8,128)S(1)}, bf16[16,120,1024]{2,1,0:T(8,128)(2,1)S(1)}) fusion(bf16[16,120,1024]{2,1,0:T(8,128)(2,1)} %bitcast.130, bf16[16,192,1024]{2,1,0:T(8,128)(2,1)} %bitcast.133, s32[16,192]{1,0:T(8,128)S(1)} %fusion.47), kind=kOutput, calls=%fused_computation.7 | convolution fusion | flops 765171840 | bytes 14175744 | tf_op jit(solution)/shard_map/srt,std->srd/dot_general | solution.py:365
  154.7 1.9 select_reduce_fusion.1
  156.6 2.7 fusion.2
  159.3 1.9 copy-done.8
  161.5 3.9 multiply_convert_fusion.1
  165.4 3.3 convolution_convert_fusion.5
  168.7 7.0 %fusion.29 = bf16[1024,1024]{1,0:T(8,128)(2,1)} fusion(bf16[1920,1024]{1,0:T(8,128)(2,1)S(1)} %bitcast.135, bf16[1920,512]{0,1:T(8,128)(2,1)S(1)} %get-tuple-element.53, bf16[1920,512]{0,1:T(8,128)(2,1)S(1)} %get-tuple-element.52), kind=kOutput, calls=%fused_computation.45 | convolution fusion | flops 4035444736 | bytes 9961472 | tf_op jit(solution)/shard_map/rd,rf->df/dot_general | solution.py:365
  175.7 6.0 %convolution_convert_fusion.2 = bf16[1920,1024]{1,0:T(8,128)(2,1)} fusion(bf16[1920,512]{0,1:T(8,128)(2,1)S(1)} %get-tuple-element.53, bf16[1920,512]{0,1:T(8,128)(2,1)S(1)} %get-tuple-element.52, bf16[1,1024,1024]{2,1,0:T(8,128)(2,1)S(1)} %copy-done), kind=kOutput, calls=%fused_computation.24 | convolution fusion | flops 4036362240 | bytes 9961472 | tf_op jit(solution)/shard_map/rf,df->rd/dot_general | solution.py:365
  181.6 5.9 %fusion.8 = bf16[16,192,2048]{2,1,0:T(8,128)(2,1)S(1)} fusion(bf16[16,120,1024]{2,1,0:T(8,128)(2,1)} %bitcast.150, bf16[16,120,1024]{2,1,0:T(8,128)(2,1)} %get-tuple-element.66, s32[16,192]{1,0:T(8,128)S(1)} %fusion.47), kind=kOutput, calls=%fused_computation.12 | convolution fusion | flops 1532338176 | bytes 20459520 | tf_op jit(solution)/shard_map/srt,srd->std/dot_general | solution.py:365
  187.7 8.6 %pad_maximum_fusion.blocks_ref = bf16[16,208,2048]{2,1,0:T(8,128)(2,1)} fusion(bf16[16,16,2048]{2,1,0:T(8,128)(2,1)S(1)} %broadcast_select_fusion, bf16[16,192,2048]{2,1,0:T(8,128)(2,1)S(1)} %fusion.8), kind=kLoop, calls=%fused_computation.1 | loop fusion | flops 27262976 | bytes 27262976 | tf_op jit(solution)/shard_map/concatenate | solution.py:504
  196.3 67.2 %shard_map.214 = f32[208,2048]{1,0:T(8,128)S(1)} custom-call(bf16[16,208,2048]{2,1,0:T(8,128)(2,1)} %pad_maximum_fusion.blocks_ref), custom_call_target="tpu_custom_call" | custom-call | bytes 109051904 | tf_op jit(solution)/shard_map/pallas_call | solution.py:250
  263.6 2.0 multiply_reduce_fusion
  265.7 2.2 multiply_subtract_fusion
  267.9 2.4 fusion.42
  270.4 1.0 copy.55
  271.4 2.9 fusion.18
  275.2 1.4 convolution_multiply_fusion
  276.6 1.4 fusion.45
  278.0 2.0 pad_maximum_fusion.2
  280.1 1.6 pad_maximum_fusion.7
  284.1 0.9 slice-done.1
  285.0 3.0 fusion.64
  288.8 0.8 concatenate.66
  289.5 0.9 convolution_convert_fusion.7
  290.4 0.9 copy.59
  291.2 1.9 convolution_convert_fusion.4
  293.2 4.5 %convolution_convert_fusion.1 = bf16[1024,2048]{1,0:T(8,128)(2,1)} fusion(bf16[192,512]{0,1:T(8,128)(2,1)S(1)} %bitcast.166, bf16[192,1536]{0,1:T(8,128)(2,1)S(1)} %bitcast.152, bf16[192,1024]{1,0:T(8,128)(2,1)} %param.13, f32[1024]{0:T(1024)} %copy-done.32, f32[192]{0:T(256)} %copy-done.47), kind=kOutput, calls=%fused_computation.23 | convolution fusion | flops 809762816 | bytes 5378816 | tf_op jit(solution)/shard_map/td,tc->dc/dot_general | solution.py:365
  298.4 10.5 %concatenate.68.blocks_ref = bf16[16,64,3328]{2,1,0:T(8,128)(2,1)} concatenate(bf16[16,64,2048]{2,1,0:T(8,128)(2,1)} %bitcast.132, bf16[16,64,1024]{2,1,0:T(8,128)(2,1)S(1)} %bitcast.136, bf16[16,64,16]{2,1,0:T(8,128)(2,1)} %bitcast.158, bf16[16,64,32]{2,1,0:T(8,128)(2,1)} %tile.2, bf16[16,64,208]{2,1,0:T(8,128)(2,1)S(1)} %broadcast_in_dim.138), dimensions={2} | concatenate | bytes 13631488 | tf_op jit(solution)/shard_map/concatenate | solution.py:548
  308.9 3.0 copy-done.2
  312.0 43.6 %shard_map.215.part_ref = bf16[64,3328]{1,0:T(8,128)(2,1)S(1)} custom-call(bf16[16,64,3328]{2,1,0:T(8,128)(2,1)S(1)} %copy-done.2), custom_call_target="tpu_custom_call" | custom-call | bytes 54525952 | tf_op jit(solution)/shard_map/pallas_call | solution.py:250
  356.4 36.7 %shard_map.216 = bf16[64,3328]{1,0:T(8,128)(2,1)} custom-call(bf16[64,3328]{1,0:T(8,128)(2,1)} %copy-done.3), custom_call_target="tpu_custom_call" | custom-call | tf_op jit(solution)/shard_map/pallas_call | solution.py:329
  394.5 0.8 fusion.104
  396.6 1.6 fusion.103
  398.2 1.8 fusion.102
  400.0 1.1 fusion.61
  401.2 2.6 convert_element_type.222
  403.8 2.6 slice_bitcast_fusion
  406.4 1.6 slice_bitcast_fusion.1
  (174 shorter events, 15.9 us)
Async XLA Ops:
  7.2 127.8 %copy-start = (bf16[1,1024,1024]{2,1,0:T(8,128)(2,1)S(1)}, bf16[1,1024,1024]{2,1,0:T(8,128)(2,1)}, u32[]{:S(2)}) copy-start(bf16[1,1024,1024]{2,1,0:T(8,128)(2,1)} %param.23) | copy-start | bytes 6291460
  7.2 141.2 %all-gather.3.cloned.1.call-start = ((), (), s32[]{:S(2)}) async-start(), calls=%async_computation.1 | async-start | bytes 6684672 | tf_op jit(solution)/shard_map/all_gather | solution.py:425
  11.8 389.4 %all-reduce.6.cloned.1.call-start = ((), (), s32[]{:S(2)}) async-start(), calls=%async_computation | async-start | bytes 6291456 | tf_op jit(solution)/shard_map/psum | solution.py:492
  12.6 48.9 %copy-start.59 = (bf16[1024]{0:T(1024)(128)(2,1)S(1)}, bf16[1024]{0:T(1024)(128)(2,1)}, u32[]{:S(2)}) copy-start(bf16[1024]{0:T(1024)(128)(2,1)} %param.16) | copy-start | bytes 6148
  12.7 49.0 %copy-start.10 = (bf16[192,1024]{1,0:T(8,128)(2,1)S(1)}, bf16[192,1024]{1,0:T(8,128)(2,1)}, u32[]{:S(2)}) copy-start(bf16[192,1024]{1,0:T(8,128)(2,1)} %param.13) | copy-start | bytes 1179652
  61.6 6.3 %copy-start.32 = (f32[1024]{0:T(1024)}, f32[1024]{0:T(1024)S(1)}, u32[]{:S(2)}) copy-start(f32[1024]{0:T(1024)S(1)} %convert_element_type.179) | copy-start | bytes 12292
  62.4 5.5 %copy-start.47 = (f32[192]{0:T(256)}, f32[192]{0:T(256)S(1)}, u32[]{:S(2)}) copy-start(f32[192]{0:T(256)S(1)} %get-tuple-element.72) | copy-start | bytes 2308
  65.7 1.1 copy-start.22
  70.9 6.7 %copy-start.54 = (s32[192,8]{0,1:T(8,128)S(1)}, s32[192,8]{0,1:T(8,128)}, u32[]{:S(2)}) copy-start(s32[192,8]{0,1:T(8,128)} %param.15) | copy-start | bytes 18436
  72.4 1.7 copy-start.29
  76.2 8.4 %copy-start.31 = (bf16[192,512]{0,1:T(8,128)(2,1)}, bf16[192,512]{0,1:T(8,128)(2,1)S(1)}, u32[]{:S(2)}) copy-start(bf16[192,512]{0,1:T(8,128)(2,1)S(1)} %copy.52) | copy-start | bytes 589828
  77.0 10.9 %copy-start.38 = (f32[1024]{0:T(1024)}, f32[1024]{0:T(1024)S(1)}, u32[]{:S(2)}) copy-start(f32[1024]{0:T(1024)S(1)} %convert_element_type.187) | copy-start | bytes 12292
  82.4 2.3 copy-start.44
  82.4 2.4 copy-start.56
  84.7 3.2 copy-start.27
  84.7 3.9 copy-start.50
  87.2 176.4 %copy-start.9 = (f32[192,1024]{1,0:T(8,128)}, f32[192,1024]{1,0:T(8,128)S(1)}, u32[]{:S(2)}) copy-start(f32[192,1024]{1,0:T(8,128)S(1)} %get-tuple-element.80) | copy-start | bytes 2359300
  89.8 38.2 %copy-start.24 = (f32[192,16]{0,1:T(8,128)}, f32[192,16]{0,1:T(8,128)S(1)}, u32[]{:S(2)}) copy-start(f32[192,16]{0,1:T(8,128)S(1)} %get-tuple-element.82) | copy-start | bytes 36868
  135.0 4.9 %copy-start.5 = (bf16[16,120,1024]{2,1,0:T(8,128)(2,1)}, bf16[16,120,1024]{2,1,0:T(8,128)(2,1)S(1)}, u32[]{:S(2)}) copy-start(bf16[16,120,1024]{2,1,0:T(8,128)(2,1)S(1)} %fusion.21) | copy-start | bytes 11796484
  139.9 3.1 copy-start.7
  139.9 4.3 %copy-start.62 = (bf16[1,512,1024]{2,1,0:T(8,128)(2,1)S(1)}, bf16[1,512,1024]{2,1,0:T(8,128)(2,1)}, u32[]{:S(2)}) copy-start(bf16[1,512,1024]{2,1,0:T(8,128)(2,1)} %param.24) | copy-start | bytes 3145732
  142.9 1.3 copy-start.19
  148.4 6.3 %copy-start.37 = (f32[16,192]{1,0:T(8,128)S(1)}, f32[16,192]{1,0:T(8,128)}, u32[]{:S(2)}) copy-start(f32[16,192]{1,0:T(8,128)} %copy-done.36) | copy-start | bytes 36868
  148.4 8.2 %copy-start.4 = (bf16[1920,1024]{1,0:T(8,128)(2,1)S(1)}, bf16[1920,1024]{1,0:T(8,128)(2,1)}, u32[]{:S(2)}) copy-start(bf16[1920,1024]{1,0:T(8,128)(2,1)} %convolution_convert_fusion) | copy-start | bytes 11796484
  156.6 4.7 %copy-start.8 = (f32[1920,1024]{0,1:T(8,128)S(1)}, f32[1920,1024]{0,1:T(8,128)}, u32[]{:S(2)}) copy-start(f32[1920,1024]{0,1:T(8,128)} %copy-done.7) | copy-start | bytes 23592964
  156.6 4.9 %copy-start.63 = (bf16[1,512,1024]{2,1,0:T(8,128)(2,1)S(1)}, bf16[1,512,1024]{2,1,0:T(8,128)(2,1)}, u32[]{:S(2)}) copy-start(bf16[1,512,1024]{2,1,0:T(8,128)(2,1)} %param.24) | copy-start | bytes 3145732
  161.5 3.9 copy-start.20
  165.4 3.3 copy-start.6
  181.6 5.9 %copy-start.61 = (pred[16]{0:T(512)(128)(4,1)S(1)}, pred[16]{0:T(512)(128)(4,1)}, u32[]{:S(2)}) copy-start(pred[16]{0:T(512)(128)(4,1)} %iota_compare_fusion.15) | copy-start | bytes 52
  196.3 67.3 %copy-start.25 = (f32[192,16]{0,1:T(8,128)S(1)}, f32[192,16]{0,1:T(8,128)}, u32[]{:S(2)}) copy-start(f32[192,16]{0,1:T(8,128)} %copy-done.24) | copy-start | bytes 36868
  196.3 67.3 %copy-start.41 = (f32[192]{0:T(256)S(1)}, f32[192]{0:T(256)}, u32[]{:S(2)}) copy-start(f32[192]{0:T(256)} %copy-done.40) | copy-start | bytes 2308
  196.3 67.3 %copy-start.43 = (f32[192]{0:T(256)S(1)}, f32[192]{0:T(256)}, u32[]{:S(2)}) copy-start(f32[192]{0:T(256)} %copy-done.42) | copy-start | bytes 2308
  196.3 67.3 %copy-start.39 = (f32[1024]{0:T(1024)S(1)}, f32[1024]{0:T(1024)}, u32[]{:S(2)}) copy-start(f32[1024]{0:T(1024)} %copy-done.38) | copy-start | bytes 12292
  196.3 67.4 %copy-start.52 = (f32[192]{0:T(256)S(1)}, f32[192]{0:T(256)}, u32[]{:S(2)}) copy-start(f32[192]{0:T(256)} %copy-done.51) | copy-start | bytes 2308
  196.3 69.4 %copy-start.21 = (bf16[192,1024]{1,0:T(8,128)(2,1)S(1)}, bf16[192,1024]{1,0:T(8,128)(2,1)}, u32[]{:S(2)}) copy-start(bf16[192,1024]{1,0:T(8,128)(2,1)} %param.25) | copy-start | bytes 1179652
  196.3 69.4 %copy-start.57 = (f32[192]{0:T(256)S(1)}, f32[192]{0:T(256)}, u32[]{:S(2)}) copy-start(f32[192]{0:T(256)} %fusion.92) | copy-start | bytes 2308
  196.3 69.4 %copy-start.58 = (f32[192]{0:T(256)S(1)}, f32[192]{0:T(256)}, u32[]{:S(2)}) copy-start(f32[192]{0:T(256)} %get-tuple-element.73) | copy-start | bytes 2308
  263.6 2.0 copy-start.53
  271.4 3.1 copy-start.15
  271.4 3.1 copy-start.45
  274.5 2.1 copy-start.18
  275.2 2.8 copy-start.17
  275.2 2.8 copy-start.23
  280.0 1.7 copy-start.30
  280.0 1.7 copy-start.35
  280.0 2.4 copy-start.16
  280.0 2.5 copy-start.28
  280.1 2.5 copy-start.46
  280.1 4.1 slice-start
  282.5 0.9 copy-start.13
  282.5 2.5 slice-start.1
  282.5 2.5 copy-start.11
  282.5 2.5 copy-start.33
  282.5 2.5 copy-start.48
  291.2 1.9 copy-start.14
  308.9 3.0 copy-start.2
  312.0 84.6 %copy-start.60 = (f32[192]{0:T(256)S(1)}, f32[192]{0:T(256)}, u32[]{:S(2)}) copy-start(f32[192]{0:T(256)} %get-tuple-element.47) | copy-start | bytes 2308
  312.0 88.1 %copy-start.12 = (bf16[192,1024]{1,0:T(8,128)(2,1)S(1)}, bf16[192,1024]{1,0:T(8,128)(2,1)}, u32[]{:S(2)}) copy-start(bf16[192,1024]{1,0:T(8,128)(2,1)} %param.13) | copy-start | bytes 1179652
  312.0 88.1 %copy-start.26 = (f32[192,1024]{1,0:T(8,128)S(1)}, f32[192,1024]{1,0:T(8,128)}, u32[]{:S(2)}) copy-start(f32[192,1024]{1,0:T(8,128)} %get-tuple-element.88) | copy-start | bytes 2359300
  312.0 88.1 %copy-start.34 = (f32[1024]{0:T(1024)S(1)}, f32[1024]{0:T(1024)}, u32[]{:S(2)}) copy-start(f32[1024]{0:T(1024)} %copy-done.32) | copy-start | bytes 12292
  312.0 88.1 %copy-start.49 = (f32[192]{0:T(256)S(1)}, f32[192]{0:T(256)}, u32[]{:S(2)}) copy-start(f32[192]{0:T(256)} %copy-done.47) | copy-start | bytes 2308
  312.0 88.1 %copy-start.55 = (f32[192]{0:T(256)S(1)}, f32[192]{0:T(256)}, u32[]{:S(2)}) copy-start(f32[192]{0:T(256)} %get-tuple-element.71) | copy-start | bytes 2308
  355.6 0.8 copy-start.3
  403.8 4.2 %copy-start.1 = (bf16[1,1024,1024]{2,1,0:T(8,128)(2,1)S(1)}, bf16[1,1024,1024]{2,1,0:T(8,128)(2,1)}, u32[]{:S(2)}) copy-start(bf16[1,1024,1024]{2,1,0:T(8,128)(2,1)} %param.23) | copy-start | bytes 6291460
  (4 other events, 2.3 us)
Sparse Core Ops, SparseCore 0:
  11.9 68.1 all-gather.2
  280.2 107.8 all-reduce.5

commit v2 on v1

--- a/solution.py
+++ b/solution.py
@@ -342,6 +342,467 @@
     )(part)
 
 
+def contract(a, b, left, right):
+    return lax.dot_general(
+        a, b, (((left,), (right,)), ((), ())), preferred_element_type=jnp.float32
+    )
+
+
+UP_OF_STEP = (0, 3, 1, 0, 2, 3, 1, 2)
+SIDE_OF_STEP = (0, 0, 0, 1, 0, 1, 1, 1)
+SLOTS = 128
+
+
+def select(table, step):
+    value = jnp.int32(table[0])
+    for place in range(1, len(table)):
+        if table[place] != table[place - 1]:
+            value = value + (table[place] - table[place - 1]) * jnp.minimum(
+                jnp.maximum(step - (place - 1), 0), 1
+            )
+    return value
+
+
+def expert_kernel(
+    cut, payload_ref, mix_ref, w_in_ref, w_out_ref, back_ref, mixture_ref, grads_ref,
+    arrived, mix_buf, w_in, w_out, blocks, weighted, rows_c, act_c, route_c, pre_c, mix_c, row_c,
+    near_mate, near_up, near_down, far_up, far_down, cross,
+    b_mate, b_near_up, b_near_down, b_far_up, b_far_down, b_cross,
+    local_sem, mix_sem, send_sem, recv_sem, a_send, a_recv, b_send, b_recv,
+):
+    me, rep, core, y, high = place()
+    width = payload_ref.shape[1]
+    rows = payload_ref.shape[0]
+    tokens = rows - 16
+    mate = (index_of(high, y, 1 - core), rep)
+    up = (index_of(high, y + 1, core), rep)
+    down = (index_of(high, y + 3, core), rep)
+    across = (index_of(1 - high, y, core), rep)
+
+    def chip_of(step):
+        side, turn = select(SIDE_OF_STEP, step), select(UP_OF_STEP, step)
+        return lax.rem(high + side, 2) * 4 + lax.rem(y + turn, 4)
+
+    load_in = pltpu.make_async_copy(w_in_ref, w_in, local_sem.at[0])
+    load_out = pltpu.make_async_copy(w_out_ref, w_out, local_sem.at[1])
+    load_own = pltpu.make_async_copy(payload_ref, arrived.at[me], local_sem.at[2])
+    load_in.start()
+    load_out.start()
+    load_own.start()
+
+    def load_mix(step):
+        slot = lax.rem(step, 2)
+        return pltpu.make_async_copy(
+            mix_ref.at[pl.ds(chip_of(step) * 2, 2)], mix_buf.at[slot], mix_sem.at[slot]
+        )
+
+    load_mix(0).start()
+    greet([mate, up, down, across])
+    whole, top, low = pl.ds(0, rows), pl.ds(0, cut), pl.ds(cut, rows - cut)
+    other = index_of(1 - high, y, core)
+    from_down = index_of(high, y + 3, core)
+    from_up = index_of(high, y + 1, core)
+    far = index_of(high, y + 2, core)
+    other_down = index_of(1 - high, y + 3, core)
+    other_up = index_of(1 - high, y + 1, core)
+    other_far = index_of(1 - high, y + 2, core)
+    plan = {
+        0: (me, whole, across),
+        1: (me, whole, up),
+        2: (me, whole, down),
+        3: (me, whole, mate),
+        4: (from_down, top, up),
+        5: (from_up, low, down),
+        6: (other, whole, up),
+        7: (other, whole, down),
+        8: (from_down, whole, mate),
+        9: (from_up, whole, mate),
+        10: (other, whole, mate),
+        11: (other_down, top, up),
+        12: (other_up, low, down),
+        13: (other_down, whole, mate),
+        14: (other_up, whole, mate),
+        15: (far, top, mate),
+        16: (far, low, mate),
+        17: (other_far, top, mate),
+        18: (other_far, low, mate),
+    }
+
+    def move(number):
+        slot, span, target = plan[number]
+        source = payload_ref if number < 4 else arrived.at[slot, span]
+        return pltpu.make_async_remote_copy(
+            src_ref=source,
+            dst_ref=arrived.at[slot, span],
+            send_sem=send_sem.at[number],
+            recv_sem=recv_sem.at[number],
+            device_id=target,
+            device_id_type=MESH,
+        )
+
+    for number in range(4):
+        move(number).start()
+    load_in.wait()
+    load_out.wait()
+    load_own.wait()
+
+    def picks(slot):
+        side = arrived[slot, pl.ds(tokens, 16), :].astype(jnp.float32)
+        line = lax.broadcasted_iota(jnp.int32, side.shape, 0)
+        own = jnp.sum(jnp.where(line == me, side, 0.0), axis=0, keepdims=True)
+        gates = own[:, :tokens] + own[:, 256 : 256 + tokens]
+        place_of = own[:, 512 : 512 + tokens].astype(jnp.int32)
+        pick = place_of == lax.broadcasted_iota(jnp.int32, (SLOTS, tokens), 0)
+        return pick, gates
+
+    def swap(step, source, buffer, sems):
+        return pltpu.make_async_remote_copy(
+            src_ref=source.at[2 * chip_of(step) + 1 - core],
+            dst_ref=buffer.at[step],
+            send_sem=sems[0].at[step],
+            recv_sem=sems[1].at[step],
+            device_id=mate,
+            device_id_type=MESH,
+        )
+
+    def work(step, carry):
+        @pl.when(step == 0)
+        def _():
+            move(3).wait_recv()
+
+        @pl.when(step == 1)
+        def _():
+            move(1).wait_recv()
+            move(4).start()
+            move(8).start()
+            move(2).wait_recv()
+            move(5).start()
+            move(9).start()
+            move(0).wait_recv()
+            for number in (6, 7, 10):
+                move(number).start()
+            move(8).wait_recv()
+
+        @pl.when(step == 2)
+        def _():
+            move(9).wait_recv()
+
+        @pl.when(step == 3)
+        def _():
+            move(10).wait_recv()
+
+        @pl.when(step == 4)
+        def _():
+            move(6).wait_recv()
+            move(11).start()
+            move(13).start()
+            move(7).wait_recv()
+            move(12).start()
+            move(14).start()
+            move(4).wait_recv()
+            move(15).start()
+            move(5).wait_recv()
+            move(16).start()
+            move(15).wait_recv()
+            move(16).wait_recv()
+
+        @pl.when(step == 5)
+        def _():
+            move(13).wait_recv()
+
+        @pl.when(step == 6)
+        def _():
+            move(14).wait_recv()
+
+        @pl.when(step == 7)
+        def _():
+            move(11).wait_recv()
+            move(17).start()
+            move(12).wait_recv()
+            move(18).start()
+            move(17).wait_recv()
+            move(18).wait_recv()
+
+        @pl.when(step < 7)
+        def _():
+            load_mix(step + 1).start()
+
+        load_mix(step).wait()
+        buffer = lax.rem(step, 2)
+        base = chip_of(step) * 2
+        both = 2 * SLOTS
+        at = pl.ds(pl.multiple_of(chip_of(step) * both, both), both)
+        kept = []
+        for b in range(2):
+            pick, gates = picks(base + b)
+            pick_b = pick.astype(jnp.bfloat16)
+            slot_gates = jnp.sum(jnp.where(pick, gates, 0.0), axis=1, keepdims=True)
+            here = pl.ds(b * SLOTS, SLOTS)
+            there = pl.ds(pl.multiple_of(chip_of(step) * both + b * SLOTS, SLOTS), SLOTS)
+            rows_c[there, :] = contract(
+                pick_b, arrived[base + b, pl.ds(0, tokens), :], 1, 0
+            ).astype(jnp.bfloat16)
+            mix_rows = contract(pick_b, mix_buf[buffer, b], 1, 0)
+            mix_c[here, :] = mix_rows.astype(jnp.bfloat16)
+            route_c[there, :] = (slot_gates * mix_rows).astype(jnp.bfloat16)
+            kept.append((pick, pick_b, slot_gates))
+        slot_gates = jnp.concatenate([kept[0][2], kept[1][2]], axis=0)
+        x, route = rows_c[at, :], route_c[at, :]
+
+        def inner(tile, carry):
+            left = pl.ds(pl.multiple_of(tile * 256, 256), 256)
+            right = pl.ds(pl.multiple_of(512 + tile * 256, 256), 256)
+            gate = contract(x, w_in[:, left], 1, 0)
+            raised = contract(x, w_in[:, right], 1, 0)
+            grad = contract(route, w_out[left, :], 1, 1)
+            sig = 1.0 / (1.0 + jnp.exp(-gate))
+            silu = gate * sig
+            act_c[at, left] = (silu * raised).astype(jnp.bfloat16)
+            pre_c[at, left] = (grad * raised * sig * (1.0 + gate * (1.0 - sig))).astype(
+                jnp.bfloat16
+            )
+            pre_c[at, right] = (grad * silu).astype(jnp.bfloat16)
+            return carry
+
+        lax.fori_loop(0, 2, inner, 0)
+        act, pre = act_c[at, :], pre_c[at, :]
+
+        def outer(tile, total):
+            span = pl.ds(pl.multiple_of(tile * 256, 256), 256)
+            result = contract(act, w_out[:, span], 1, 0).astype(jnp.bfloat16).astype(jnp.float32)
+            weighted[at, span] = (slot_gates * result).astype(jnp.bfloat16)
+            row_c[:, span] = contract(pre, w_in[span, :], 1, 1).astype(jnp.bfloat16)
+            return total + jnp.sum(
+                result * mix_c[:, span].astype(jnp.float32), axis=1, keepdims=True
+            )
+
+        gate_grad = lax.fori_loop(0, 4, outer, jnp.zeros((both, 1), jnp.float32))
+        for b in range(2):
+            pick, pick_b, _ = kept[b]
+            here = pl.ds(b * SLOTS, SLOTS)
+            blocks[base + b, pl.ds(0, tokens), :] = contract(pick_b, row_c[here, :], 0, 0).astype(
+                jnp.bfloat16
+            )
+            line_grad = jnp.sum(
+                jnp.where(pick, gate_grad[b * SLOTS : (b + 1) * SLOTS], 0.0), axis=0, keepdims=True
+            )
+            upper = line_grad.astype(jnp.bfloat16).astype(jnp.float32)
+            mine = lax.broadcasted_iota(jnp.int32, (16, tokens), 0) == me
+            tail = pl.ds(tokens, 16)
+            blocks[base + b, tail, :] = jnp.zeros((16, width), jnp.bfloat16)
+            blocks[base + b, tail, pl.ds(0, tokens)] = jnp.where(mine, upper, 0.0).astype(
+                jnp.bfloat16
+            )
+            blocks[base + b, tail, pl.ds(256, tokens)] = jnp.where(
+                mine, line_grad - upper, 0.0
+            ).astype(jnp.bfloat16)
+        swap(step, blocks, near_mate, (a_send, a_recv)).start()
+        return carry
+
+    lax.fori_loop(0, 8, work, 0)
+    for number in range(19):
+        move(number).wait_send()
+
+    class Sum:
+        def __init__(self, source, bufs, sems, count, split):
+            self.source, self.bufs, self.sems = source, bufs, sems
+            self.count, self.split = count, split
+            self.pending = {}
+
+        def block(self, step):
+            return self.source.at[2 * chip_of(jnp.int32(step)) + core]
+
+        def settle(self, step):
+            swap(jnp.int32(step), self.source, self.bufs[0], self.sems).wait_recv()
+            add_rows(self.block(step), self.bufs[0].at[step], 0, self.count)
+
+        def send(self, number, source, target_ref, target):
+            copy = pltpu.make_async_remote_copy(
+                src_ref=source,
+                dst_ref=target_ref,
+                send_sem=self.sems[0].at[number],
+                recv_sem=self.sems[1].at[number],
+                device_id=target,
+                device_id_type=MESH,
+            )
+            copy.start()
+            self.pending[number] = copy
+
+        def first(self, o):
+            step = (7, 4)[o]
+            self.settle(step)
+            block = self.block(step)
+            spans = pl.ds(0, self.split), pl.ds(self.split, self.count - self.split)
+            self.send(8 + o, block.at[spans[0]], self.bufs[3].at[o], up)
+            self.send(10 + o, block.at[spans[1]], self.bufs[4].at[o], down)
+
+        def second(self, o):
+            above, below = (6, 2)[o], (5, 1)[o]
+            self.settle(above)
+            self.settle(below)
+            self.pending[8 + o].wait_recv()
+            add_rows(self.block(above), self.bufs[3].at[o], 0, self.split)
+            self.send(12 + o, self.block(above), self.bufs[1].at[o], up)
+            self.pending[10 + o].wait_recv()
+            add_rows(self.block(below), self.bufs[4].at[o], self.split, self.count - self.split)
+            self.send(14 + o, self.block(below), self.bufs[2].at[o], down)
+
+        def third(self, o):
+            step = (3, 0)[o]
+            self.settle(step)
+            self.pending[12 + o].wait_recv()
+            add_rows(self.block(step), self.bufs[1].at[o], 0, self.count)
+            self.pending[14 + o].wait_recv()
+            add_rows(self.block(step), self.bufs[2].at[o], 0, self.count)
+            if o == 0:
+                self.send(16, self.block(step), self.bufs[5], across)
+
+        def last(self, out_ref):
+            self.pending[16].wait_recv()
+            own, beside = self.block(0), self.bufs[5]
+
+            def body(step, carry):
+                span = pl.ds(pl.multiple_of(step * 16, 16), 16)
+                out_ref[span, :] = own[span, :].astype(jnp.float32) + beside[span, :].astype(
+                    jnp.float32
+                )
+                return carry
+
+            lax.fori_loop(0, self.count // 16, body, 0)
+
+        def finish(self):
+            for step in range(8):
+                swap(jnp.int32(step), self.source, self.bufs[0], self.sems).wait_send()
+            for copy in self.pending.values():
+                copy.wait_send()
+
+    a = Sum(
+        blocks, (near_mate, near_up, near_down, far_up, far_down, cross), (a_send, a_recv),
+        rows, cut,
+    )
+    mixes = arrived.at[:, pl.ds(0, tokens)]
+    b = Sum(
+        mixes, (b_mate, b_near_up, b_near_down, b_far_up, b_far_down, b_cross), (b_send, b_recv),
+        tokens, 96,
+    )
+    a.first(0)
+    a.first(1)
+
+    def spread(turn, carry):
+        step = 7 - turn
+        for b in range(2):
+            slot = chip_of(step) * 2 + b
+            pick, _ = picks(slot)
+            here = pl.ds(pl.multiple_of(slot * SLOTS, SLOTS), SLOTS)
+            arrived[slot, pl.ds(0, tokens), :] = contract(
+                pick.astype(jnp.bfloat16), weighted[here, :], 0, 0
+            ).astype(jnp.bfloat16)
+        swap(step, mixes, b_mate, (b_send, b_recv)).start()
+        return carry
+
+    lax.fori_loop(0, 8, spread, 0)
+    a.second(0)
+    a.second(1)
+
+    def grad_in(tile, carry):
+        span = pl.ds(pl.multiple_of(tile * 256, 256), 256)
+        grads_ref[span, :] = contract(rows_c[:, span], pre_c[...], 0, 0).astype(jnp.bfloat16)
+        return carry
+
+    def grad_out(tile, carry):
+        span = pl.ds(pl.multiple_of(tile * 256, 256), 256)
+        there = pl.ds(pl.multiple_of(width + tile * 256, 256), 256)
+        grads_ref[there, :] = contract(act_c[:, span], route_c[...], 0, 0).astype(jnp.bfloat16)
+        return carry
+
+    b.first(0)
+    b.first(1)
+    lax.fori_loop(0, 2, grad_in, 0)
+    a.third(0)
+    a.third(1)
+    b.second(0)
+    lax.fori_loop(2, 4, grad_in, 0)
+    b.second(1)
+    a.last(back_ref)
+    lax.fori_loop(0, 2, grad_out, 0)
+    b.third(0)
+    b.third(1)
+    b.last(mixture_ref)
+    a.finish()
+    b.finish()
+
+
+def expert_layer(payload, mix, w_in, w_out, collective_id):
+    rows, width = payload.shape
+    tokens = rows - 16
+    hidden = w_out.shape[0]
+    cut = (rows // 16 + 1) // 2 * 16
+    half = 96
+    kind = jnp.bfloat16
+    slots = 16 * SLOTS
+    dma = pltpu.SemaphoreType.DMA
+
+    def sums(count, split):
+        return [
+            pltpu.VMEM((8, count, width), kind),
+            pltpu.VMEM((2, count, width), kind),
+            pltpu.VMEM((2, count, width), kind),
+            pltpu.VMEM((2, split, width), kind),
+            pltpu.VMEM((2, count - split, width), kind),
+            pltpu.VMEM((count, width), kind),
+        ]
+
+    return pl.pallas_call(
+        functools.partial(expert_kernel, cut),
+        out_shape=(
+            jax.ShapeDtypeStruct((rows, width), jnp.float32),
+            jax.ShapeDtypeStruct((tokens, width), jnp.float32),
+            jax.ShapeDtypeStruct((width + hidden, width), kind),
+        ),
+        in_specs=[
+            pl.BlockSpec(memory_space=pltpu.VMEM),
+            pl.BlockSpec(memory_space=pl.ANY),
+            pl.BlockSpec(memory_space=pl.ANY),
+            pl.BlockSpec(memory_space=pl.ANY),
+        ],
+        out_specs=(
+            pl.BlockSpec(memory_space=pltpu.VMEM),
+            pl.BlockSpec(memory_space=pltpu.VMEM),
+            pl.BlockSpec(memory_space=pltpu.VMEM),
+        ),
+        scratch_shapes=[
+            pltpu.VMEM((16, rows, width), kind),
+            pltpu.VMEM((2, 2, tokens, width), kind),
+            pltpu.VMEM((width, 2 * hidden), kind),
+            pltpu.VMEM((hidden, width), kind),
+            pltpu.VMEM((16, rows, width), kind),
+            pltpu.VMEM((slots, width), kind),
+            pltpu.VMEM((slots, width), kind),
+            pltpu.VMEM((slots, hidden), kind),
+            pltpu.VMEM((slots, width), kind),
+            pltpu.VMEM((slots, 2 * hidden), kind),
+            pltpu.VMEM((2 * SLOTS, width), kind),
+            pltpu.VMEM((2 * SLOTS, width), kind),
+            *sums(rows, cut),
+            *sums(tokens, half),
+            dma((3,)),
+            dma((2,)),
+            dma((19,)),
+            dma((19,)),
+            dma((17,)),
+            dma((17,)),
+            dma((17,)),
+            dma((17,)),
+        ],
+        compiler_params=pltpu.CompilerParams(
+            collective_id=collective_id, has_side_effects=True, vmem_limit_bytes=60 * 1024 * 1024
+        ),
+        cost_estimate=pl.CostEstimate(
+            flops=24 * 10**9, bytes_accessed=10**8, transcendentals=10**6
+        ),
+    )(payload, mix, w_in, w_out)
+
+
 def heads_first(rows, width):
     return rows.reshape(rows.shape[0], -1, width)
 
@@ -388,7 +849,6 @@
     rows, width = tokens.shape
     group = QUERY_HEADS // KEY_VALUE_HEADS
     scale = HEAD_SIZE ** (-0.5)
-    expert = lax.axis_index("shard")
     w_in, w_out = w_in[0], w_out[0]
     bf16, f32 = jnp.bfloat16, jnp.float32
 
@@ -452,63 +912,24 @@
     raised = jnp.exp(logits - jnp.max(logits, axis=1, keepdims=True))
     gates = raised / jnp.sum(raised, axis=1, keepdims=True)
 
-    def side_rows(table):
-        upper, lower = split_two(table)
-        return jnp.concatenate(
-            [jnp.pad(upper, ((0, 0), (0, 64))), jnp.pad(lower, ((0, 0), (0, 1024 - 448)))], axis=1
-        )
-
-    payload = jnp.concatenate([normed_second, side_rows(gates.T)], axis=0)
-    arrived = gather_rows(payload, 2)
-    own = lax.dynamic_slice(arrived, (0, rows + expert, 0), (16, 1, 448))[:, 0].astype(f32)
-    own_gates = own[:, :rows] + own[:, 256 : 256 + rows]
-    member = own_gates > 0
-    earlier = (row_index[:, None] < row_index[None, :]).astype(bf16)
-    rank = dot(member.astype(bf16), earlier).astype(jnp.int32)
-    slot_of = jnp.where(member, rank, -1)
-    pick = slot_of[:, None, :] == jnp.arange(CAP, dtype=jnp.int32)[None, :, None]
-    pick_b = pick.astype(bf16)
-    slot_gates = jnp.sum(jnp.where(pick, own_gates[:, None, :], 0.0), axis=2)[:, :, None]
-
-    expert_rows = einsum("srt,std->srd", pick_b, arrived[:, :rows]).astype(bf16)
-    mix_rows = einsum("srt,std->srd", pick_b, all_mix_grad).astype(bf16)
-    expert_rows = expert_rows.reshape(16 * CAP, width)
-    pre_act = dot(expert_rows, w_in)
-    gate, up = pre_act[:, :H], pre_act[:, H:]
-    sig = jax.nn.sigmoid(gate)
-    silu = gate * sig
-    activation = (silu * up).astype(bf16)
-    expert_out = dot(activation, w_out).astype(bf16).astype(f32).reshape(16, CAP, width)
-    mix_rows = mix_rows.astype(f32)
-    slot_gate_grad = jnp.sum(expert_out * mix_rows, axis=2, keepdims=True)
-    weighted = (slot_gates * expert_out).astype(bf16)
-    route_grad = (slot_gates * mix_rows).astype(bf16).reshape(16 * CAP, width)
-    activation_grad = einsum("rd,hd->rh", route_grad, w_out)
-    pre_grad = jnp.concatenate(
-        [activation_grad * up * sig * (1 + gate * (1 - sig)), activation_grad * silu], axis=1
-    ).astype(bf16)
-    grad_in = einsum("rd,rf->df", expert_rows, pre_grad)
-    grad_out = einsum("rh,rd->hd", activation, route_grad)
-    expert_grads = lax.psum(jnp.concatenate([grad_in, grad_out], axis=0).astype(bf16), "replica")
-    row_grad = einsum("rf,df->rd", pre_grad, w_in).astype(bf16).reshape(16, CAP, width)
-    returned = einsum(
-        "srt,srd->std", pick_b, jnp.concatenate([weighted, row_grad], axis=2)
-    ).astype(bf16)
-    token_gate_grad = jnp.sum(jnp.where(pick, slot_gate_grad, 0.0), axis=1)
-    upper, lower = split_two(token_gate_grad)
+    earlier = (row_index[:, None] > row_index[None, :]).astype(bf16)
+    rank = dot(earlier, named.astype(bf16))
+    place_of = jnp.where(named, rank, -1.0).T.astype(bf16)
+    upper, lower = split_two(gates.T)
+    gap = jnp.zeros((E, 64), bf16)
     side = jnp.concatenate(
-        [jnp.pad(upper, ((0, 0), (0, 64))), jnp.pad(lower, ((0, 0), (0, 2048 - 448)))], axis=1
-    )
-    mine = (jnp.arange(E) == expert)[None, :, None]
-    side = jnp.where(mine, side[:, None, :], 0).astype(bf16)
-    back = scatter_rows(jnp.concatenate([returned, side], axis=1), 3, f32)
-
-    output = (hidden_one + live * back[:rows, :width]).astype(bf16)
+        [upper, gap, lower, gap, place_of, jnp.zeros((E, width - 512 - rows), bf16)], axis=1
+    )
+    payload = jnp.concatenate([normed_second, side], axis=0)
+    back, mixture, expert_grads = expert_layer(payload, all_mix_grad, w_in, w_out, 2)
+    expert_grads = lax.psum(expert_grads, "replica")
+
+    output = (hidden_one + live * mixture).astype(bf16)
     gate_grad = (back[rows:, :rows] + back[rows:, 256 : 256 + rows]).T
     logit_grad = (gates * (gate_grad - jnp.sum(gates * gate_grad, axis=1, keepdims=True))).astype(
         bf16
     )
-    normed_second_grad = back[:rows, width:] + einsum("te,de->td", logit_grad, full_router)
+    normed_second_grad = back[:rows] + einsum("te,de->td", logit_grad, full_router)
     d_router = einsum("td,te->de", normed_second, logit_grad)
     d_ffn_gain = jnp.sum(normed_second_grad * hidden_one * scale_second, axis=0)
     gained = normed_second_grad * gain_second

time: 422 us -> 343 us (0.81); the launches traced: 415 us -> 341 us
  matrix products: 80.6 us -> 29.6 us
  other arithmetic: 36.3 us -> 14.7 us
  local copies, waits for them, and re-layouts: 50.4 us -> 41.3 us
  Pallas kernels: 231 us -> 240 us
    pallas_call x0 -> x1, Pallas kernels: none -> 111 us  [expert_layer(): pl.pallas_call(functools.partial(expert_kernel, cut), out_shape=(jax.Shap...]
    pallas_call x2 -> x1, Pallas kernels: 111 us -> 43.5 us  [scatter_rows(): pl.pallas_call(functools.partial(scatter_kernel, cut), out_shape=jax.Shap...]
    dot_general x18 -> x11, matrix products: 60.3 us -> 19.5 us  [einsum(): return jnp.einsum(form, a, b, preferred_element_type=jnp.float32)]
    pallas_call x2 -> x1, Pallas kernels: 83.8 us -> 47 us  [gather_rows(): pl.pallas_call(functools.partial(gather_kernel, cut), out_shape=jax.Shape...]
    concatenate x4 -> x1, other arithmetic: 11.4 us -> 0.79 us  [local(): payload = jnp.concatenate([normed_second, side], axis=0)]
    dot_general x6 -> x4, matrix products: 16.1 us -> 7.19 us  [dot(): return jnp.dot(a, b, preferred_element_type=jnp.float32)]
    unnamed x135 -> x68, local copies, waits for them, and re-layouts: 15.9 us -> 11 us
    convert_element_type x4 -> x0, other arithmetic: 4.85 us -> none  [the longest x1 2.73 us: local(): weighted = (slot_gates * expert_out).astype(bf16)]
  transfers between devices with their start and end apart: 2 -> 2, of which waited for: 0 -> 0; matrix products, arithmetic and copies ran while one was open for 19% -> 16% of each run, Pallas kernels for 40% -> 38%
where the time goes in v2:
time: 343 us; the launch traced here: 341 us
  Pallas kernels  240 us (70%)
  local copies, waits for them, and re-layouts  41.3 us (12%)
  matrix products  29.6 us (9%)
  between operations  15.8 us (5%)
  other arithmetic  14.7 us (4%)
    pallas_call x1, Pallas kernels, expert_layer(): pl.pallas_call(functools.partial(expert_kernel, cut), out_shape=(jax.Shap...  111 us
    pallas_call x1, Pallas kernels, gather_rows(): pl.pallas_call(functools.partial(gather_kernel, cut), out_shape=jax.Shape...  47 us
    pallas_call x1, Pallas kernels, scatter_rows(): pl.pallas_call(functools.partial(scatter_kernel, cut), out_shape=jax.Shap...  43.5 us
    pallas_call x1, Pallas kernels, total_rows(): pl.pallas_call(total_kernel, out_shape=jax.ShapeDtypeStruct((rows, width)...  38.5 us
    dot_general x11, matrix products, einsum(): return jnp.einsum(form, a, b, preferred_element_type=jnp.float32)  19.5 us
    unnamed x68, local copies, waits for them, and re-layouts  11 us
    concatenate x1, local copies, waits for them, and re-layouts, local(): jnp.concatenate([d_qkv, d_output, d_router.astype(bf16), jnp.tile(gains,...  10.5 us
    dot_general x4, matrix products, dot(): return jnp.dot(a, b, preferred_element_type=jnp.float32)  7.19 us
  transfers between devices with their start and end apart: 2, of which 0 were waited for; matrix products, arithmetic and copies ran while one was open for 16% of the time, Pallas kernels for 38%

profile of v2, /device:TPU:8, one launch (start us, length us, event | category | flops | bytes accessed | tf_op | source)
XLA Modules:
  0.0 341.5 jit_solution(15709424753393535309)
XLA Ops:
  7.2 1.3 fusion.66
  9.8 1.8 broadcast_multiply_fusion
  11.8 0.8 copy.51
  12.6 1.9 concatenate.36.block_ref
  14.4 47.0 %shard_map.212 = bf16[16,64,3328]{2,1,0:T(8,128)(2,1)} custom-call(bf16[64,3328]{1,0:T(8,128)(2,1)} %concatenate.36.block_ref), custom_call_target="tpu_custom_call" | custom-call | bytes 54525952 | tf_op jit(solution)/shard_map/pallas_call | solution.py:125
  61.6 0.6 multiply_multiply_fusion
  62.2 3.2 fusion.3
  65.5 1.1 copy-done.10
  66.7 0.5 copy.53
  67.2 0.7 subtract_convert_fusion.3
  67.8 0.8 fusion.54
  68.7 0.2 subtract_convert_fusion.1
  69.1 0.8 slice.115
  69.9 0.7 slice.114
  70.6 1.0 slice.169
  71.6 0.8 copy.52
  72.5 0.6 fusion.56
  73.1 0.7 fusion.42
  73.8 2.9 fusion.67
  76.7 1.6 convolution_convert_fusion.2
  78.4 2.6 multiply_reduce_fusion.2
  81.1 1.2 fusion.55
  82.7 0.8 pad_maximum_fusion.6.payload_ref
  83.5 111.0 %shard_map.213 = (f32[208,1024]{1,0:T(8,128)}, f32[192,1024]{1,0:T(8,128)}, bf16[1536,1024]{1,0:T(8,128)(2,1)}) custom-call(bf16[208,1024]{1,0:T(8,128)(2,1)} %pad_maximum_fusion.6.payload_ref, bf16[16,192,1024]{2,1,0:T(8,128)(2,1)} %bitcast.153, bf16[1024,1024]{1,0:T(8,128)(2,1)} %bitcast.154, bf16[512,1024]{1,0:T(8,128)(2,1)} %bitcast.155), custom_call_target="tpu_custom_call" | custom-call | flops 24000000000 | bytes 100000000 | tf_op jit(solution)/shard_map/pallas_call | solution.py:755
  194.5 0.8 fusion.46
  195.2 1.8 multiply_reduce_fusion
  197.0 2.2 multiply_subtract_fusion
  199.3 2.5 fusion.21
  202.0 2.8 fusion.5
  204.8 0.2 copy-done.6
  205.0 0.7 fusion.7
  205.7 0.3 copy-done.11
  206.0 0.4 convolution_multiply_fusion
  206.4 0.6 copy-done.8
  207.0 0.6 fusion.24
  207.8 0.6 copy-done.17
  208.4 0.3 subtract_convert_fusion
  208.8 0.8 copy-done.7
  209.7 0.6 fusion.25
  210.3 0.2 copy-done.3
  210.6 0.9 slice-done
  211.4 0.7 slice-done.1
  212.2 3.0 fusion.34
  215.3 0.9 convolution_convert_fusion.3
  216.5 1.9 convolution_convert_fusion.1
  218.4 3.5 %convolution_convert_fusion = bf16[1024,2048]{1,0:T(8,128)(2,1)} fusion(bf16[192,512]{0,1:T(8,128)(2,1)S(1)} %bitcast.150, bf16[192,1536]{0,1:T(8,128)(2,1)S(1)} %bitcast.136, bf16[192,1024]{1,0:T(8,128)(2,1)S(1)} %copy-done.2, f32[1024]{0:T(1024)S(1)} %convert_element_type.124, f32[192]{0:T(256)S(1)} %get-tuple-element.72), kind=kOutput, calls=%fused_computation.2 | convolution fusion | flops 809762816 | bytes 5378816 | tf_op jit(solution)/shard_map/td,tc->dc/dot_general | solution.py:826
  221.9 0.8 tile.2
  222.6 0.8 broadcast_in_dim.93
  223.5 10.5 %concatenate.47.blocks_ref = bf16[16,64,3328]{2,1,0:T(8,128)(2,1)} concatenate(bf16[16,64,2048]{2,1,0:T(8,128)(2,1)} %bitcast.122, bf16[16,64,1024]{2,1,0:T(8,128)(2,1)S(1)} %bitcast.123, bf16[16,64,16]{2,1,0:T(8,128)(2,1)S(1)} %bitcast.142, bf16[16,64,32]{2,1,0:T(8,128)(2,1)} %tile.2, bf16[16,64,208]{2,1,0:T(8,128)(2,1)} %broadcast_in_dim.93), dimensions={2} | concatenate | bytes 13631488 | tf_op jit(solution)/shard_map/concatenate | solution.py:969
  234.0 3.0 copy-done
  237.0 43.5 %shard_map.214.part_ref = bf16[64,3328]{1,0:T(8,128)(2,1)S(1)} custom-call(bf16[16,64,3328]{2,1,0:T(8,128)(2,1)S(1)} %copy-done), custom_call_target="tpu_custom_call" | custom-call | bytes 54525952 | tf_op jit(solution)/shard_map/pallas_call | solution.py:250
  280.5 0.7 copy-done.1
  281.2 38.5 %shard_map.215 = bf16[64,3328]{1,0:T(8,128)(2,1)} custom-call(bf16[64,3328]{1,0:T(8,128)(2,1)} %copy-done.1), custom_call_target="tpu_custom_call" | custom-call | tf_op jit(solution)/shard_map/pallas_call | solution.py:329
  319.8 0.7 slice.126
  320.5 0.7 copy.60
  321.1 0.8 fusion.65
  321.9 0.7 squeeze.28
  322.6 0.7 squeeze.29
  323.3 1.6 fusion.64
  324.9 1.8 fusion.63
  326.7 1.1 fusion.31
  327.8 2.6 convert_element_type.153
  330.5 2.6 slice_bitcast_fusion
  333.1 1.6 slice_bitcast_fusion.1
  (88 shorter events, 2.1 us)
Async XLA Ops:
  7.2 76.3 %all-gather.3.cloned.1.call-start = ((), (), s32[]{:S(2)}) async-start(), calls=%async_computation.1 | async-start | bytes 6684672 | tf_op jit(solution)/shard_map/all_gather | solution.py:885
  11.7 316.1 %all-reduce.2.cloned.1.call-start = ((), (), s32[]{:S(2)}) async-start(), calls=%async_computation | async-start | bytes 6291456 | tf_op jit(solution)/shard_map/psum | solution.py:925
  14.4 47.0 %copy-start.28 = (bf16[1024]{0:T(1024)(128)(2,1)S(1)}, bf16[1024]{0:T(1024)(128)(2,1)}, u32[]{:S(2)}) copy-start(bf16[1024]{0:T(1024)(128)(2,1)} %param.16) | copy-start | bytes 6148
  14.4 47.0 %copy-start.2 = (bf16[192,1024]{1,0:T(8,128)(2,1)S(1)}, bf16[192,1024]{1,0:T(8,128)(2,1)}, u32[]{:S(2)}) copy-start(bf16[192,1024]{1,0:T(8,128)(2,1)} %param.13) | copy-start | bytes 1179652
  65.5 1.1 copy-start.10
  68.7 1.9 copy-start.16
  68.7 3.8 %copy-start.29 = (bf16[1024]{0:T(1024)(128)(2,1)S(1)}, bf16[1024]{0:T(1024)(128)(2,1)}, u32[]{:S(2)}) copy-start(bf16[1024]{0:T(1024)(128)(2,1)} %param.17) | copy-start | bytes 6148
  68.7 4.4 %copy-start.23 = (s32[192,8]{0,1:T(8,128)S(1)}, s32[192,8]{0,1:T(8,128)}, u32[]{:S(2)}) copy-start(s32[192,8]{0,1:T(8,128)} %param.15) | copy-start | bytes 18436
  76.7 1.7 copy-start.5
  76.7 1.7 copy-start.25
  78.4 4.2 %copy-start.13 = (bf16[8,64,2,192]{3,1,2,0:T(8,128)(2,1)}, bf16[8,64,2,192]{3,1,2,0:T(8,128)(2,1)S(1)}, u32[]{:S(2)}) copy-start(bf16[8,64,2,192]{3,1,2,0:T(8,128)(2,1)S(1)} %convolution_convert_fusion.2) | copy-start | bytes 1179652
  83.5 113.5 %copy-start.9 = (bf16[192,1024]{1,0:T(8,128)(2,1)S(1)}, bf16[192,1024]{1,0:T(8,128)(2,1)}, u32[]{:S(2)}) copy-start(bf16[192,1024]{1,0:T(8,128)(2,1)} %param.25) | copy-start | bytes 1179652
  83.5 113.5 %copy-start.26 = (f32[192]{0:T(256)S(1)}, f32[192]{0:T(256)}, u32[]{:S(2)}) copy-start(f32[192]{0:T(256)} %fusion.56) | copy-start | bytes 2308
  199.3 2.7 copy-start.20
  199.3 2.7 copy-start.22
  202.0 2.8 copy-start.14
  202.0 3.0 copy-start.6
  205.0 0.9 copy-start.11
  206.0 1.0 copy-start.8
  207.6 0.8 copy-start.17
  207.6 0.8 copy-start.21
  207.7 1.9 copy-start.7
  207.7 2.0 copy-start.15
  208.4 3.0 slice-start
  209.7 0.9 copy-start.3
  209.7 2.5 slice-start.1
  210.3 4.9 %copy-start.18 = (bf16[8,64,192]{2,1,0:T(8,128)(2,1)}, bf16[8,64,192]{2,1,0:T(8,128)(2,1)S(1)}, u32[]{:S(2)}) copy-start(bf16[8,64,192]{2,1,0:T(8,128)(2,1)S(1)} %fusion.25) | copy-start | bytes 589828
  212.2 4.3 %copy-start.27 = (f32[192]{0:T(256)S(1)}, f32[192]{0:T(256)}, u32[]{:S(2)}) copy-start(f32[192]{0:T(256)} %fusion.56) | copy-start | bytes 2308
  216.4 1.9 copy-start.4
  216.4 1.9 copy-start.19
  234.0 3.0 copy-start
  237.0 86.3 %copy-start.30 = (f32[192]{0:T(256)S(1)}, f32[192]{0:T(256)}, u32[]{:S(2)}) copy-start(f32[192]{0:T(256)} %get-tuple-element.53) | copy-start | bytes 2308
  237.0 89.7 %copy-start.12 = (f32[192,1024]{1,0:T(8,128)S(1)}, f32[192,1024]{1,0:T(8,128)}, u32[]{:S(2)}) copy-start(f32[192,1024]{1,0:T(8,128)} %get-tuple-element.86) | copy-start | bytes 2359300
  237.0 89.7 %copy-start.24 = (f32[192]{0:T(256)S(1)}, f32[192]{0:T(256)}, u32[]{:S(2)}) copy-start(f32[192]{0:T(256)} %get-tuple-element.71) | copy-start | bytes 2308
  280.5 0.8 copy-start.1
Sparse Core Ops, SparseCore 0:
  11.8 68.2 all-gather.2
  207.8 108.1 all-reduce.1

commit v3 on v2

v3 whole, which is shorter than its diff:
```python
import functools
import math

import jax
import jax.numpy as jnp
from jax import lax
from jax.experimental import pallas as pl
from jax.experimental.pallas import tpu as pltpu
from jax.sharding import PartitionSpec as P

QUERY_HEADS = 16
KEY_VALUE_HEADS = 8
HEAD_SIZE = 64
H = 512
E = 16
CAP = 120

EPS = 1e-06
ROPE_BASE = 10000.0
NEGATIVE = -1e30

MESH = pl.DeviceIdType.MESH


def place():
    me = lax.axis_index("shard")
    rep = lax.axis_index("replica")
    core = lax.rem(me, 2)
    y = lax.rem(me // 2, 4)
    high = me // 8
    return me, rep, core, y, high


def index_of(high, y, core):
    return (high * 4 + lax.rem(y, 4)) * 2 + core


def greet(targets):
    barrier = pltpu.get_barrier_semaphore()
    for target in targets:
        pl.semaphore_signal(barrier, inc=1, device_id=target, device_id_type=MESH)
    pl.semaphore_wait(barrier, len(targets))


def add_rows(target, source, start, count):
    def body(step, carry):
        at = pl.ds(pl.multiple_of(start + step * 16, 16), 16)
        here = pl.ds(pl.multiple_of(step * 16, 16), 16)
        target[at, :] = (
            target[at, :].astype(jnp.float32) + source[here, :].astype(jnp.float32)
        ).astype(target.dtype)
        return carry

    lax.fori_loop(0, count // 16, body, 0)


def contract(a, b, left, right):
    return lax.dot_general(
        a, b, (((left,), (right,)), ((), ())), preferred_element_type=jnp.float32
    )


UP_OF_STEP = (0, 3, 1, 0, 2, 3, 1, 2)
SIDE_OF_STEP = (0, 0, 0, 1, 0, 1, 1, 1)
SLOTS = 128


def select(table, step):
    value = jnp.int32(table[0])
    for place in range(1, len(table)):
        if table[place] != table[place - 1]:
            value = value + (table[place] - table[place - 1]) * jnp.minimum(
                jnp.maximum(step - (place - 1), 0), 1
            )
    return value


def expert_kernel(
    cut, payload_ref, mix_ref, w_in_ref, w_out_ref, back_ref, mixture_ref, grads_ref,
    arrived, mix_buf, w_in, w_out, blocks, weighted, rows_c, act_c, route_c, pre_c, mix_c, row_c,
    near_mate, near_up, near_down, far_up, far_down, cross,
    a_send, a_recv, local_sem, mix_sem, store_sem, send_sem, recv_sem,
):
    me, rep, core, y, high = place()
    width = payload_ref.shape[1]
    rows = payload_ref.shape[0]
    tokens = rows - 16
    mate = (index_of(high, y, 1 - core), rep)
    up = (index_of(high, y + 1, core), rep)
    down = (index_of(high, y + 3, core), rep)
    across = (index_of(1 - high, y, core), rep)

    load_in = pltpu.make_async_copy(w_in_ref, w_in, local_sem.at[0])
    load_out = pltpu.make_async_copy(w_out_ref, w_out, local_sem.at[1])
    load_own = pltpu.make_async_copy(payload_ref, arrived.at[me], local_sem.at[2])
    load_in.start()
    load_out.start()
    load_own.start()

    def load_mix(step):
        slot = lax.rem(step, 2)
        return pltpu.make_async_copy(
            mix_ref.at[pl.ds(chip_of(step) * 2, 2)], mix_buf.at[slot], mix_sem.at[slot]
        )

    load_mix(0).start()
    greet([mate, up, down, across])
    whole, top, low = pl.ds(0, rows), pl.ds(0, cut), pl.ds(cut, rows - cut)
    other = index_of(1 - high, y, core)
    from_down = index_of(high, y + 3, core)
    from_up = index_of(high, y + 1, core)
    far = index_of(high, y + 2, core)
    other_down = index_of(1 - high, y + 3, core)
    other_up = index_of(1 - high, y + 1, core)
    other_far = index_of(1 - high, y + 2, core)
    plan = {
        0: (me, whole, across),
        1: (me, whole, up),
        2: (me, whole, down),
        3: (me, whole, mate),
        4: (from_down, top, up),
        5: (from_up, low, down),
        6: (other, whole, up),
        7: (other, whole, down),
        8: (from_down, whole, mate),
        9: (from_up, whole, mate),
        10: (other, whole, mate),
        11: (other_down, top, up),
        12: (other_up, low, down),
        13: (other_down, whole, mate),
        14: (other_up, whole, mate),
        15: (far, top, mate),
        16: (far, low, mate),
        17: (other_far, top, mate),
        18: (other_far, low, mate),
    }

    def move(number):
        slot, span, target = plan[number]
        source = payload_ref if number < 4 else arrived.at[slot, span]
        return pltpu.make_async_remote_copy(
            src_ref=source,
            dst_ref=arrived.at[slot, span],
            send_sem=send_sem.at[number],
            recv_sem=recv_sem.at[number],
            device_id=target,
            device_id_type=MESH,
        )

    for number in range(4):
        move(number).start()
    load_in.wait()
    load_out.wait()
    load_own.wait()

    def picks(slot):
        side = arrived[slot, pl.ds(tokens, 16), :].astype(jnp.float32)
        line = lax.broadcasted_iota(jnp.int32, side.shape, 0)
        own = jnp.sum(jnp.where(line == me, side, 0.0), axis=0, keepdims=True)
        gates = own[:, :tokens] + own[:, 256 : 256 + tokens]
        place_of = own[:, 512 : 512 + tokens].astype(jnp.int32)
        pick = place_of == lax.broadcasted_iota(jnp.int32, (SLOTS, tokens), 0)
        return pick, gates

    a = Scatter(
        blocks, None, (near_mate, near_up, near_down, far_up, far_down, cross), (a_send, a_recv),
        cut,
    )

    def work(step, carry):
        @pl.when(step == 0)
        def _():
            move(3).wait_recv()

        @pl.when(step == 1)
        def _():
            move(1).wait_recv()
            move(4).start()
            move(8).start()
            move(2).wait_recv()
            move(5).start()
            move(9).start()
            move(0).wait_recv()
            for number in (6, 7, 10):
                move(number).start()
            move(8).wait_recv()

        @pl.when(step == 2)
        def _():
            move(9).wait_recv()

        @pl.when(step == 3)
        def _():
            move(10).wait_recv()

        @pl.when(step == 4)
        def _():
            move(6).wait_recv()
            move(11).start()
            move(13).start()
            move(7).wait_recv()
            move(12).start()
            move(14).start()
            move(4).wait_recv()
            move(15).start()
            move(5).wait_recv()
            move(16).start()
            move(15).wait_recv()
            move(16).wait_recv()

        @pl.when(step == 5)
        def _():
            move(13).wait_recv()

        @pl.when(step == 6)
        def _():
            move(14).wait_recv()

        @pl.when(step == 7)
        def _():
            move(11).wait_recv()
            move(17).start()
            move(12).wait_recv()
            move(18).start()
            move(17).wait_recv()
            move(18).wait_recv()

        @pl.when(step < 7)
        def _():
            load_mix(step + 1).start()

        load_mix(step).wait()
        buffer = lax.rem(step, 2)
        base = chip_of(step) * 2
        both = 2 * SLOTS
        at = pl.ds(pl.multiple_of(chip_of(step) * both, both), both)
        kept = []
        for b in range(2):
            pick, gates = picks(base + b)
            pick_b = pick.astype(jnp.bfloat16)
            slot_gates = jnp.sum(jnp.where(pick, gates, 0.0), axis=1, keepdims=True)
            here = pl.ds(b * SLOTS, SLOTS)
            there = pl.ds(pl.multiple_of(chip_of(step) * both + b * SLOTS, SLOTS), SLOTS)
            rows_c[there, :] = contract(
                pick_b, arrived[base + b, pl.ds(0, tokens), :], 1, 0
            ).astype(jnp.bfloat16)
            mix_rows = contract(pick_b, mix_buf[buffer, b], 1, 0)
            mix_c[here, :] = mix_rows.astype(jnp.bfloat16)
            route_c[there, :] = (slot_gates * mix_rows).astype(jnp.bfloat16)
            kept.append((pick, pick_b, slot_gates))
        slot_gates = jnp.concatenate([kept[0][2], kept[1][2]], axis=0)
        x, route = rows_c[at, :], route_c[at, :]

        def inner(tile, carry):
            left = pl.ds(pl.multiple_of(tile * 256, 256), 256)
            right = pl.ds(pl.multiple_of(512 + tile * 256, 256), 256)
            gate = contract(x, w_in[:, left], 1, 0)
            raised = contract(x, w_in[:, right], 1, 0)
            grad = contract(route, w_out[left, :], 1, 1)
            sig = 1.0 / (1.0 + jnp.exp(-gate))
            silu = gate * sig
            act_c[at, left] = (silu * raised).astype(jnp.bfloat16)
            pre_c[at, left] = (grad * raised * sig * (1.0 + gate * (1.0 - sig))).astype(
                jnp.bfloat16
            )
            pre_c[at, right] = (grad * silu).astype(jnp.bfloat16)
            return carry

        lax.fori_loop(0, 2, inner, 0)
        act, pre = act_c[at, :], pre_c[at, :]

        def outer(tile, total):
            span = pl.ds(pl.multiple_of(tile * 256, 256), 256)
            result = contract(act, w_out[:, span], 1, 0).astype(jnp.bfloat16).astype(jnp.float32)
            weighted[at, span] = (slot_gates * result).astype(jnp.bfloat16)
            row_c[:, span] = contract(pre, w_in[span, :], 1, 1).astype(jnp.bfloat16)
            return total + jnp.sum(
                result * mix_c[:, span].astype(jnp.float32), axis=1, keepdims=True
            )

        gate_grad = lax.fori_loop(0, 4, outer, jnp.zeros((both, 1), jnp.float32))
        for b in range(2):
            pick, pick_b, _ = kept[b]
            here = pl.ds(b * SLOTS, SLOTS)
            blocks[base + b, pl.ds(0, tokens), :] = contract(pick_b, row_c[here, :], 0, 0).astype(
                jnp.bfloat16
            )
            line_grad = jnp.sum(
                jnp.where(pick, gate_grad[b * SLOTS : (b + 1) * SLOTS], 0.0), axis=0, keepdims=True
            )
            upper = line_grad.astype(jnp.bfloat16).astype(jnp.float32)
            mine = lax.broadcasted_iota(jnp.int32, (16, tokens), 0) == me
            tail = pl.ds(tokens, 16)
            blocks[base + b, tail, :] = jnp.zeros((16, width), jnp.bfloat16)
            blocks[base + b, tail, pl.ds(0, tokens)] = jnp.where(mine, upper, 0.0).astype(
                jnp.bfloat16
            )
            blocks[base + b, tail, pl.ds(256, tokens)] = jnp.where(
                mine, line_grad - upper, 0.0
            ).astype(jnp.bfloat16)
        a.swap(step).start()
        return carry

    lax.fori_loop(0, 8, work, 0)
    for number in range(19):
        move(number).wait_send()

    a.first(0)
    a.first(1)

    def store(step):
        chip = chip_of(step) * 2
        return pltpu.make_async_copy(
            arrived.at[pl.ds(chip, 2), pl.ds(0, tokens)],
            mixture_ref.at[pl.ds(chip, 2)],
            store_sem.at[step],
        )

    def spread(step, carry):
        for b in range(2):
            slot = chip_of(step) * 2 + b
            pick, _ = picks(slot)
            here = pl.ds(pl.multiple_of(slot * SLOTS, SLOTS), SLOTS)
            arrived[slot, pl.ds(0, tokens), :] = contract(
                pick.astype(jnp.bfloat16), weighted[here, :], 0, 0
            ).astype(jnp.bfloat16)
        store(step).start()
        return carry

    def grad_in(tile, carry):
        span = pl.ds(pl.multiple_of(tile * 256, 256), 256)
        grads_ref[span, :] = contract(rows_c[:, span], pre_c[...], 0, 0).astype(jnp.bfloat16)
        return carry

    def grad_out(tile, carry):
        span = pl.ds(pl.multiple_of(tile * 256, 256), 256)
        there = pl.ds(pl.multiple_of(width + tile * 256, 256), 256)
        grads_ref[there, :] = contract(act_c[:, span], route_c[...], 0, 0).astype(jnp.bfloat16)
        return carry

    def give_back(span, value):
        back_ref[span, :] = value

    lax.fori_loop(0, 8, spread, 0)
    a.second(0)
    lax.fori_loop(0, 1, grad_in, 0)
    a.second(1)
    lax.fori_loop(1, 4, grad_in, 0)
    a.third(0)
    lax.fori_loop(0, 2, grad_out, 0)
    a.third(1)
    a.last(give_back)
    a.finish()

    def stored(step, carry):
        store(step).wait()
        return carry

    lax.fori_loop(0, 8, stored, 0)


def expert_layer(payload, mix, w_in, w_out, collective_id):
    rows, width = payload.shape
    tokens = rows - 16
    hidden = w_out.shape[0]
    cut = (rows // 16 + 1) // 2 * 16
    kind = jnp.bfloat16
    slots = 16 * SLOTS
    dma = pltpu.SemaphoreType.DMA

    return pl.pallas_call(
        functools.partial(expert_kernel, cut),
        out_shape=(
            jax.ShapeDtypeStruct((rows, width), jnp.float32),
            jax.ShapeDtypeStruct((16, tokens, width), kind),
            jax.ShapeDtypeStruct((width + hidden, width), kind),
        ),
        in_specs=[
            pl.BlockSpec(memory_space=pl.ANY),
            pl.BlockSpec(memory_space=pl.ANY),
            pl.BlockSpec(memory_space=pl.ANY),
            pl.BlockSpec(memory_space=pl.ANY),
        ],
        out_specs=(
            pl.BlockSpec(memory_space=pltpu.VMEM),
            pl.BlockSpec(memory_space=pl.ANY),
            pl.BlockSpec(memory_space=pltpu.VMEM),
        ),
        scratch_shapes=[
            pltpu.VMEM((16, rows, width), kind),
            pltpu.VMEM((2, 2, tokens, width), kind),
            pltpu.VMEM((width, 2 * hidden), kind),
            pltpu.VMEM((hidden, width), kind),
            pltpu.VMEM((16, rows, width), kind),
            pltpu.VMEM((slots, width), kind),
            pltpu.VMEM((slots, width), kind),
            pltpu.VMEM((slots, hidden), kind),
            pltpu.VMEM((slots, width), kind),
            pltpu.VMEM((slots, 2 * hidden), kind),
            pltpu.VMEM((2 * SLOTS, width), kind),
            pltpu.VMEM((2 * SLOTS, width), kind),
            *scatter_scratch(rows, width, cut),
            dma((3,)),
            dma((2,)),
            dma((8,)),
            dma((19,)),
            dma((19,)),
        ],
        compiler_params=pltpu.CompilerParams(
            collective_id=collective_id, has_side_effects=True, vmem_limit_bytes=60 * 1024 * 1024
        ),
        cost_estimate=pl.CostEstimate(
            flops=24 * 10**9, bytes_accessed=10**8, transcendentals=10**6
        ),
    )(payload, mix, w_in, w_out)


class Spots:
    def __init__(self, axis):
        me, rep, core, y, high = place()
        self.paired = axis == "shard"
        if self.paired:
            self.bits = (high, y, core)
            device = lambda slot: (slot, rep)
        else:
            self.bits = (rep // 4, lax.rem(rep, 4), None)
            device = lambda slot: (me, slot)
        self.targets = {
            "up": device(self.slot(0, 1)),
            "down": device(self.slot(0, 3)),
            "across": device(self.slot(1, 0)),
        }
        if self.paired:
            self.targets["mate"] = device(self.slot(0, 0, True))

    def slot(self, side, rise, swapped=False):
        high, ring, core = self.bits
        chip = lax.rem(high + side, 2) * 4 + lax.rem(ring + rise, 4)
        if not self.paired:
            return chip
        return 2 * chip + (1 - core if swapped else core)

    def of_step(self, step, swapped=False):
        return self.slot(select(SIDE_OF_STEP, step), select(UP_OF_STEP, step), swapped)


def neighbours():
    return list(Spots("shard").targets.values())


class Gather:
    def __init__(self, slots, split, sems, axis="shard", own=None):
        spots = Spots(axis)
        self.spots, self.slots, self.sems, self.own = spots, slots, sems, own
        rows = slots.shape[1]
        whole, top, low = pl.ds(0, rows), pl.ds(0, split), pl.ds(split, rows - split)
        me, other, far = spots.slot(0, 0), spots.slot(1, 0), spots.slot(0, 2)
        from_down, from_up = spots.slot(0, 3), spots.slot(0, 1)
        other_down, other_up = spots.slot(1, 3), spots.slot(1, 1)
        other_far = spots.slot(1, 2)
        self.plan = (
            (me, whole, "across"),
            (me, whole, "up"),
            (me, whole, "down"),
            (me, whole, "mate"),
            (from_down, top, "up"),
            (from_up, low, "down"),
            (other, whole, "up"),
            (other, whole, "down"),
            (from_down, whole, "mate"),
            (from_up, whole, "mate"),
            (other, whole, "mate"),
            (other_down, top, "up"),
            (other_up, low, "down"),
            (other_down, whole, "mate"),
            (other_up, whole, "mate"),
            (far, top, "mate"),
            (far, low, "mate"),
            (other_far, top, "mate"),
            (other_far, low, "mate"),
        )

    def used(self, numbers):
        return [n for n in numbers if self.plan[n][2] in self.spots.targets]

    def move(self, number):
        slot, span, target = self.plan[number]
        target_ref = self.slots.at[slot, span]
        return pltpu.make_async_remote_copy(
            src_ref=self.own if self.own is not None and number < 4 else target_ref,
            dst_ref=target_ref,
            send_sem=self.sems[0].at[number],
            recv_sem=self.sems[1].at[number],
            device_id=self.spots.targets[target],
            device_id_type=MESH,
        )

    def start(self, *numbers):
        for number in self.used(numbers):
            self.move(number).start()

    def arrive(self, *numbers):
        for number in self.used(numbers):
            self.move(number).wait_recv()

    def begin(self):
        self.start(0, 1, 2, 3)

    def first(self):
        self.arrive(1)
        self.start(4, 8)
        self.arrive(2)
        self.start(5, 9)
        self.arrive(0)
        self.start(6, 7, 10)

    def second(self):
        self.arrive(6)
        self.start(11, 13)
        self.arrive(7)
        self.start(12, 14)
        self.arrive(4)
        self.start(15)
        self.arrive(5)
        self.start(16)

    def third(self):
        self.arrive(11)
        self.start(17)
        self.arrive(12)
        self.start(18)

    def complete(self):
        self.arrive(3, 8, 9, 10, 13, 14, 15, 16, 17, 18)

    def finish(self):
        for number in self.used(range(19)):
            self.move(number).wait_send()


def rows_of(lengths_ref, shape):
    row = lax.broadcasted_iota(jnp.int32, shape, 0)
    first = lengths_ref[0, 0]
    total = first + lengths_ref[0, 1]
    start = jnp.where(row < first, 0, jnp.where(row < total, first, total))
    return row, start, row < total


def turn(value, cosine, sine):
    width = value.shape[1]
    lane = lax.rem(lax.broadcasted_iota(jnp.int32, value.shape, 1), HEAD_SIZE)
    beside = jnp.where(
        lane < HEAD_SIZE // 2,
        pltpu.roll(value, width - HEAD_SIZE // 2, 1),
        pltpu.roll(value, HEAD_SIZE // 2, 1),
    )
    return value * cosine + beside * sine


def norm_scale(value):
    return lax.rsqrt(jnp.mean(value * value, axis=1, keepdims=True) + EPS)


def unit(size):
    return (
        lax.broadcasted_iota(jnp.int32, (size, size), 0)
        == lax.broadcasted_iota(jnp.int32, (size, size), 1)
    ).astype(jnp.bfloat16)


def flat(ref, lanes):
    value = ref[:, :, lanes]
    return value.reshape(value.shape[0] * value.shape[1], value.shape[2])


class Loads:
    def __init__(self, sems):
        self.sems, self.copies = sems, []

    def add(self, source, target):
        copy = pltpu.make_async_copy(source, target, self.sems.at[len(self.copies)])
        copy.start()
        self.copies.append(copy)
        return copy

    def wait(self, *numbers):
        for number in numbers:
            self.copies[number].wait()


def front_kernel(
    tokens_any, lengths_ref, routes_any, gain_one_any, gain_two_any,
    query_any, key_any, value_any, output_any, router_any,
    payload_out, hidden_out, normed_out, qkv_out, mixed_out, prob_out, gates_out,
    cosine_out, sine_out, all_qkv_out, all_out_out,
    tokens_ref, routes_ref, gain_one_ref, gain_two_ref, router_ref,
    payload_ref, hidden_ref, normed_ref, qkv_ref, mixed_ref, prob_ref, gates_ref,
    cosine_ref, sine_ref, all_qkv, all_out,
    load_sem, store_sem, q_send, q_recv, o_send, o_recv,
):
    me = lax.axis_index("shard")
    rows, width = tokens_ref.shape
    f32, bf16 = jnp.float32, jnp.bfloat16
    half = KEY_VALUE_HEADS * HEAD_SIZE
    loads, stores = Loads(load_sem), Loads(store_sem)
    loads.add(query_any, all_qkv.at[me, :, pl.ds(0, width)])
    loads.add(key_any, all_qkv.at[me, :, pl.ds(width, half)])
    loads.add(value_any, all_qkv.at[me, :, pl.ds(width + half, half)])
    loads.add(output_any, all_out.at[me, :, pl.ds(0, width)])
    loads.add(router_any, router_ref)
    loads.add(tokens_any, tokens_ref)
    loads.add(routes_any, routes_ref)
    loads.add(gain_one_any, gain_one_ref)
    loads.add(gain_two_any, gain_two_ref)
    greet(neighbours())
    one = Gather(all_qkv, 32, (q_send, q_recv))
    two = Gather(all_out, 32, (o_send, o_recv))
    loads.wait(0, 1, 2)
    one.begin()
    loads.wait(4)
    pad = jnp.zeros((128 - E, router_ref.shape[1]), bf16)
    all_out[me, :, pl.ds(width, 128)] = contract(
        jnp.concatenate([router_ref[...], pad], axis=0), unit(128), 0, 0
    ).astype(bf16)
    all_out[me, :, pl.ds(width + 128, 128)] = jnp.zeros((router_ref.shape[1], 128), bf16)
    loads.wait(3)
    two.begin()
    loads.wait(5, 6, 7, 8)

    inputs = tokens_ref[...].astype(f32)
    normed_ref[...] = (inputs * norm_scale(inputs) * gain_one_ref[...].astype(f32).reshape(1, width)).astype(bf16)
    row, start, _ = rows_of(lengths_ref, (rows, 128))
    lane = lax.broadcasted_iota(jnp.int32, (rows, 128), 1)
    frequency = jnp.exp(
        lax.rem(lane, HEAD_SIZE // 2).astype(f32) * (-2.0 * math.log(ROPE_BASE) / HEAD_SIZE)
    )
    angle = (row - start).astype(f32) * frequency
    cosine_ref[...] = jnp.cos(angle)
    sine = jnp.sin(angle)
    sine_ref[...] = jnp.where(lax.rem(lane, HEAD_SIZE) < HEAD_SIZE // 2, -sine, sine)
    square = (rows, rows)
    across_row = lax.broadcasted_iota(jnp.int32, square, 0)
    across_col = lax.broadcasted_iota(jnp.int32, square, 1)
    earlier = (across_row > across_col).astype(bf16)
    expert = lax.broadcasted_iota(jnp.int32, (128, rows), 0)
    named = expert < 0
    for k in range(routes_ref.shape[0]):
        named = named | (routes_ref[k : k + 1, :] == expert)
    token = lax.broadcasted_iota(jnp.int32, (128, rows), 1)
    used = named & (token < lengths_ref[0, 0] + lengths_ref[0, 1])
    rank = contract(used.astype(bf16), earlier, 1, 1)
    place_of = jnp.where(used, rank, -1.0)
    eye = unit(rows)
    named = contract(eye, named.astype(bf16), 1, 1) > 0.5
    one.first()
    two.first()
    one.second()
    two.second()
    one.third()
    one.complete()
    stores.add(all_qkv, all_qkv_out)

    normed = normed_ref[...]
    cosine, signed = cosine_ref[...], sine_ref[...]
    for tile in range(4):
        lanes = pl.ds(tile * 512, 512)
        part = contract(normed, flat(all_qkv, lanes), 1, 0)
        if tile < 3:
            part = turn(part, jnp.tile(cosine, (1, 4)), jnp.tile(signed, (1, 4)))
        qkv_ref[:, lanes] = part.astype(bf16)
    two.third()
    _, start_row, _ = rows_of(lengths_ref, square)
    allowed = (across_col >= start_row) & (across_col <= across_row)
    both = jnp.concatenate([allowed, allowed], axis=0)
    for g in range(KEY_VALUE_HEADS):
        key = qkv_ref[:, pl.ds(width + g * HEAD_SIZE, HEAD_SIZE)]
        value = qkv_ref[:, pl.ds(width + half + g * HEAD_SIZE, HEAD_SIZE)]
        query = jnp.concatenate(
            [qkv_ref[:, pl.ds((2 * g + p) * HEAD_SIZE, HEAD_SIZE)] for p in range(2)], axis=0
        )
        scores = jnp.where(both, contract(query, key, 1, 1) * HEAD_SIZE**-0.5, NEGATIVE)
        raised = jnp.exp(scores - jnp.max(scores, axis=1, keepdims=True))
        prob = raised / jnp.sum(raised, axis=1, keepdims=True)
        prob_ref[g] = prob
        mixed = contract(prob.astype(bf16), value, 1, 0).astype(bf16)
        for p in range(2):
            mixed_ref[:, pl.ds((2 * g + p) * HEAD_SIZE, HEAD_SIZE)] = mixed[
                p * rows : (p + 1) * rows
            ]
    two.complete()
    for source, target in (
        (all_out, all_out_out), (normed_ref, normed_out), (qkv_ref, qkv_out),
        (mixed_ref, mixed_out), (prob_ref, prob_out), (cosine_ref, cosine_out),
        (sine_ref, sine_out),
    ):
        stores.add(source, target)
    _, _, live = rows_of(lengths_ref, (rows, 1))
    hidden = inputs + live.astype(f32) * contract(
        mixed_ref[...], flat(all_out, pl.ds(0, width)), 1, 0
    )
    hidden_ref[...] = hidden
    stores.add(hidden_ref, hidden_out)
    normed_two = (hidden * norm_scale(hidden) * gain_two_ref[...].astype(f32).reshape(1, width)).astype(bf16)
    payload_ref[pl.ds(0, rows), :] = normed_two
    logits = contract(normed_two, flat(all_out, pl.ds(width, 128)), 1, 0)
    logits = jnp.where(named, logits, NEGATIVE)
    raised = jnp.exp(logits - jnp.max(logits, axis=1, keepdims=True))
    gates = raised / jnp.sum(raised, axis=1, keepdims=True)
    gates_ref[...] = gates
    upper = gates.astype(bf16)
    lower = (gates - upper.astype(f32)).astype(bf16)
    tail = pl.ds(rows, E)
    payload_ref[tail, :] = jnp.zeros((E, width), bf16)
    for spot, table in enumerate((upper, lower)):
        payload_ref[tail, pl.ds(spot * 256, rows)] = contract(table, eye, 0, 0)[:E].astype(bf16)
    payload_ref[tail, pl.ds(512, rows)] = place_of[:E].astype(bf16)
    stores.add(gates_ref, gates_out)
    stores.add(payload_ref, payload_out)
    stores.wait(*range(11))
    one.finish()
    two.finish()


def front_layer(
    tokens, lengths, routes, gain_one, gain_two, query, key, value, output, router, collective_id
):
    rows, width = tokens.shape
    share = query.shape[0]
    f32, bf16 = jnp.float32, jnp.bfloat16
    dma = pltpu.SemaphoreType.DMA
    shape = jax.ShapeDtypeStruct
    kept = (
        shape((rows + E, width), bf16),
        shape((rows, width), f32),
        shape((rows, width), bf16),
        shape((rows, 2 * width), bf16),
        shape((rows, width), bf16),
        shape((KEY_VALUE_HEADS, 2 * rows, rows), f32),
        shape((rows, 128), f32),
        shape((rows, 128), f32),
        shape((rows, 128), f32),
        shape((16, share, 2 * width), bf16),
        shape((16, share, width + 256), bf16),
    )
    anywhere = pl.BlockSpec(memory_space=pl.ANY)
    inputs = (
        tokens, lengths, routes.T, gain_one, gain_two, query, key, value, output, router.T,
    )
    taken = [inputs[place] for place in (0, 2, 3, 4, 9)]
    return pl.pallas_call(
        front_kernel,
        out_shape=kept,
        in_specs=[anywhere, pl.BlockSpec(memory_space=pltpu.SMEM)] + [anywhere] * 8,
        out_specs=(anywhere,) * 11,
        scratch_shapes=[pltpu.VMEM(value.shape, value.dtype) for value in (*taken, *kept)]
        + [dma((9,)), dma((11,)), dma((19,)), dma((19,)), dma((19,)), dma((19,))],
        compiler_params=pltpu.CompilerParams(
            collective_id=collective_id, has_side_effects=True, vmem_limit_bytes=48 * 1024 * 1024
        ),
        cost_estimate=pl.CostEstimate(
            flops=24 * 10**9, bytes_accessed=10**8, transcendentals=10**6
        ),
    )(*inputs)


def chip_of(step):
    _, _, _, y, high = place()
    side, rise = select(SIDE_OF_STEP, step), select(UP_OF_STEP, step)
    return lax.rem(high + side, 2) * 4 + lax.rem(y + rise, 4)


class Scatter:
    def __init__(self, source, sums, bufs, sems, split, local_sem=None, axis="shard"):
        self.source, self.sums, self.bufs, self.sems = source, sums, bufs, sems
        self.count, self.split, self.local_sem = bufs[5].shape[0], split, local_sem
        self.spots = Spots(axis)
        self.pending = {}

    def block(self, step):
        if self.sums is None:
            return self.source.at[self.spots.of_step(step)]
        return self.sums.at[step]

    def load(self, step):
        return pltpu.make_async_copy(
            self.source.at[self.spots.of_step(step)], self.sums.at[step], self.local_sem.at[step]
        )

    def swap(self, step):
        return pltpu.make_async_remote_copy(
            src_ref=self.source.at[self.spots.of_step(step, True)],
            dst_ref=self.bufs[0].at[step],
            send_sem=self.sems[0].at[step],
            recv_sem=self.sems[1].at[step],
            device_id=self.spots.targets["mate"],
            device_id_type=MESH,
        )

    def begin(self):
        for step in (7, 4, 6, 5, 2, 1, 3, 0):
            if self.spots.paired:
                self.swap(jnp.int32(step)).start()
            if self.sums is not None:
                self.load(jnp.int32(step)).start()

    def settle(self, step):
        step = jnp.int32(step)
        if self.sums is not None:
            self.load(step).wait()
        if self.spots.paired:
            self.swap(step).wait_recv()
            add_rows(self.block(step), self.bufs[0].at[step], 0, self.count)

    def send(self, number, source, target_ref, target):
        copy = pltpu.make_async_remote_copy(
            src_ref=source,
            dst_ref=target_ref,
            send_sem=self.sems[0].at[number],
            recv_sem=self.sems[1].at[number],
            device_id=self.spots.targets[target],
            device_id_type=MESH,
        )
        copy.start()
        self.pending[number] = copy

    def first(self, o):
        step = (7, 4)[o]
        self.settle(step)
        block = self.block(jnp.int32(step))
        spans = pl.ds(0, self.split), pl.ds(self.split, self.count - self.split)
        self.send(8 + o, block.at[spans[0]], self.bufs[3].at[o], "up")
        self.send(10 + o, block.at[spans[1]], self.bufs[4].at[o], "down")

    def second(self, o):
        above, below = (6, 2)[o], (5, 1)[o]
        self.settle(above)
        self.settle(below)
        above, below = self.block(jnp.int32(above)), self.block(jnp.int32(below))
        self.pending[8 + o].wait_recv()
        add_rows(above, self.bufs[3].at[o], 0, self.split)
        self.send(12 + o, above, self.bufs[1].at[o], "up")
        self.pending[10 + o].wait_recv()
        add_rows(below, self.bufs[4].at[o], self.split, self.count - self.split)
        self.send(14 + o, below, self.bufs[2].at[o], "down")

    def third(self, o):
        step = (3, 0)[o]
        self.settle(step)
        block = self.block(jnp.int32(step))
        self.pending[12 + o].wait_recv()
        add_rows(block, self.bufs[1].at[o], 0, self.count)
        self.pending[14 + o].wait_recv()
        add_rows(block, self.bufs[2].at[o], 0, self.count)
        if o == 0:
            self.send(16, block, self.bufs[5], "across")

    def last(self, emit):
        self.pending[16].wait_recv()
        own, beside = self.block(jnp.int32(0)), self.bufs[5]

        def body(step, carry):
            span = pl.ds(pl.multiple_of(step * 16, 16), 16)
            emit(span, own[span, :].astype(jnp.float32) + beside[span, :].astype(jnp.float32))
            return carry

        lax.fori_loop(0, self.count // 16, body, 0)

    def finish(self):
        for step in range(8 if self.spots.paired else 0):
            self.swap(jnp.int32(step)).wait_send()
        for copy in self.pending.values():
            copy.wait_send()


def scatter_scratch(count, width, split, swapped=8):
    kind = jnp.bfloat16
    return [
        pltpu.VMEM((swapped, count, width), kind),
        pltpu.VMEM((2, count, width), kind),
        pltpu.VMEM((2, count, width), kind),
        pltpu.VMEM((2, split, width), kind),
        pltpu.VMEM((2, count - split, width), kind),
        pltpu.VMEM((count, width), kind),
        pltpu.SemaphoreType.DMA((17,)),
        pltpu.SemaphoreType.DMA((17,)),
    ]


class Total:
    def __init__(self, source, out, pieces, sems, piece):
        self.source, self.out, self.pieces = source, out, pieces
        self.sems, self.piece = sems, piece
        self.shard, self.me = lax.axis_index("shard"), lax.axis_index("replica")

    def copy(self, way, step):
        target = lax.rem(self.me + step, 8)
        if way == 0:
            source, place_of = self.piece(self.source, target), self.pieces.at[step - 1]
        else:
            source = place_of = self.piece(self.out, self.me)
        return pltpu.make_async_remote_copy(
            src_ref=source,
            dst_ref=place_of,
            send_sem=self.sems[2 * way].at[step - 1],
            recv_sem=self.sems[2 * way + 1].at[step - 1],
            device_id=(self.shard, target),
            device_id_type=MESH,
        )

    def begin(self):
        for step in range(1, 8):
            self.copy(0, step).start()

    def middle(self):
        for step in range(1, 8):
            self.copy(0, step).wait_recv()
        own = self.piece(self.source, self.me)
        result = self.piece(self.out, self.me)

        def body(turn_of, carry):
            span = pl.ds(pl.multiple_of(turn_of * 16, 16), 16)
            total = own[span, :].astype(jnp.float32)
            for step in range(7):
                total = total + self.pieces[step, span, :].astype(jnp.float32)
            result[span, :] = total.astype(jnp.bfloat16)
            return carry

        lax.fori_loop(0, self.pieces.shape[1] // 16, body, 0)
        for step in range(1, 8):
            self.copy(1, step).start()

    def end(self):
        for step in range(1, 8):
            self.copy(1, step).wait_recv()

    def finish(self):
        for step in range(1, 8):
            self.copy(0, step).wait_send()
            self.copy(1, step).wait_send()


def total_scratch(rows, width):
    dma = pltpu.SemaphoreType.DMA
    return [pltpu.VMEM((7, rows, width), jnp.bfloat16), dma((7,)), dma((7,)), dma((7,)), dma((7,))]


def quarter(ref, which):
    half = ref.shape[1] // 2
    return ref.at[
        pl.ds(pl.multiple_of((which // 2) * 16, 16), 16),
        pl.ds(pl.multiple_of(lax.rem(which, 2) * half, 128), half),
    ]


def norm_back(value, scale, gain, grad):
    gained = grad * gain
    return scale * gained - value * scale**3 * jnp.mean(gained * value, axis=1, keepdims=True)


def rear_kernel(
    lengths_ref, tokens_any, cotangent_any, gain_one_any, gain_two_any, payload_any, hidden_any,
    normed_any, qkv_any, mixed_any, prob_any, gates_any, cosine_any, sine_any, all_qkv_any,
    all_out_any, back_any, mixes_ref, grads_ref,
    output_ref, d_tokens_ref, d_gain_one_ref, d_gain_two_ref, d_query_ref, d_key_ref,
    d_value_ref, d_output_ref, d_router_ref, d_expert_ref,
    tokens_ref, cotangent_ref, gain_one_ref, gain_two_ref, payload_ref, hidden_ref,
    normed_ref, qkv_ref, mixed_ref, prob_ref, gates_ref, cosine_ref, sine_ref, all_qkv,
    all_out, back_ref,
    *scratch,
):
    scratch = list(scratch)

    def take(count):
        taken = scratch[:count]
        del scratch[:count]
        return taken

    load_sem, own_sem = take(2)
    mix_sums, mix_local = take(2)
    mix_bufs, mix_sems = take(6), take(2)
    (one_blocks,) = take(1)
    one_bufs, one_sems = take(6), take(2)
    (two_blocks,) = take(1)
    two_bufs, two_sems = take(6), take(2)
    expert_sums, expert_local = take(2)
    expert_bufs, expert_sems = take(6), take(2)
    expert_own, spread_send, spread_recv = take(3)
    (one_pieces,), one_total_sems = take(1), take(4)
    (two_pieces,), two_total_sems = take(1), take(4)
    one_part, two_part, one_total, two_total = take(4)
    mixed_grad_ref, turned_ref, qkv_grad_ref, first_grad_ref, hidden_grad_ref = take(5)
    f32, bf16 = jnp.float32, jnp.bfloat16
    rows, width = tokens_ref.shape
    half = KEY_VALUE_HEADS * HEAD_SIZE
    shard, me = lax.axis_index("shard"), lax.axis_index("replica")
    loads = Loads(load_sem)
    early = (
        (back_any, back_ref), (hidden_any, hidden_ref), (gates_any, gates_ref),
        (cotangent_any, cotangent_ref), (gain_two_any, gain_two_ref), (all_out_any, all_out),
        (mixed_any, mixed_ref), (payload_any, payload_ref),
    )
    late = (
        (qkv_any, qkv_ref), (prob_any, prob_ref), (cosine_any, cosine_ref), (sine_any, sine_ref),
        (all_qkv_any, all_qkv), (normed_any, normed_ref), (tokens_any, tokens_ref),
        (gain_one_any, gain_one_ref),
    )
    for source, target in early + late:
        loads.add(source, target)
    greet(neighbours() + [(shard, lax.rem(me + step, 8)) for step in range(1, 8)])
    mixes = Scatter(mixes_ref, mix_sums, mix_bufs, mix_sems, 96, mix_local)
    one = Scatter(one_blocks, None, one_bufs, one_sems, 32)
    two = Scatter(two_blocks, None, two_bufs, two_sems, 32)
    experts = Scatter(
        grads_ref, expert_sums, expert_bufs, expert_sems, 96, expert_local, "replica"
    )
    spread = Gather(d_expert_ref, 96, (spread_send, spread_recv), "replica", expert_own)
    one_sum = Total(one_part, one_total, one_pieces, one_total_sems, quarter)
    two_sum = Total(two_part, two_total, two_pieces, two_total_sems, quarter)
    mixes.begin()
    experts.begin()
    experts.first(0)
    experts.first(1)
    loads.wait(*range(len(early)))

    _, _, live = rows_of(lengths_ref, (rows, 1))
    live = live.astype(f32)
    eye = unit(rows)
    line = back_ref[pl.ds(rows, E), :]
    gap = jnp.zeros((128 - E, rows), bf16)

    def columns(part):
        return contract(eye, jnp.concatenate([part.astype(bf16), gap], axis=0), 1, 1)

    gate_grad = columns(line[:, :rows]) + columns(line[:, 256 : 256 + rows])
    gates = gates_ref[...]
    logit_grad = (gates * (gate_grad - jnp.sum(gates * gate_grad, axis=1, keepdims=True))).astype(
        bf16
    )
    second_grad = back_ref[pl.ds(0, rows), :] + contract(
        logit_grad, flat(all_out, pl.ds(width, 128)), 1, 1
    )
    hidden = hidden_ref[...]
    scale_two = norm_scale(hidden)
    d_gain_two = jnp.sum(second_grad * hidden * scale_two, axis=0, keepdims=True)
    hidden_grad = cotangent_ref[...].astype(f32) + norm_back(
        hidden, scale_two, gain_two_ref[...].astype(f32).reshape(1, width), second_grad
    )
    hidden_grad_ref[...] = hidden_grad
    attn_grad = (live * hidden_grad).astype(bf16)

    def weights_of(ref, tile, lanes):
        value = ref[4 * tile : 4 * tile + 4, :, :lanes]
        return value.reshape(256, lanes)

    for tile in range(4):
        span = pl.ds(tile * 256, 256)
        mixed_grad_ref[:, span] = contract(
            attn_grad, weights_of(all_out, tile, width), 1, 1
        ).astype(bf16)
        one_blocks[4 * tile : 4 * tile + 4, :, :width] = (
            contract(mixed_ref[:, span], attn_grad, 0, 0).astype(bf16).reshape(4, 64, width)
        )
        one_blocks[4 * tile : 4 * tile + 4, :, width : width + 128] = (
            contract(payload_ref[pl.ds(0, rows), span], logit_grad, 0, 0)
            .astype(bf16)
            .reshape(4, 64, 128)
        )
    one_blocks[:, :, width + 128 :] = jnp.zeros((16, 64, 128), bf16)
    one.begin()
    mixes.first(0)
    mixes.first(1)

    def heads(ref, g):
        return jnp.concatenate(
            [ref[:, pl.ds((2 * g + p) * HEAD_SIZE, HEAD_SIZE)] for p in range(2)], axis=0
        )

    def head_back(g):
        mixed_grad, query = heads(mixed_grad_ref, g), heads(qkv_ref, g)
        key = qkv_ref[:, pl.ds(width + g * HEAD_SIZE, HEAD_SIZE)]
        value = qkv_ref[:, pl.ds(width + half + g * HEAD_SIZE, HEAD_SIZE)]
        prob = prob_ref[g]
        prob_grad = contract(mixed_grad, value, 1, 1)
        qkv_grad_ref[:, pl.ds(width + half + g * HEAD_SIZE, HEAD_SIZE)] = contract(
            prob.astype(bf16), mixed_grad, 0, 0
        ).astype(bf16)
        score_grad = prob * (prob_grad - jnp.sum(prob * prob_grad, axis=1, keepdims=True))
        score_grad = score_grad.astype(bf16)
        query_grad = contract(score_grad, key, 1, 0) * HEAD_SIZE**-0.5
        for p in range(2):
            turned_ref[:, pl.ds((2 * g + p) * HEAD_SIZE, HEAD_SIZE)] = query_grad[
                p * rows : (p + 1) * rows
            ]
        turned_ref[:, pl.ds(width + g * HEAD_SIZE, HEAD_SIZE)] = (
            contract(score_grad, query, 0, 0) * HEAD_SIZE**-0.5
        )

    loads.wait(*range(len(early), len(early + late)))
    for g in range(2):
        head_back(g)
    experts.second(0)
    for g in range(2, 4):
        head_back(g)
    mixes.second(0)
    for g in range(4, 6):
        head_back(g)
    experts.second(1)
    mixes.second(1)
    one.first(0)
    one.first(1)
    for g in range(6, 8):
        head_back(g)
    cosine, signed = cosine_ref[...], -sine_ref[...]
    for tile in range(3):
        lanes = pl.ds(tile * 512, 512)
        qkv_grad_ref[:, lanes] = turn(
            turned_ref[:, lanes], jnp.tile(cosine, (1, 4)), jnp.tile(signed, (1, 4))
        ).astype(bf16)
    mixes.third(0)
    qkv_grad = qkv_grad_ref[...]
    for tile in range(4):
        span = pl.ds(tile * 256, 256)
        first_grad_ref[:, span] = contract(qkv_grad, weights_of(all_qkv, tile, 2 * width), 1, 1)
        two_blocks[4 * tile : 4 * tile + 4, :, : 2 * width] = (
            contract(normed_ref[:, span], qkv_grad, 0, 0).astype(bf16).reshape(4, 64, 2 * width)
        )
    inputs = tokens_ref[...].astype(f32)
    scale_one = norm_scale(inputs)
    first_grad = first_grad_ref[...]
    d_gain_one = jnp.sum(first_grad * inputs * scale_one, axis=0, keepdims=True)
    two_blocks[:, :, 2 * width :] = jnp.zeros((16, 64, 256), bf16)
    pieces = [
        gain[:, 128 * part : 128 * part + 128]
        for gain in (d_gain_one, d_gain_two)
        for part in range(8)
    ]
    gain_tile = jnp.concatenate(pieces, axis=0).astype(bf16)
    for block in range(16):
        two_blocks[block, pl.ds(0, 16), pl.ds(2 * width, 128)] = gain_tile
    two.begin()
    experts.third(0)
    one.second(0)
    mixes.third(1)
    one.second(1)
    two.first(0)
    two.first(1)
    experts.third(1)
    d_tokens_ref[...] = hidden_grad_ref[...] + norm_back(
        inputs, scale_one, gain_one_ref[...].astype(f32).reshape(1, width), first_grad
    )

    def give_output(span, value):
        row = lax.broadcasted_iota(jnp.int32, (16, 1), 0) + span.start
        alive = (row < lengths_ref[0, 0] + lengths_ref[0, 1]).astype(f32)
        output_ref[span, :] = (hidden_ref[span, :] + alive * value).astype(bf16)

    def give(ref):
        def emit(span, value):
            ref[span, :] = value.astype(bf16)

        return emit

    experts.last(give(expert_own))
    own_store = pltpu.make_async_copy(expert_own, d_expert_ref.at[me], own_sem)
    own_store.start()
    spread.begin()
    mixes.last(give_output)

    one.third(0)
    two.second(0)
    one.third(1)
    two.second(1)
    spread.first()
    one.last(give(one_part))
    one_sum.begin()
    two.third(0)
    two.third(1)
    spread.second()
    one_sum.middle()
    two.last(give(two_part))
    two_sum.begin()
    one_sum.end()
    d_output_ref[...] = one_total[:, pl.ds(0, width)].astype(f32)
    d_router_ref[...] = one_total[:, pl.ds(width, 128)].astype(f32)
    two_sum.middle()
    spread.third()
    two_sum.end()
    d_query_ref[...] = two_total[:, pl.ds(0, width)].astype(f32)
    d_key_ref[...] = two_total[:, pl.ds(width, half)].astype(f32)
    d_value_ref[...] = two_total[:, pl.ds(width + half, half)].astype(f32)
    gains = two_total[pl.ds(0, 16), pl.ds(2 * width, 128)].astype(f32)
    d_gain_one_ref[...] = gains[:8]
    d_gain_two_ref[...] = gains[8:]
    spread.complete()
    own_store.wait()
    for user in (mixes, one, two, experts, spread, one_sum, two_sum):
        user.finish()


def rear_layer(
    tokens, lengths, cotangent, gain_one, gain_two, kept, back, mixes, grads, collective_id
):
    rows, width = tokens.shape
    half = KEY_VALUE_HEADS * HEAD_SIZE
    f32, bf16 = jnp.float32, jnp.bfloat16
    vmem = pl.BlockSpec(memory_space=pltpu.VMEM)
    anywhere = pl.BlockSpec(memory_space=pl.ANY)
    dma = pltpu.SemaphoreType.DMA
    shape = jax.ShapeDtypeStruct
    wide_one, wide_two = width + 256, 2 * width + 256
    slab = grads.shape[0] // 8
    inputs = (tokens, cotangent, gain_one, gain_two, *kept, back)
    return pl.pallas_call(
        rear_kernel,
        out_shape=(
            shape((rows, width), bf16),
            shape((rows, width), f32),
            shape((8, 128), f32),
            shape((8, 128), f32),
            shape((64, width), f32),
            shape((64, half), f32),
            shape((64, half), f32),
            shape((64, width), f32),
            shape((64, 128), f32),
            shape((8, slab, width), bf16),
        ),
        in_specs=[pl.BlockSpec(memory_space=pltpu.SMEM)] + [anywhere] * (len(inputs) + 2),
        out_specs=(vmem,) * 9 + (anywhere,),
        scratch_shapes=[
            *(pltpu.VMEM(value.shape, value.dtype) for value in inputs),
            dma((len(inputs),)),
            dma,
            pltpu.VMEM((8, rows, width), bf16),
            dma((8,)),
            *scatter_scratch(rows, width, 96),
            pltpu.VMEM((16, 64, wide_one), bf16),
            *scatter_scratch(64, wide_one, 32),
            pltpu.VMEM((16, 64, wide_two), bf16),
            *scatter_scratch(64, wide_two, 32),
            pltpu.VMEM((8, slab, width), bf16),
            dma((8,)),
            *scatter_scratch(slab, width, 96, 1),
            pltpu.VMEM((slab, width), bf16),
            dma((19,)),
            dma((19,)),
            *total_scratch(16, wide_one // 2),
            *total_scratch(16, wide_two // 2),
            pltpu.VMEM((64, wide_one), bf16),
            pltpu.VMEM((64, wide_two), bf16),
            pltpu.VMEM((64, wide_one), bf16),
            pltpu.VMEM((64, wide_two), bf16),
            pltpu.VMEM((rows, width), bf16),
            pltpu.VMEM((rows, width + half), f32),
            pltpu.VMEM((rows, 2 * width), bf16),
            pltpu.VMEM((rows, width), f32),
            pltpu.VMEM((rows, width), f32),
        ],
        compiler_params=pltpu.CompilerParams(
            collective_id=collective_id, has_side_effects=True, vmem_limit_bytes=60 * 1024 * 1024
        ),
        cost_estimate=pl.CostEstimate(
            flops=24 * 10**9, bytes_accessed=10**8, transcendentals=10**6
        ),
    )(lengths, *inputs, mixes, grads.reshape(8, slab, width))


def local(
    tokens,
    seq_lengths,
    routes,
    attn_gain,
    ffn_gain,
    w_query,
    key_projection,
    value_projection,
    w_output,
    w_router,
    w_in,
    w_out,
    cotangent,
):
    rows, width = tokens.shape
    all_cotangent = lax.all_gather(cotangent, "shard", axis=0)
    payload, *kept = front_layer(
        tokens, seq_lengths, routes, attn_gain, ffn_gain,
        w_query, key_projection, value_projection, w_output, w_router, 1,
    )
    back, mixes, expert_grads = expert_layer(payload, all_cotangent, w_in[0], w_out[0], 2)
    (
        output, d_tokens, d_attn_gain, d_ffn_gain, d_query, d_key, d_value, d_output, d_router,
        expert_grads,
    ) = rear_layer(
        tokens, seq_lengths, cotangent, attn_gain, ffn_gain,
        (payload, *kept), back, mixes, expert_grads, 3,
    )
    expert_grads = expert_grads.reshape(-1, width)
    return (
        output,
        d_tokens,
        d_attn_gain.reshape(width),
        d_ffn_gain.reshape(width),
        d_query,
        d_key,
        d_value,
        d_output,
        d_router[:, :E],
        expert_grads[:width].astype(jnp.float32)[None],
        expert_grads[width:].astype(jnp.float32)[None],
    )


def solution(mesh):
    return jax.shard_map(
        local,
        mesh=mesh,
        in_specs=(
            P(("shard", "replica"), None),
            P(("shard", "replica"), None),
            P(("shard", "replica"), None),
            P(),
            P(),
            P("shard", None),
            P("shard", None),
            P("shard", None),
            P("shard", None),
            P("shard", None),
            P("shard", None, None),
            P("shard", None, None),
            P(("shard", "replica"), None),
        ),
        out_specs=(
            P(("shard", "replica"), None),
            P(("shard", "replica"), None),
            P(),
            P(),
            P("shard", None),
            P("shard", None),
            P("shard", None),
            P("shard", None),
            P("shard", None),
            P("shard", None, None),
            P("shard", None, None),
        ),
        check_vma=False,
    )
```

time: 343 us -> 282 us (0.82)
  matrix products: 29.6 us -> 0 us
  local copies, waits for them, and re-layouts: 41.3 us -> 20 us
  Pallas kernels: 240 us -> 230 us
  waiting for transfers between devices: 0.04 us -> 9.79 us
  other arithmetic: 14.7 us -> 5.42 us
    pallas_call x1, Pallas kernels: 111 us -> 84.1 us  [expert_layer(): pl.pallas_call(functools.partial(expert_kernel, cut), out_shape=(jax.Shap...]
    dot_general x15 -> x0, matrix products: 26.6 us -> none  [the longest x11 19.5 us: einsum(): return jnp.einsum(form, a, b, preferred_element_type=jnp.float32)]
    pallas_call x3 -> x2, Pallas kernels: 129 us -> 146 us  [the longest x1 96.5 us: rear_layer(): pl.pallas_call(rear_kernel, out_shape=(shape((rows, width), bf16), shape(...]
    concatenate x5 -> x0, local copies, waits for them, and re-layouts: 12.6 us -> none  [the longest x1 10.5 us: local(): jnp.concatenate([d_qkv, d_output, d_router.astype(bf16), jnp.tile(gains,...]
    slice x11 -> x0, local copies, waits for them, and re-layouts: 10.2 us -> none  [the longest x2 1.86 us: local(): value = qkv[:, 1536:].astype(bf16).reshape(rows, KEY_VALUE_HEADS, HEAD_SIZE)]
    all_gather x1, waiting for transfers between devices: 0.01 us -> 9.11 us  [local(): all_cotangent = lax.all_gather(cotangent, 'shard', axis=0)]
    unnamed x68 -> x65, local copies, waits for them, and re-layouts: 11 us -> 20 us
    broadcast_in_dim x0 -> x2, other arithmetic: none -> 5.42 us  [the longest x1 2.94 us: local(): expert_grads[width:].astype(jnp.float32)[None]]
  transfers between devices with their start and end apart: 2 -> 1, of which waited for: 0 -> 1; matrix products, arithmetic and copies ran while one was open for 16% -> 0% of each run, Pallas kernels for 38% -> 18%
where the time goes in v3:
time: 282 us; the launch traced here: 279 us
  Pallas kernels  230 us (82%)
  local copies, waits for them, and re-layouts  20 us (7%)
  between operations  14.2 us (5%)
  waiting for transfers between devices  9.79 us (3%)
  other arithmetic  5.42 us (2%)
    pallas_call x1, Pallas kernels, rear_layer(): pl.pallas_call(rear_kernel, out_shape=(shape((rows, width), bf16), shape(...  96.5 us
    pallas_call x1, Pallas kernels, expert_layer(): pl.pallas_call(functools.partial(expert_kernel, cut), out_shape=(jax.Shap...  84.1 us
    pallas_call x1, Pallas kernels, front_layer(): pl.pallas_call(front_kernel, out_shape=kept, in_specs=[anywhere, pl.Block...  49.5 us
    unnamed x65, local copies, waits for them, and re-layouts  20 us
    all_gather x1, waiting for transfers between devices, local(): all_cotangent = lax.all_gather(cotangent, 'shard', axis=0)  9.11 us
  transfers between devices with their start and end apart: 1, of which 1 were waited for; matrix products, arithmetic and copies ran while one was open for 0% of the time, Pallas kernels for 18%

profile of v3, /device:TPU:8, one launch (start us, length us, event | category | flops | bytes accessed | tf_op | source)
XLA Modules:
  0.0 279.5 jit_solution(14278985857545235896)
XLA Ops:
  7.2 0.0 all-gather.3.cloned.1.call-start
  7.2 0.7 all-gather.3.cloned.1.call-update
  7.9 0.0 copy-start
  7.9 1.0 copy-done
  8.9 0.0 copy-start.1
  8.9 0.9 copy-done.1
  9.8 0.0 copy-start.2
  9.8 0.9 copy-done.2
  10.7 0.0 copy-start.3
  10.7 0.8 copy-done.3
  11.6 0.0 copy-start.4
  11.6 0.8 copy-done.4
  12.4 0.0 copy-start.5
  12.4 0.7 copy-done.5
  13.1 0.0 copy-start.6
  13.1 0.7 copy-done.6
  13.8 0.0 copy-start.7
  13.8 0.7 copy-done.7
  14.5 0.0 copy-start.8
  14.5 0.7 copy-done.8
  15.2 0.0 copy-start.9
  15.2 0.7 copy-done.9
  15.8 49.5 %shard_map.212 = (bf16[208,1024]{1,0:T(8,128)(2,1)S(1)}, f32[192,1024]{1,0:T(8,128)S(1)}, bf16[192,1024]{1,0:T(8,128)(2,1)S(1)}, bf16[192,2048]{1,0:T(8,128)(2,1...) custom-call(bf16[192,1024]{1,0:T(8,128)(2,1)S(1)} %copy-done, ...), custom_call_target="tpu_custom_call" | custom-call | flops 24000000000 | bytes 100000000 | tf_op jit(solution)/shard_map/pallas_call | solution.py:750
  65.3 0.0 copy-start.10
  65.3 0.9 copy-done.10
  66.2 0.0 copy-start.11
  66.2 0.9 copy-done.11
  67.0 0.0 copy-start.12
  67.0 0.8 copy-done.12
  67.8 0.0 copy-start.13
  67.8 0.7 copy-done.13
  68.5 0.8 copy-done.14
  69.3 0.6 copy-done.15
  69.9 0.6 copy-done.16
  70.6 0.6 copy-done.17
  71.2 9.1 %all-gather.3.cloned.1.call-done = bf16[3072,1024]{1,0:T(8,128)(2,1)} async-done(((bf16[192,1024]{1,0:T(8,128)(2,1)}), bf16[3072,1024]{1,0:T(8,128)(2,1)}) %all-gather.3.cloned.1.call-update) | async-done | bytes 6291472 | tf_op jit(solution)/shard_map/all_gather | solution.py:1283
  80.3 84.1 %shard_map.213 = (f32[208,1024]{1,0:T(8,128)}, bf16[16,192,1024]{2,1,0:T(8,128)(2,1)}, bf16[1536,1024]{1,0:T(8,128)(2,1)}) custom-call(bf16[208,1024]{1,0:T(8,128)(2,1)} %copy-done.12, bf16[16,192,1024]{2,1,0:T(8,128)(2,1)} %bitcast.27, bf16[1024,1024]{1,0:T(8,128)(2,1)} %bitcast.28, bf16[512,1024]{1,0:T(8,128)(2,1)} %bitcast.29), custom_call_target="tpu_custom_call" | custom-call | flops 24000000000 | bytes 100000000 | tf_op jit(solution)/shard_map/pallas_call | solution.py:371
  164.4 96.5 %shard_map.214 = (bf16[192,1024]{1,0:T(8,128)(2,1)}, f32[192,1024]{1,0:T(8,128)}, f32[8,128]{1,0:T(8,128)}, f32[8,128]{1,0:T(8,128)}, f32[64,1024]{1,0:T(8,128)}...) custom-call(s32[1,2]{1,0:T(1,128)} %lengths_ref.3, ...), custom_call_target="tpu_custom_call" | custom-call | flops 24000000000 | bytes 100000000 | tf_op jit(solution)/shard_map/pallas_call | solution.py:1213
  260.9 0.0 copy-start.18
  261.0 2.9 %fusion.1 = f32[1,512,1024]{2,1,0:T(8,128)} fusion(bf16[1536,1024]{1,0:T(8,128)(2,1)} %bitcast.22), kind=kLoop, calls=%fused_computation.3 | loop fusion | flops 524288 | bytes 3145728 | tf_op jit(solution)/shard_map/broadcast_in_dim | solution.py:1308
  263.9 0.0 copy-done.18
  263.9 0.0 copy-start.27
  263.9 0.0 copy-start.26
  263.9 0.0 copy-start.22
  263.9 0.0 copy-start.24
  263.9 2.5 fusion
  266.4 0.0 copy-done.25
  266.4 0.7 copy.24
  267.1 0.0 copy-done.20
  267.1 0.7 copy.33
  267.8 0.0 copy-done.19
  267.9 0.9 copy.34
  268.7 0.0 copy-done.27
  268.7 0.6 copy.35
  269.3 0.0 copy-done.26
  269.3 0.6 copy.36
  269.9 0.0 copy-done.22
  269.9 0.7 copy.37
  270.6 0.0 copy-done.24
  270.6 0.7 copy.38
  271.3 0.0 copy-done.23
  271.3 0.7 copy.39
  271.9 0.0 copy-done.21
  271.9 0.7 copy.40
  (9 shorter events, 0.0 us)
Async XLA Ops:
  7.2 73.2 %all-gather.3.cloned.1.call-start = ((), (), s32[]{:S(2)}) async-start(), calls=%async_computation | async-start | bytes 6684672 | tf_op jit(solution)/shard_map/all_gather | solution.py:1283
  7.9 1.0 copy-start
  8.9 0.9 copy-start.1
  9.8 0.9 copy-start.2
  10.7 0.8 copy-start.3
  11.6 0.8 copy-start.4
  12.4 0.7 copy-start.5
  13.1 0.7 copy-start.6
  13.8 0.7 copy-start.7
  14.5 0.7 copy-start.8
  15.2 0.7 copy-start.9
  65.3 0.9 copy-start.10
  66.2 0.9 copy-start.11
  67.0 0.8 copy-start.12
  67.8 0.7 copy-start.13
  68.5 0.8 copy-start.14
  69.3 0.6 copy-start.15
  69.9 0.6 copy-start.16
  70.6 0.6 copy-start.17
  260.9 3.0 %copy-start.18 = (bf16[8,192,1024]{2,1,0:T(8,128)(2,1)S(1)}, bf16[8,192,1024]{2,1,0:T(8,128)(2,1)}, u32[]{:S(2)}) copy-start(bf16[8,192,1024]{2,1,0:T(8,128)(2,1)} %get-tuple-element.58) | copy-start | bytes 9437188
  263.9 2.5 copy-start.25
  263.9 3.2 %copy-start.20 = (bf16[192,1024]{1,0:T(8,128)(2,1)S(1)}, bf16[192,1024]{1,0:T(8,128)(2,1)}, u32[]{:S(2)}) copy-start(bf16[192,1024]{1,0:T(8,128)(2,1)} %get-tuple-element.81) | copy-start | bytes 1179652
  263.9 4.0 %copy-start.19 = (f32[192,1024]{1,0:T(8,128)S(1)}, f32[192,1024]{1,0:T(8,128)}, u32[]{:S(2)}) copy-start(f32[192,1024]{1,0:T(8,128)} %get-tuple-element.82) | copy-start | bytes 2359300
  263.9 4.8 %copy-start.27 = (f32[8,128]{1,0:T(8,128)S(1)}, f32[8,128]{1,0:T(8,128)}, u32[]{:S(2)}) copy-start(f32[8,128]{1,0:T(8,128)} %get-tuple-element.51) | copy-start | bytes 12292
  263.9 5.4 %copy-start.26 = (f32[8,128]{1,0:T(8,128)S(1)}, f32[8,128]{1,0:T(8,128)}, u32[]{:S(2)}) copy-start(f32[8,128]{1,0:T(8,128)} %get-tuple-element.52) | copy-start | bytes 12292
  263.9 6.0 %copy-start.22 = (f32[64,1024]{1,0:T(8,128)S(1)}, f32[64,1024]{1,0:T(8,128)}, u32[]{:S(2)}) copy-start(f32[64,1024]{1,0:T(8,128)} %get-tuple-element.85) | copy-start | bytes 786436
  263.9 6.7 %copy-start.24 = (f32[64,512]{1,0:T(8,128)S(1)}, f32[64,512]{1,0:T(8,128)}, u32[]{:S(2)}) copy-start(f32[64,512]{1,0:T(8,128)} %get-tuple-element.86) | copy-start | bytes 393220
  266.4 4.9 %copy-start.23 = (f32[64,512]{1,0:T(8,128)S(1)}, f32[64,512]{1,0:T(8,128)}, u32[]{:S(2)}) copy-start(f32[64,512]{1,0:T(8,128)} %get-tuple-element.87) | copy-start | bytes 393220
  266.4 5.5 %copy-start.21 = (f32[64,1024]{1,0:T(8,128)S(1)}, f32[64,1024]{1,0:T(8,128)}, u32[]{:S(2)}) copy-start(f32[64,1024]{1,0:T(8,128)} %get-tuple-element.88) | copy-start | bytes 786436
Sparse Core Ops, SparseCore 0:
  10.5 69.7 all-gather.2

commit v4 on v3

--- a/solution.py
+++ b/solution.py
@@ -81,15 +81,10 @@
     near_mate, near_up, near_down, far_up, far_down, cross,
     a_send, a_recv, local_sem, mix_sem, store_sem, send_sem, recv_sem,
 ):
-    me, rep, core, y, high = place()
+    me = lax.axis_index("shard")
     width = payload_ref.shape[1]
     rows = payload_ref.shape[0]
     tokens = rows - 16
-    mate = (index_of(high, y, 1 - core), rep)
-    up = (index_of(high, y + 1, core), rep)
-    down = (index_of(high, y + 3, core), rep)
-    across = (index_of(1 - high, y, core), rep)
-
     load_in = pltpu.make_async_copy(w_in_ref, w_in, local_sem.at[0])
     load_out = pltpu.make_async_copy(w_out_ref, w_out, local_sem.at[1])
     load_own = pltpu.make_async_copy(payload_ref, arrived.at[me], local_sem.at[2])
@@ -104,51 +99,9 @@
         )
 
     load_mix(0).start()
-    greet([mate, up, down, across])
-    whole, top, low = pl.ds(0, rows), pl.ds(0, cut), pl.ds(cut, rows - cut)
-    other = index_of(1 - high, y, core)
-    from_down = index_of(high, y + 3, core)
-    from_up = index_of(high, y + 1, core)
-    far = index_of(high, y + 2, core)
-    other_down = index_of(1 - high, y + 3, core)
-    other_up = index_of(1 - high, y + 1, core)
-    other_far = index_of(1 - high, y + 2, core)
-    plan = {
-        0: (me, whole, across),
-        1: (me, whole, up),
-        2: (me, whole, down),
-        3: (me, whole, mate),
-        4: (from_down, top, up),
-        5: (from_up, low, down),
-        6: (other, whole, up),
-        7: (other, whole, down),
-        8: (from_down, whole, mate),
-        9: (from_up, whole, mate),
-        10: (other, whole, mate),
-        11: (other_down, top, up),
-        12: (other_up, low, down),
-        13: (other_down, whole, mate),
-        14: (other_up, whole, mate),
-        15: (far, top, mate),
-        16: (far, low, mate),
-        17: (other_far, top, mate),
-        18: (other_far, low, mate),
-    }
-
-    def move(number):
-        slot, span, target = plan[number]
-        source = payload_ref if number < 4 else arrived.at[slot, span]
-        return pltpu.make_async_remote_copy(
-            src_ref=source,
-            dst_ref=arrived.at[slot, span],
-            send_sem=send_sem.at[number],
-            recv_sem=recv_sem.at[number],
-            device_id=target,
-            device_id_type=MESH,
-        )
-
-    for number in range(4):
-        move(number).start()
+    greet(neighbours())
+    gather = Gather(arrived, cut, 96, (send_sem, recv_sem), own=payload_ref)
+    gather.begin()
     load_in.wait()
     load_out.wait()
     load_own.wait()
@@ -170,60 +123,38 @@
     def work(step, carry):
         @pl.when(step == 0)
         def _():
-            move(3).wait_recv()
+            gather.arrive(3)
 
         @pl.when(step == 1)
         def _():
-            move(1).wait_recv()
-            move(4).start()
-            move(8).start()
-            move(2).wait_recv()
-            move(5).start()
-            move(9).start()
-            move(0).wait_recv()
-            for number in (6, 7, 10):
-                move(number).start()
-            move(8).wait_recv()
+            gather.first()
+            gather.arrive(8)
 
         @pl.when(step == 2)
         def _():
-            move(9).wait_recv()
+            gather.arrive(9)
 
         @pl.when(step == 3)
         def _():
-            move(10).wait_recv()
+            gather.arrive(10)
 
         @pl.when(step == 4)
         def _():
-            move(6).wait_recv()
-            move(11).start()
-            move(13).start()
-            move(7).wait_recv()
-            move(12).start()
-            move(14).start()
-            move(4).wait_recv()
-            move(15).start()
-            move(5).wait_recv()
-            move(16).start()
-            move(15).wait_recv()
-            move(16).wait_recv()
+            gather.second()
+            gather.arrive(15, 16)
 
         @pl.when(step == 5)
         def _():
-            move(13).wait_recv()
+            gather.arrive(13)
 
         @pl.when(step == 6)
         def _():
-            move(14).wait_recv()
+            gather.arrive(14)
 
         @pl.when(step == 7)
         def _():
-            move(11).wait_recv()
-            move(17).start()
-            move(12).wait_recv()
-            move(18).start()
-            move(17).wait_recv()
-            move(18).wait_recv()
+            gather.third()
+            gather.arrive(17, 18)
 
         @pl.when(step < 7)
         def _():
@@ -302,8 +233,7 @@
         return carry
 
     lax.fori_loop(0, 8, work, 0)
-    for number in range(19):
-        move(number).wait_send()
+    gather.finish()
 
     a.first(0)
     a.first(1)
@@ -403,11 +333,11 @@
             dma((3,)),
             dma((2,)),
             dma((8,)),
-            dma((19,)),
-            dma((19,)),
+            dma((22,)),
+            dma((22,)),
         ],
         compiler_params=pltpu.CompilerParams(
-            collective_id=collective_id, has_side_effects=True, vmem_limit_bytes=60 * 1024 * 1024
+            collective_id=collective_id, has_side_effects=True, vmem_limit_bytes=62 * 1024 * 1024
         ),
         cost_estimate=pl.CostEstimate(
             flops=24 * 10**9, bytes_accessed=10**8, transcendentals=10**6
@@ -449,11 +379,15 @@
 
 
 class Gather:
-    def __init__(self, slots, split, sems, axis="shard", own=None):
+    def __init__(self, slots, split, crossed, sems, axis="shard", own=None):
         spots = Spots(axis)
         self.spots, self.slots, self.sems, self.own = spots, slots, sems, own
         rows = slots.shape[1]
         whole, top, low = pl.ds(0, rows), pl.ds(0, split), pl.ds(split, rows - split)
+        half = (rows - crossed + 16) // 32 * 16 + crossed
+        cross, late = pl.ds(0, crossed), pl.ds(crossed, rows - crossed)
+        late_top, late_low = pl.ds(crossed, half - crossed), pl.ds(half, rows - half)
+        self.crossed = crossed
         me, other, far = spots.slot(0, 0), spots.slot(1, 0), spots.slot(0, 2)
         from_down, from_up = spots.slot(0, 3), spots.slot(0, 1)
         other_down, other_up = spots.slot(1, 3), spots.slot(1, 1)
@@ -465,23 +399,27 @@
             (me, whole, "mate"),
             (from_down, top, "up"),
             (from_up, low, "down"),
-            (other, whole, "up"),
-            (other, whole, "down"),
+            (other, late, "up"),
+            (other, late, "down"),
             (from_down, whole, "mate"),
             (from_up, whole, "mate"),
             (other, whole, "mate"),
-            (other_down, top, "up"),
-            (other_up, low, "down"),
+            (other_down, late_top, "up"),
+            (other_up, late_low, "down"),
             (other_down, whole, "mate"),
             (other_up, whole, "mate"),
             (far, top, "mate"),
             (far, low, "mate"),
-            (other_far, top, "mate"),
-            (other_far, low, "mate"),
+            (other_far, pl.ds(0, half), "mate"),
+            (other_far, late_low, "mate"),
+            (from_down, cross, "across"),
+            (from_up, cross, "across"),
+            (far, cross, "across"),
         )
 
     def used(self, numbers):
-        return [n for n in numbers if self.plan[n][2] in self.spots.targets]
+        skipped = () if self.crossed else (19, 20, 21)
+        return [n for n in numbers if n not in skipped and self.plan[n][2] in self.spots.targets]
 
     def move(self, number):
         slot, span, target = self.plan[number]
@@ -508,24 +446,28 @@
 
     def first(self):
         self.arrive(1)
-        self.start(4, 8)
+        self.start(4, 19, 8)
         self.arrive(2)
-        self.start(5, 9)
+        self.start(5, 20, 9)
         self.arrive(0)
         self.start(6, 7, 10)
 
     def second(self):
-        self.arrive(6)
-        self.start(11, 13)
-        self.arrive(7)
-        self.start(12, 14)
         self.arrive(4)
-        self.start(15)
+        self.start(21, 15)
         self.arrive(5)
         self.start(16)
+        self.arrive(6)
+        self.start(11)
+        self.arrive(7)
+        self.start(12)
+        self.arrive(19)
+        self.start(13)
+        self.arrive(20)
+        self.start(14)
 
     def third(self):
-        self.arrive(11)
+        self.arrive(11, 21)
         self.start(17)
         self.arrive(12)
         self.start(18)
@@ -534,7 +476,7 @@
         self.arrive(3, 8, 9, 10, 13, 14, 15, 16, 17, 18)
 
     def finish(self):
-        for number in self.used(range(19)):
+        for number in self.used(range(22)):
             self.move(number).wait_send()
 
 
@@ -590,13 +532,13 @@
 
 def front_kernel(
     tokens_any, lengths_ref, routes_any, gain_one_any, gain_two_any,
-    query_any, key_any, value_any, output_any, router_any,
+    query_any, key_any, value_any, output_any, router_any, cotangent_any,
     payload_out, hidden_out, normed_out, qkv_out, mixed_out, prob_out, gates_out,
-    cosine_out, sine_out, all_qkv_out, all_out_out,
-    tokens_ref, routes_ref, gain_one_ref, gain_two_ref, router_ref,
+    cosine_out, sine_out, all_qkv_out, all_out_out, all_cotangent,
+    tokens_ref, routes_ref, gain_one_ref, gain_two_ref, router_ref, cotangent_ref,
     payload_ref, hidden_ref, normed_ref, qkv_ref, mixed_ref, prob_ref, gates_ref,
     cosine_ref, sine_ref, all_qkv, all_out,
-    load_sem, store_sem, q_send, q_recv, o_send, o_recv,
+    load_sem, store_sem, q_send, q_recv, o_send, o_recv, c_send, c_recv,
 ):
     me = lax.axis_index("shard")
     rows, width = tokens_ref.shape
@@ -612,9 +554,11 @@
     loads.add(routes_any, routes_ref)
     loads.add(gain_one_any, gain_one_ref)
     loads.add(gain_two_any, gain_two_ref)
+    loads.add(cotangent_any, cotangent_ref)
     greet(neighbours())
-    one = Gather(all_qkv, 32, (q_send, q_recv))
-    two = Gather(all_out, 32, (o_send, o_recv))
+    one = Gather(all_qkv, 32, 32, (q_send, q_recv))
+    two = Gather(all_out, 32, 32, (o_send, o_recv))
+    three = Gather(all_cotangent, 96, 96, (c_send, c_recv), own=cotangent_ref)
     loads.wait(0, 1, 2)
     one.begin()
     loads.wait(4)
@@ -625,7 +569,8 @@
     all_out[me, :, pl.ds(width + 128, 128)] = jnp.zeros((router_ref.shape[1], 128), bf16)
     loads.wait(3)
     two.begin()
-    loads.wait(5, 6, 7, 8)
+    loads.wait(5, 6, 7, 8, 9)
+    stores.add(cotangent_ref, all_cotangent.at[me])
 
     inputs = tokens_ref[...].astype(f32)
     normed_ref[...] = (inputs * norm_scale(inputs) * gain_one_ref[...].astype(f32).reshape(1, width)).astype(bf16)
@@ -654,6 +599,7 @@
     named = contract(eye, named.astype(bf16), 1, 1) > 0.5
     one.first()
     two.first()
+    three.begin()
     one.second()
     two.second()
     one.third()
@@ -669,10 +615,13 @@
             part = turn(part, jnp.tile(cosine, (1, 4)), jnp.tile(signed, (1, 4)))
         qkv_ref[:, lanes] = part.astype(bf16)
     two.third()
+    three.first()
     _, start_row, _ = rows_of(lengths_ref, square)
     allowed = (across_col >= start_row) & (across_col <= across_row)
     both = jnp.concatenate([allowed, allowed], axis=0)
     for g in range(KEY_VALUE_HEADS):
+        if g == 4:
+            three.second()
         key = qkv_ref[:, pl.ds(width + g * HEAD_SIZE, HEAD_SIZE)]
         value = qkv_ref[:, pl.ds(width + half + g * HEAD_SIZE, HEAD_SIZE)]
         query = jnp.concatenate(
@@ -688,6 +637,7 @@
                 p * rows : (p + 1) * rows
             ]
     two.complete()
+    three.third()
     for source, target in (
         (all_out, all_out_out), (normed_ref, normed_out), (qkv_ref, qkv_out),
         (mixed_ref, mixed_out), (prob_ref, prob_out), (cosine_ref, cosine_out),
@@ -716,13 +666,16 @@
     payload_ref[tail, pl.ds(512, rows)] = place_of[:E].astype(bf16)
     stores.add(gates_ref, gates_out)
     stores.add(payload_ref, payload_out)
-    stores.wait(*range(11))
+    stores.wait(*range(12))
+    three.complete()
     one.finish()
     two.finish()
+    three.finish()
 
 
 def front_layer(
-    tokens, lengths, routes, gain_one, gain_two, query, key, value, output, router, collective_id
+    tokens, lengths, routes, gain_one, gain_two, query, key, value, output, router, cotangent,
+    collective_id,
 ):
     rows, width = tokens.shape
     share = query.shape[0]
@@ -745,17 +698,18 @@
     anywhere = pl.BlockSpec(memory_space=pl.ANY)
     inputs = (
         tokens, lengths, routes.T, gain_one, gain_two, query, key, value, output, router.T,
-    )
-    taken = [inputs[place] for place in (0, 2, 3, 4, 9)]
+        cotangent,
+    )
+    taken = [inputs[place] for place in (0, 2, 3, 4, 9, 10)]
     return pl.pallas_call(
         front_kernel,
-        out_shape=kept,
-        in_specs=[anywhere, pl.BlockSpec(memory_space=pltpu.SMEM)] + [anywhere] * 8,
-        out_specs=(anywhere,) * 11,
+        out_shape=(*kept, shape((16, rows, width), bf16)),
+        in_specs=[anywhere, pl.BlockSpec(memory_space=pltpu.SMEM)] + [anywhere] * 9,
+        out_specs=(anywhere,) * 12,
         scratch_shapes=[pltpu.VMEM(value.shape, value.dtype) for value in (*taken, *kept)]
-        + [dma((9,)), dma((11,)), dma((19,)), dma((19,)), dma((19,)), dma((19,))],
+        + [dma((10,)), dma((12,))] + [dma((22,))] * 6,
         compiler_params=pltpu.CompilerParams(
-            collective_id=collective_id, has_side_effects=True, vmem_limit_bytes=48 * 1024 * 1024
+            collective_id=collective_id, has_side_effects=True, vmem_limit_bytes=62 * 1024 * 1024
         ),
         cost_estimate=pl.CostEstimate(
             flops=24 * 10**9, bytes_accessed=10**8, transcendentals=10**6
@@ -961,8 +915,7 @@
     lengths_ref, tokens_any, cotangent_any, gain_one_any, gain_two_any, payload_any, hidden_any,
     normed_any, qkv_any, mixed_any, prob_any, gates_any, cosine_any, sine_any, all_qkv_any,
     all_out_any, back_any, mixes_ref, grads_ref,
-    output_ref, d_tokens_ref, d_gain_one_ref, d_gain_two_ref, d_query_ref, d_key_ref,
-    d_value_ref, d_output_ref, d_router_ref, d_expert_ref,
+    output_ref, d_tokens_ref, one_total, two_total, d_expert_ref,
     tokens_ref, cotangent_ref, gain_one_ref, gain_two_ref, payload_ref, hidden_ref,
     normed_ref, qkv_ref, mixed_ref, prob_ref, gates_ref, cosine_ref, sine_ref, all_qkv,
     all_out, back_ref,
@@ -987,7 +940,7 @@
     expert_own, spread_send, spread_recv = take(3)
     (one_pieces,), one_total_sems = take(1), take(4)
     (two_pieces,), two_total_sems = take(1), take(4)
-    one_part, two_part, one_total, two_total = take(4)
+    one_part, two_part = take(2)
     mixed_grad_ref, turned_ref, qkv_grad_ref, first_grad_ref, hidden_grad_ref = take(5)
     f32, bf16 = jnp.float32, jnp.bfloat16
     rows, width = tokens_ref.shape
@@ -1013,7 +966,7 @@
     experts = Scatter(
         grads_ref, expert_sums, expert_bufs, expert_sems, 96, expert_local, "replica"
     )
-    spread = Gather(d_expert_ref, 96, (spread_send, spread_recv), "replica", expert_own)
+    spread = Gather(d_expert_ref, 96, 0, (spread_send, spread_recv), "replica", expert_own)
     one_sum = Total(one_part, one_total, one_pieces, one_total_sems, quarter)
     two_sum = Total(two_part, two_total, two_pieces, two_total_sems, quarter)
     mixes.begin()
@@ -1180,17 +1133,9 @@
     two.last(give(two_part))
     two_sum.begin()
     one_sum.end()
-    d_output_ref[...] = one_total[:, pl.ds(0, width)].astype(f32)
-    d_router_ref[...] = one_total[:, pl.ds(width, 128)].astype(f32)
     two_sum.middle()
     spread.third()
     two_sum.end()
-    d_query_ref[...] = two_total[:, pl.ds(0, width)].astype(f32)
-    d_key_ref[...] = two_total[:, pl.ds(width, half)].astype(f32)
-    d_value_ref[...] = two_total[:, pl.ds(width + half, half)].astype(f32)
-    gains = two_total[pl.ds(0, 16), pl.ds(2 * width, 128)].astype(f32)
-    d_gain_one_ref[...] = gains[:8]
-    d_gain_two_ref[...] = gains[8:]
     spread.complete()
     own_store.wait()
     for user in (mixes, one, two, experts, spread, one_sum, two_sum):
@@ -1201,7 +1146,6 @@
     tokens, lengths, cotangent, gain_one, gain_two, kept, back, mixes, grads, collective_id
 ):
     rows, width = tokens.shape
-    half = KEY_VALUE_HEADS * HEAD_SIZE
     f32, bf16 = jnp.float32, jnp.bfloat16
     vmem = pl.BlockSpec(memory_space=pltpu.VMEM)
     anywhere = pl.BlockSpec(memory_space=pl.ANY)
@@ -1215,17 +1159,12 @@
         out_shape=(
             shape((rows, width), bf16),
             shape((rows, width), f32),
-            shape((8, 128), f32),
-            shape((8, 128), f32),
-            shape((64, width), f32),
-            shape((64, half), f32),
-            shape((64, half), f32),
-            shape((64, width), f32),
-            shape((64, 128), f32),
+            shape((64, wide_one), bf16),
+            shape((64, wide_two), bf16),
             shape((8, slab, width), bf16),
         ),
         in_specs=[pl.BlockSpec(memory_space=pltpu.SMEM)] + [anywhere] * (len(inputs) + 2),
-        out_specs=(vmem,) * 9 + (anywhere,),
+        out_specs=(vmem,) * 4 + (anywhere,),
         scratch_shapes=[
             *(pltpu.VMEM(value.shape, value.dtype) for value in inputs),
             dma((len(inputs),)),
@@ -1241,27 +1180,117 @@
             dma((8,)),
             *scatter_scratch(slab, width, 96, 1),
             pltpu.VMEM((slab, width), bf16),
-            dma((19,)),
-            dma((19,)),
+            dma((22,)),
+            dma((22,)),
             *total_scratch(16, wide_one // 2),
             *total_scratch(16, wide_two // 2),
             pltpu.VMEM((64, wide_one), bf16),
             pltpu.VMEM((64, wide_two), bf16),
-            pltpu.VMEM((64, wide_one), bf16),
-            pltpu.VMEM((64, wide_two), bf16),
             pltpu.VMEM((rows, width), bf16),
-            pltpu.VMEM((rows, width + half), f32),
+            pltpu.VMEM((rows, width + KEY_VALUE_HEADS * HEAD_SIZE), f32),
             pltpu.VMEM((rows, 2 * width), bf16),
             pltpu.VMEM((rows, width), f32),
             pltpu.VMEM((rows, width), f32),
         ],
         compiler_params=pltpu.CompilerParams(
-            collective_id=collective_id, has_side_effects=True, vmem_limit_bytes=60 * 1024 * 1024
+            collective_id=collective_id, has_side_effects=True, vmem_limit_bytes=62 * 1024 * 1024
         ),
         cost_estimate=pl.CostEstimate(
             flops=24 * 10**9, bytes_accessed=10**8, transcendentals=10**6
         ),
     )(lengths, *inputs, mixes, grads.reshape(8, slab, width))
+
+
+def close_kernel(
+    output_any, d_tokens_any, one_any, two_any, expert_any,
+    output_out, d_tokens_out, d_gain_one_out, d_gain_two_out, d_query_out, d_key_out,
+    d_value_out, d_output_out, d_router_out, d_in_out, d_out_out,
+    output_ref, d_tokens_ref, one_ref, two_ref, expert_ref, query_ref, key_ref, value_ref,
+    matrix_ref, wide_ref,
+    router_ref, gain_one_ref, gain_two_ref, load_sem, store_sem,
+):
+    f32 = jnp.float32
+    width = query_ref.shape[1]
+    half = key_ref.shape[1]
+    loads, stores = Loads(load_sem), Loads(store_sem)
+    parts = expert_ref.shape[0] // 256
+    spans = [pl.ds(256 * part, 256) for part in range(parts)]
+    loads.add(one_any, one_ref)
+    loads.add(two_any, two_ref)
+    for span in spans:
+        loads.add(expert_any.at[span], expert_ref.at[span])
+    loads.add(output_any, output_ref)
+    loads.add(d_tokens_any, d_tokens_ref)
+    loads.wait(0, 1)
+    query_ref[...] = two_ref[:, pl.ds(0, width)].astype(f32)
+    key_ref[...] = two_ref[:, pl.ds(width, half)].astype(f32)
+    value_ref[...] = two_ref[:, pl.ds(width + half, half)].astype(f32)
+    matrix_ref[...] = one_ref[:, pl.ds(0, width)].astype(f32)
+    router_ref[...] = contract(one_ref[:, pl.ds(width, 128)], unit(64), 0, 0)[:E]
+    gains = two_ref[pl.ds(0, 16), pl.ds(2 * width, 128)].astype(f32)
+    gain_one_ref[...] = gains[:8]
+    gain_two_ref[...] = gains[8:]
+    for source, target in (
+        (query_ref, d_query_out), (key_ref, d_key_out), (value_ref, d_value_out),
+        (matrix_ref, d_output_out), (router_ref, d_router_out),
+        (gain_one_ref, d_gain_one_out), (gain_two_ref, d_gain_two_out),
+    ):
+        stores.add(source, target)
+    for part, span in enumerate(spans):
+        loads.wait(2 + part)
+        wide_ref[span, :] = expert_ref[span, :].astype(f32)
+        if part < width // 256:
+            stores.add(wide_ref.at[span], d_in_out.at[span])
+        else:
+            stores.add(wide_ref.at[span], d_out_out.at[pl.ds(256 * part - width, 256)])
+    loads.wait(2 + parts, 3 + parts)
+    stores.add(output_ref, output_out)
+    stores.add(d_tokens_ref, d_tokens_out)
+    stores.wait(*range(9 + parts))
+
+
+def close_layer(output, d_tokens, one, two, expert):
+    rows, width = output.shape
+    half = KEY_VALUE_HEADS * HEAD_SIZE
+    hidden = expert.shape[0] - width
+    f32 = jnp.float32
+    shape = jax.ShapeDtypeStruct
+    small = (
+        (64, width), (64, half), (64, half), (64, width), (E, 64), (8, 128), (8, 128),
+    )
+    dma = pltpu.SemaphoreType.DMA
+    anywhere = pl.BlockSpec(memory_space=pl.ANY)
+    query, key, value, matrix, router, gain_one, gain_two = small
+    outs = (gain_one, gain_two, query, key, value, matrix, router, (width, width), (hidden, width))
+    return pl.pallas_call(
+        close_kernel,
+        out_shape=(
+            shape(output.shape, output.dtype),
+            shape(d_tokens.shape, f32),
+            *(shape(extent, f32) for extent in outs),
+        ),
+        in_specs=[anywhere] * 5,
+        out_specs=(anywhere,) * 11,
+        scratch_shapes=[
+            pltpu.VMEM(output.shape, output.dtype),
+            pltpu.VMEM(d_tokens.shape, f32),
+            pltpu.VMEM(one.shape, one.dtype),
+            pltpu.VMEM(two.shape, two.dtype),
+            pltpu.VMEM(expert.shape, expert.dtype),
+            pltpu.VMEM(query, f32),
+            pltpu.VMEM(key, f32),
+            pltpu.VMEM(value, f32),
+            pltpu.VMEM(matrix, f32),
+            pltpu.VMEM(expert.shape, f32),
+            pltpu.VMEM(router, f32),
+            pltpu.VMEM(gain_one, f32),
+            pltpu.VMEM(gain_two, f32),
+            dma((4 + expert.shape[0] // 256,)),
+            dma((9 + expert.shape[0] // 256,)),
+        ],
+        compiler_params=pltpu.CompilerParams(vmem_limit_bytes=62 * 1024 * 1024),
+        cost_estimate=pl.CostEstimate(flops=0, bytes_accessed=12 * 10**6, transcendentals=0),
+    )(output, d_tokens, one, two, expert)
 
 
 def local(
@@ -1280,20 +1309,19 @@
     cotangent,
 ):
     rows, width = tokens.shape
-    all_cotangent = lax.all_gather(cotangent, "shard", axis=0)
-    payload, *kept = front_layer(
+    payload, *kept, all_cotangent = front_layer(
         tokens, seq_lengths, routes, attn_gain, ffn_gain,
-        w_query, key_projection, value_projection, w_output, w_router, 1,
+        w_query, key_projection, value_projection, w_output, w_router, cotangent, 1,
     )
     back, mixes, expert_grads = expert_layer(payload, all_cotangent, w_in[0], w_out[0], 2)
+    output, d_tokens, one, two, expert_grads = rear_layer(
+        tokens, seq_lengths, cotangent, attn_gain, ffn_gain, (payload, *kept), back, mixes,
+        expert_grads, 3,
+    )
     (
         output, d_tokens, d_attn_gain, d_ffn_gain, d_query, d_key, d_value, d_output, d_router,
-        expert_grads,
-    ) = rear_layer(
-        tokens, seq_lengths, cotangent, attn_gain, ffn_gain,
-        (payload, *kept), back, mixes, expert_grads, 3,
-    )
-    expert_grads = expert_grads.reshape(-1, width)
+        d_in, d_out,
+    ) = close_layer(output, d_tokens, one, two, expert_grads.reshape(-1, width))
     return (
         output,
         d_tokens,
@@ -1303,9 +1331,9 @@
         d_key,
         d_value,
         d_output,
-        d_router[:, :E],
-        expert_grads[:width].astype(jnp.float32)[None],
-        expert_grads[width:].astype(jnp.float32)[None],
+        d_router.T,
+        d_in[None],
+        d_out[None],
     )
 
 

time: 282 us -> 242 us (0.86)
  local copies, waits for them, and re-layouts: 20 us -> 0 us
  between operations: 14.2 us -> 0.85 us
  Pallas kernels: 230 us -> 241 us
  waiting for transfers between devices: 9.79 us -> 0 us
  other arithmetic: 5.42 us -> 0 us
    unnamed x65 -> x0, local copies, waits for them, and re-layouts: 20 us -> none
    pallas_call x1 -> x2, Pallas kernels: 49.5 us -> 63 us  [the longest x1 58.3 us: front_layer(): pl.pallas_call(front_kernel, out_shape=(*kept, shape((16, rows, width), b...]
    all_gather x1 -> x0, waiting for transfers between devices: 9.11 us -> none  [local(): all_cotangent = lax.all_gather(cotangent, 'shard', axis=0)]
    broadcast_in_dim x2 -> x0, other arithmetic: 5.42 us -> none  [the longest x1 2.94 us: local(): expert_grads[width:].astype(jnp.float32)[None]]
  transfers between devices with their start and end apart: 1 -> 0, of which waited for: 1 -> 0; matrix products, arithmetic and copies ran while one was open for 0% -> 0% of each run, Pallas kernels for 18% -> 0%
where the time goes in v4:
time: 242 us
  Pallas kernels  241 us (100%)
    pallas_call x1, Pallas kernels, rear_layer(): pl.pallas_call(rear_kernel, out_shape=(shape((rows, width), bf16), shape(...  95.5 us
    pallas_call x1, Pallas kernels, expert_layer(): pl.pallas_call(functools.partial(expert_kernel, cut), out_shape=(jax.Shap...  82.3 us
    pallas_call x1, Pallas kernels, front_layer(): pl.pallas_call(front_kernel, out_shape=(*kept, shape((16, rows, width), b...  58.3 us

profile of v4, /device:TPU:8, one launch (start us, length us, event | category | flops | bytes accessed | tf_op | source)
XLA Modules:
  0.0 241.6 jit_solution(10652206151444509727)
XLA Ops:
  0.6 58.3 %shard_map.212 = (bf16[208,1024]{1,0:T(8,128)(2,1)}, f32[192,1024]{1,0:T(8,128)}, bf16[192,1024]{1,0:T(8,128)(2,1)}, bf16[192,2048]{1,0:T(8,128)(2,1)}, bf16[192...) custom-call(bf16[192,1024]{1,0:T(8,128)(2,1)} %tokens_any.3, ...), custom_call_target="tpu_custom_call" | custom-call | flops 24000000000 | bytes 100000000 | tf_op jit(solution)/shard_map/pallas_call | solution.py:704
  59.0 82.3 %shard_map.213 = (f32[208,1024]{1,0:T(8,128)}, bf16[16,192,1024]{2,1,0:T(8,128)(2,1)}, bf16[1536,1024]{1,0:T(8,128)(2,1)}) custom-call(bf16[208,1024]{1,0:T(8,128)(2,1)} %get-tuple-element.42.payload_ref.payload_any, bf16[16,192,1024]{2,1,0:T(8,128)(2,1)} %get-tuple-element.53.mix_ref, bf16[1024,1024]{1,0:T(8,128)(2,1)} %bitcast.13, bf16[512,1024]{1,0:T(8,128)(2,1)} %bitcast.15), custom_call_target="tpu_custom_call" | custom-call | flops 24000000000 | bytes 100000000 | tf_op jit(solution)/shard_map/pallas_call | solution.py:301
  141.3 95.5 %shard_map.214 = (bf16[192,1024]{1,0:T(8,128)(2,1)}, f32[192,1024]{1,0:T(8,128)}, bf16[64,1280]{1,0:T(8,128)(2,1)}, bf16[64,2304]{1,0:T(8,128)(2,1)}, bf16[8,192,1024]{2,1,0:T(8,128)(2,1)}) custom-call(s32[1,2]{1,0:T(1,128)} %lengths_ref.3, bf16[192,1024]{1,0:T(8,128)(2,1)} %tokens_any.3, bf16[192,1024]{1,0:T(8,128)(2,1)} %cotangent_any.3, ...), custom_call_target="tpu_custom_call" | custom-call | flops 24000000000 | bytes 100000000 | tf_op jit(solution)/shard_map/pallas_call | solution.py:1157
  236.8 4.6 %shard_map.215 = (bf16[192,1024]{1,0:T(8,128)(2,1)}, f32[192,1024]{1,0:T(8,128)}, f32[8,128]{1,0:T(8,128)}, f32[8,128]{1,0:T(8,128)}, f32[64,1024]{1,0:T(8,128)}...) custom-call(bf16[192,1024]{1,0:T(8,128)(2,1)} %get-tuple-element.57., ...), custom_call_target="tpu_custom_call" | custom-call | bytes 12000000 | tf_op jit(solution)/shard_map/pallas_call | solution.py:1265

commit v5 on v4

--- a/solution.py
+++ b/solution.py
@@ -76,10 +76,11 @@
 
 
 def expert_kernel(
-    cut, payload_ref, mix_ref, w_in_ref, w_out_ref, back_ref, mixture_ref, grads_ref,
+    cut, payload_ref, mix_ref, w_in_ref, w_out_ref, back_ref, mixture_ref, grads_in_ref, grads_out_ref,
     arrived, mix_buf, w_in, w_out, blocks, weighted, rows_c, act_c, route_c, pre_c, mix_c, row_c,
-    near_mate, near_up, near_down, far_up, far_down, cross,
-    a_send, a_recv, local_sem, mix_sem, store_sem, send_sem, recv_sem,
+    near_mate, near_up, near_down, far_up, far_down, cross, crossing,
+    a_send, a_recv, sums_in, in_up, in_down, in_far_up, in_far_down, in_send, in_recv,
+    half_sem, local_sem, mix_sem, store_sem, send_sem, recv_sem,
 ):
     me = lax.axis_index("shard")
     width = payload_ref.shape[1]
@@ -99,7 +100,8 @@
         )
 
     load_mix(0).start()
-    greet(neighbours())
+    ring = Spots("replica").targets
+    greet(neighbours() + [ring["up"], ring["down"]])
     gather = Gather(arrived, cut, 96, (send_sem, recv_sem), own=payload_ref)
     gather.begin()
     load_in.wait()
@@ -116,8 +118,8 @@
         return pick, gates
 
     a = Scatter(
-        blocks, None, (near_mate, near_up, near_down, far_up, far_down, cross), (a_send, a_recv),
-        cut,
+        blocks, None, (near_mate, near_up, near_down, far_up, far_down, cross, crossing), (a_send, a_recv),
+        cut, 96,
     )
 
     def work(step, carry):
@@ -235,6 +237,10 @@
     lax.fori_loop(0, 8, work, 0)
     gather.finish()
 
+    matrix = Scatter(
+        sums_in, None, (None, in_up, in_down, in_far_up, in_far_down, None, None),
+        (in_send, in_recv), sums_in.shape[1] // 2, 0, None, "replica",
+    )
     a.first(0)
     a.first(1)
 
@@ -259,28 +265,48 @@
 
     def grad_in(tile, carry):
         span = pl.ds(pl.multiple_of(tile * 256, 256), 256)
-        grads_ref[span, :] = contract(rows_c[:, span], pre_c[...], 0, 0).astype(jnp.bfloat16)
+        slab = sums_in.shape[1]
+        sums_in[pl.ds(tile * (256 // slab), 256 // slab)] = (
+            contract(rows_c[:, span], pre_c[...], 0, 0)
+            .astype(jnp.bfloat16)
+            .reshape(256 // slab, slab, width)
+        )
         return carry
 
     def grad_out(tile, carry):
         span = pl.ds(pl.multiple_of(tile * 256, 256), 256)
-        there = pl.ds(pl.multiple_of(width + tile * 256, 256), 256)
-        grads_ref[there, :] = contract(act_c[:, span], route_c[...], 0, 0).astype(jnp.bfloat16)
+        grads_out_ref[span, :] = contract(act_c[:, span], route_c[...], 0, 0).astype(jnp.bfloat16)
         return carry
 
     def give_back(span, value):
         back_ref[span, :] = value
 
+    lax.fori_loop(0, 4, grad_in, 0)
+    matrix.first(0)
+    matrix.first(1)
+    a.second(0)
+    a.second(1)
     lax.fori_loop(0, 8, spread, 0)
-    a.second(0)
-    lax.fori_loop(0, 1, grad_in, 0)
-    a.second(1)
-    lax.fori_loop(1, 4, grad_in, 0)
+    matrix.second(0)
+    matrix.second(1)
+    lax.fori_loop(0, 2, grad_out, 0)
     a.third(0)
-    lax.fori_loop(0, 2, grad_out, 0)
+    matrix.third(0)
+    matrix.third(1)
+    halves = [
+        pltpu.make_async_copy(
+            matrix.block(jnp.int32(step)), grads_in_ref.at[place_of], half_sem.at[place_of]
+        )
+        for place_of, step in enumerate((0, 3))
+    ]
+    for copy in halves:
+        copy.start()
     a.third(1)
     a.last(give_back)
     a.finish()
+    matrix.finish()
+    for copy in halves:
+        copy.wait()
 
     def stored(step, carry):
         store(step).wait()
@@ -303,7 +329,8 @@
         out_shape=(
             jax.ShapeDtypeStruct((rows, width), jnp.float32),
             jax.ShapeDtypeStruct((16, tokens, width), kind),
-            jax.ShapeDtypeStruct((width + hidden, width), kind),
+            jax.ShapeDtypeStruct((2, width // 8, width), kind),
+            jax.ShapeDtypeStruct((hidden, width), kind),
         ),
         in_specs=[
             pl.BlockSpec(memory_space=pl.ANY),
@@ -313,6 +340,7 @@
         ],
         out_specs=(
             pl.BlockSpec(memory_space=pltpu.VMEM),
+            pl.BlockSpec(memory_space=pl.ANY),
             pl.BlockSpec(memory_space=pl.ANY),
             pl.BlockSpec(memory_space=pltpu.VMEM),
         ),
@@ -329,7 +357,15 @@
             pltpu.VMEM((slots, 2 * hidden), kind),
             pltpu.VMEM((2 * SLOTS, width), kind),
             pltpu.VMEM((2 * SLOTS, width), kind),
-            *scatter_scratch(rows, width, cut),
+            *scatter_scratch(rows, width, cut, 96),
+            pltpu.VMEM((8, width // 8, width), kind),
+            pltpu.VMEM((2, width // 8, width), kind),
+            pltpu.VMEM((2, width // 8, width), kind),
+            pltpu.VMEM((2, width // 16, width), kind),
+            pltpu.VMEM((2, width // 16, width), kind),
+            dma((20,)),
+            dma((20,)),
+            dma((2,)),
             dma((3,)),
             dma((2,)),
             dma((8,)),
@@ -558,7 +594,7 @@
     greet(neighbours())
     one = Gather(all_qkv, 32, 32, (q_send, q_recv))
     two = Gather(all_out, 32, 32, (o_send, o_recv))
-    three = Gather(all_cotangent, 96, 96, (c_send, c_recv), own=cotangent_ref)
+    three = Gather(all_cotangent, 96, 64, (c_send, c_recv), own=cotangent_ref)
     loads.wait(0, 1, 2)
     one.begin()
     loads.wait(4)
@@ -570,6 +606,7 @@
     loads.wait(3)
     two.begin()
     loads.wait(5, 6, 7, 8, 9)
+    three.begin()
     stores.add(cotangent_ref, all_cotangent.at[me])
 
     inputs = tokens_ref[...].astype(f32)
@@ -599,7 +636,7 @@
     named = contract(eye, named.astype(bf16), 1, 1) > 0.5
     one.first()
     two.first()
-    three.begin()
+    three.first()
     one.second()
     two.second()
     one.third()
@@ -615,13 +652,14 @@
             part = turn(part, jnp.tile(cosine, (1, 4)), jnp.tile(signed, (1, 4)))
         qkv_ref[:, lanes] = part.astype(bf16)
     two.third()
-    three.first()
     _, start_row, _ = rows_of(lengths_ref, square)
     allowed = (across_col >= start_row) & (across_col <= across_row)
     both = jnp.concatenate([allowed, allowed], axis=0)
     for g in range(KEY_VALUE_HEADS):
+        if g == 0:
+            three.second()
         if g == 4:
-            three.second()
+            three.third()
         key = qkv_ref[:, pl.ds(width + g * HEAD_SIZE, HEAD_SIZE)]
         value = qkv_ref[:, pl.ds(width + half + g * HEAD_SIZE, HEAD_SIZE)]
         query = jnp.concatenate(
@@ -637,7 +675,6 @@
                 p * rows : (p + 1) * rows
             ]
     two.complete()
-    three.third()
     for source, target in (
         (all_out, all_out_out), (normed_ref, normed_out), (qkv_ref, qkv_out),
         (mixed_ref, mixed_out), (prob_ref, prob_out), (cosine_ref, cosine_out),
@@ -724,9 +761,13 @@
 
 
 class Scatter:
-    def __init__(self, source, sums, bufs, sems, split, local_sem=None, axis="shard"):
+    def __init__(
+        self, source, sums, bufs, sems, split, crossed, local_sem=None, axis="shard"
+    ):
         self.source, self.sums, self.bufs, self.sems = source, sums, bufs, sems
-        self.count, self.split, self.local_sem = bufs[5].shape[0], split, local_sem
+        self.count, self.split, self.local_sem = bufs[1].shape[1], split, local_sem
+        self.crossed = crossed
+        self.half = (self.count - crossed + 16) // 32 * 16 + crossed
         self.spots = Spots(axis)
         self.pending = {}
 
@@ -778,34 +819,67 @@
         self.pending[number] = copy
 
     def first(self, o):
-        step = (7, 4)[o]
-        self.settle(step)
-        block = self.block(jnp.int32(step))
-        spans = pl.ds(0, self.split), pl.ds(self.split, self.count - self.split)
-        self.send(8 + o, block.at[spans[0]], self.bufs[3].at[o], "up")
-        self.send(10 + o, block.at[spans[1]], self.bufs[4].at[o], "down")
+        rows, count = self.crossed, self.count
+        if o == 0:
+            self.settle(7)
+            far = self.block(jnp.int32(7))
+            ends = (rows, self.half, count)
+        else:
+            self.settle(4)
+            far = self.block(jnp.int32(4))
+            ends = (0, self.split, count)
+            self.meet(17, far)
+        upper, lower = ends[1] - ends[0], ends[2] - ends[1]
+        self.send(8 + o, far.at[pl.ds(ends[0], upper)], self.bufs[3].at[o, pl.ds(0, upper)], "up")
+        self.send(
+            10 + o, far.at[pl.ds(ends[1], lower)], self.bufs[4].at[o, pl.ds(0, lower)], "down"
+        )
+        if o == 0:
+            for place_of, step in enumerate((7, 6, 5)):
+                if place_of > 0:
+                    self.settle(step)
+                if rows > 0:
+                    self.send(
+                        17 + place_of,
+                        self.block(jnp.int32(step)).at[pl.ds(0, rows)],
+                        self.bufs[6].at[place_of],
+                        "across",
+                    )
+
+    def meet(self, number, block):
+        if self.crossed > 0:
+            self.pending[number].wait_recv()
+            add_rows(block, self.bufs[6].at[number - 17], 0, self.crossed)
 
     def second(self, o):
         above, below = (6, 2)[o], (5, 1)[o]
-        self.settle(above)
-        self.settle(below)
+        first, middle = (self.crossed, 0)[o], (self.half, self.split)[o]
+        count = self.count - first
+        if o == 1:
+            self.settle(above)
+            self.settle(below)
         above, below = self.block(jnp.int32(above)), self.block(jnp.int32(below))
+        if o == 1:
+            self.meet(18, above)
+            self.meet(19, below)
+        part, here = pl.ds(first, count), pl.ds(0, count)
         self.pending[8 + o].wait_recv()
-        add_rows(above, self.bufs[3].at[o], 0, self.split)
-        self.send(12 + o, above, self.bufs[1].at[o], "up")
+        add_rows(above, self.bufs[3].at[o], first, middle - first)
+        self.send(12 + o, above.at[part], self.bufs[1].at[o, here], "up")
         self.pending[10 + o].wait_recv()
-        add_rows(below, self.bufs[4].at[o], self.split, self.count - self.split)
-        self.send(14 + o, below, self.bufs[2].at[o], "down")
+        add_rows(below, self.bufs[4].at[o], middle, self.count - middle)
+        self.send(14 + o, below.at[part], self.bufs[2].at[o, here], "down")
 
     def third(self, o):
         step = (3, 0)[o]
         self.settle(step)
         block = self.block(jnp.int32(step))
+        first = (self.crossed, 0)[o]
         self.pending[12 + o].wait_recv()
-        add_rows(block, self.bufs[1].at[o], 0, self.count)
+        add_rows(block, self.bufs[1].at[o], first, self.count - first)
         self.pending[14 + o].wait_recv()
-        add_rows(block, self.bufs[2].at[o], 0, self.count)
-        if o == 0:
+        add_rows(block, self.bufs[2].at[o], first, self.count - first)
+        if o == 0 and self.bufs[5] is not None:
             self.send(16, block, self.bufs[5], "across")
 
     def last(self, emit):
@@ -826,7 +900,7 @@
             copy.wait_send()
 
 
-def scatter_scratch(count, width, split, swapped=8):
+def scatter_scratch(count, width, split, crossed, swapped=8):
     kind = jnp.bfloat16
     return [
         pltpu.VMEM((swapped, count, width), kind),
@@ -835,9 +909,67 @@
         pltpu.VMEM((2, split, width), kind),
         pltpu.VMEM((2, count - split, width), kind),
         pltpu.VMEM((count, width), kind),
-        pltpu.SemaphoreType.DMA((17,)),
-        pltpu.SemaphoreType.DMA((17,)),
+        pltpu.VMEM((3, max(crossed, 16), width), kind),
+        pltpu.SemaphoreType.DMA((20,)),
+        pltpu.SemaphoreType.DMA((20,)),
     ]
+
+
+class Expert:
+    def __init__(self, source, total, loads, bufs, sems, rest):
+        (sums, local_sem), (own, own_sem, send, recv) = loads, rest
+        count = own.shape[0]
+        self.own = own
+        self.sums = Scatter(source, sums, bufs, sems, count // 2, 0, local_sem, "replica")
+        self.spread = Gather(total, count // 2, 0, (send, recv), "replica", own)
+        self.store = pltpu.make_async_copy(own, total.at[lax.axis_index("replica")], own_sem)
+
+    def turn_round(self):
+        def emit(span, value):
+            self.own[span, :] = value.astype(jnp.bfloat16)
+
+        self.sums.last(emit)
+        self.store.start()
+        self.spread.begin()
+
+    def finish(self):
+        self.store.wait()
+        self.sums.finish()
+        self.spread.finish()
+
+
+class Joined:
+    def __init__(self, source, total, loads, rest):
+        (self.cross, join_sems), (own, own_sem, send, recv) = loads, rest
+        self.own = own
+        load_sem, send_sem, recv_sem = join_sems
+        self.load = pltpu.make_async_copy(source.at[0], own, load_sem)
+        self.copy = pltpu.make_async_remote_copy(
+            src_ref=source.at[1],
+            dst_ref=self.cross,
+            send_sem=send_sem,
+            recv_sem=recv_sem,
+            device_id=Spots("replica").targets["across"],
+            device_id_type=MESH,
+        )
+        self.spread = Gather(total, own.shape[0] // 2, 0, (send, recv), "replica", own)
+        self.store = pltpu.make_async_copy(own, total.at[lax.axis_index("replica")], own_sem)
+
+    def begin(self):
+        self.load.start()
+        self.copy.start()
+
+    def turn_round(self):
+        self.load.wait()
+        self.copy.wait_recv()
+        add_rows(self.own, self.cross, 0, self.own.shape[0])
+        self.store.start()
+        self.spread.begin()
+
+    def finish(self):
+        self.copy.wait_send()
+        self.store.wait()
+        self.spread.finish()
 
 
 class Total:
@@ -898,6 +1030,19 @@
     return [pltpu.VMEM((7, rows, width), jnp.bfloat16), dma((7,)), dma((7,)), dma((7,)), dma((7,))]
 
 
+def expert_scratch(slab, width):
+    kind, dma = jnp.bfloat16, pltpu.SemaphoreType.DMA
+    return [
+        pltpu.VMEM((8, slab, width), kind),
+        dma((8,)),
+        *scatter_scratch(slab, width, slab // 2, 0, 1),
+        pltpu.VMEM((slab, width), kind),
+        dma,
+        dma((22,)),
+        dma((22,)),
+    ]
+
+
 def quarter(ref, which):
     half = ref.shape[1] // 2
     return ref.at[
@@ -914,8 +1059,8 @@
 def rear_kernel(
     lengths_ref, tokens_any, cotangent_any, gain_one_any, gain_two_any, payload_any, hidden_any,
     normed_any, qkv_any, mixed_any, prob_any, gates_any, cosine_any, sine_any, all_qkv_any,
-    all_out_any, back_any, mixes_ref, grads_ref,
-    output_ref, d_tokens_ref, one_total, two_total, d_expert_ref,
+    all_out_any, back_any, mixes_ref, grads_in_ref, grads_out_ref,
+    output_ref, d_tokens_ref, one_total, two_total, d_in_ref, d_out_ref,
     tokens_ref, cotangent_ref, gain_one_ref, gain_two_ref, payload_ref, hidden_ref,
     normed_ref, qkv_ref, mixed_ref, prob_ref, gates_ref, cosine_ref, sine_ref, all_qkv,
     all_out, back_ref,
@@ -928,16 +1073,15 @@
         del scratch[:count]
         return taken
 
-    load_sem, own_sem = take(2)
+    (load_sem,) = take(1)
     mix_sums, mix_local = take(2)
-    mix_bufs, mix_sems = take(6), take(2)
+    mix_bufs, mix_sems = take(7), take(2)
     (one_blocks,) = take(1)
-    one_bufs, one_sems = take(6), take(2)
+    one_bufs, one_sems = take(7), take(2)
     (two_blocks,) = take(1)
-    two_bufs, two_sems = take(6), take(2)
-    expert_sums, expert_local = take(2)
-    expert_bufs, expert_sems = take(6), take(2)
-    expert_own, spread_send, spread_recv = take(3)
+    two_bufs, two_sems = take(7), take(2)
+    (join_cross,), join_sems, in_rest = take(1), take(3), take(4)
+    out_parts = (take(2), take(7), take(2), take(4))
     (one_pieces,), one_total_sems = take(1), take(4)
     (two_pieces,), two_total_sems = take(1), take(4)
     one_part, two_part = take(2)
@@ -960,19 +1104,20 @@
     for source, target in early + late:
         loads.add(source, target)
     greet(neighbours() + [(shard, lax.rem(me + step, 8)) for step in range(1, 8)])
-    mixes = Scatter(mixes_ref, mix_sums, mix_bufs, mix_sems, 96, mix_local)
-    one = Scatter(one_blocks, None, one_bufs, one_sems, 32)
-    two = Scatter(two_blocks, None, two_bufs, two_sems, 32)
-    experts = Scatter(
-        grads_ref, expert_sums, expert_bufs, expert_sems, 96, expert_local, "replica"
-    )
-    spread = Gather(d_expert_ref, 96, 0, (spread_send, spread_recv), "replica", expert_own)
+    mixes = Scatter(mixes_ref, mix_sums, mix_bufs, mix_sems, 96, 0, mix_local)
+    one = Scatter(one_blocks, None, one_bufs, one_sems, 32, 0)
+    two = Scatter(two_blocks, None, two_bufs, two_sems, 32, 0)
+    matrix_in = Joined(grads_in_ref, d_in_ref, (join_cross, join_sems), in_rest)
+    matrix_out = Expert(grads_out_ref, d_out_ref, *out_parts)
     one_sum = Total(one_part, one_total, one_pieces, one_total_sems, quarter)
     two_sum = Total(two_part, two_total, two_pieces, two_total_sems, quarter)
     mixes.begin()
-    experts.begin()
-    experts.first(0)
-    experts.first(1)
+    matrix_in.begin()
+    matrix_out.sums.begin()
+    matrix_out.sums.first(0)
+    matrix_out.sums.first(1)
+    mixes.first(0)
+    mixes.first(1)
     loads.wait(*range(len(early)))
 
     _, _, live = rows_of(lengths_ref, (rows, 1))
@@ -1020,8 +1165,8 @@
         )
     one_blocks[:, :, width + 128 :] = jnp.zeros((16, 64, 128), bf16)
     one.begin()
-    mixes.first(0)
-    mixes.first(1)
+    one.first(0)
+    matrix_in.turn_round()
 
     def heads(ref, g):
         return jnp.concatenate(
@@ -1049,27 +1194,21 @@
         )
 
     loads.wait(*range(len(early), len(early + late)))
-    for g in range(2):
+    for g in range(4):
         head_back(g)
-    experts.second(0)
-    for g in range(2, 4):
+    matrix_out.sums.second(0)
+    matrix_out.sums.second(1)
+    mixes.second(0)
+    one.first(1)
+    for g in range(4, 8):
         head_back(g)
-    mixes.second(0)
-    for g in range(4, 6):
-        head_back(g)
-    experts.second(1)
-    mixes.second(1)
-    one.first(0)
-    one.first(1)
-    for g in range(6, 8):
-        head_back(g)
+    matrix_in.spread.first()
     cosine, signed = cosine_ref[...], -sine_ref[...]
     for tile in range(3):
         lanes = pl.ds(tile * 512, 512)
         qkv_grad_ref[:, lanes] = turn(
             turned_ref[:, lanes], jnp.tile(cosine, (1, 4)), jnp.tile(signed, (1, 4))
         ).astype(bf16)
-    mixes.third(0)
     qkv_grad = qkv_grad_ref[...]
     for tile in range(4):
         span = pl.ds(tile * 256, 256)
@@ -1091,13 +1230,13 @@
     for block in range(16):
         two_blocks[block, pl.ds(0, 16), pl.ds(2 * width, 128)] = gain_tile
     two.begin()
-    experts.third(0)
+    mixes.second(1)
     one.second(0)
-    mixes.third(1)
+    two.first(0)
     one.second(1)
-    two.first(0)
     two.first(1)
-    experts.third(1)
+    matrix_out.sums.third(0)
+    matrix_out.sums.third(1)
     d_tokens_ref[...] = hidden_grad_ref[...] + norm_back(
         inputs, scale_one, gain_one_ref[...].astype(f32).reshape(1, width), first_grad
     )
@@ -1113,37 +1252,35 @@
 
         return emit
 
-    experts.last(give(expert_own))
-    own_store = pltpu.make_async_copy(expert_own, d_expert_ref.at[me], own_sem)
-    own_store.start()
-    spread.begin()
-    mixes.last(give_output)
-
+    mixes.third(0)
     one.third(0)
+    matrix_in.spread.second()
+    matrix_out.turn_round()
     two.second(0)
+    two.second(1)
     one.third(1)
-    two.second(1)
-    spread.first()
+    matrix_in.spread.third()
+    matrix_out.spread.first()
     one.last(give(one_part))
     one_sum.begin()
+    mixes.third(1)
+    matrix_out.spread.second()
     two.third(0)
+    mixes.last(give_output)
+    matrix_out.spread.third()
     two.third(1)
-    spread.second()
     one_sum.middle()
     two.last(give(two_part))
     two_sum.begin()
+    two_sum.middle()
     one_sum.end()
-    two_sum.middle()
-    spread.third()
     two_sum.end()
-    spread.complete()
-    own_store.wait()
-    for user in (mixes, one, two, experts, spread, one_sum, two_sum):
+    for user in (mixes, one, two, matrix_in, matrix_out, one_sum, two_sum):
         user.finish()
 
 
 def rear_layer(
-    tokens, lengths, cotangent, gain_one, gain_two, kept, back, mixes, grads, collective_id
+    tokens, lengths, cotangent, gain_one, gain_two, kept, back, mixes, grads_in, grads_out, collective_id
 ):
     rows, width = tokens.shape
     f32, bf16 = jnp.float32, jnp.bfloat16
@@ -1152,7 +1289,7 @@
     dma = pltpu.SemaphoreType.DMA
     shape = jax.ShapeDtypeStruct
     wide_one, wide_two = width + 256, 2 * width + 256
-    slab = grads.shape[0] // 8
+    slabs = (grads_in.shape[1], grads_out.shape[0] // 8)
     inputs = (tokens, cotangent, gain_one, gain_two, *kept, back)
     return pl.pallas_call(
         rear_kernel,
@@ -1161,27 +1298,29 @@
             shape((rows, width), f32),
             shape((64, wide_one), bf16),
             shape((64, wide_two), bf16),
-            shape((8, slab, width), bf16),
+            *(shape((8, slab, width), bf16) for slab in slabs),
         ),
-        in_specs=[pl.BlockSpec(memory_space=pltpu.SMEM)] + [anywhere] * (len(inputs) + 2),
-        out_specs=(vmem,) * 4 + (anywhere,),
+        in_specs=[pl.BlockSpec(memory_space=pltpu.SMEM)] + [anywhere] * (len(inputs) + 3),
+        out_specs=(vmem,) * 4 + (anywhere,) * 2,
         scratch_shapes=[
             *(pltpu.VMEM(value.shape, value.dtype) for value in inputs),
             dma((len(inputs),)),
-            dma,
             pltpu.VMEM((8, rows, width), bf16),
             dma((8,)),
-            *scatter_scratch(rows, width, 96),
+            *scatter_scratch(rows, width, 96, 0),
             pltpu.VMEM((16, 64, wide_one), bf16),
-            *scatter_scratch(64, wide_one, 32),
+            *scatter_scratch(64, wide_one, 32, 0),
             pltpu.VMEM((16, 64, wide_two), bf16),
-            *scatter_scratch(64, wide_two, 32),
-            pltpu.VMEM((8, slab, width), bf16),
-            dma((8,)),
-            *scatter_scratch(slab, width, 96, 1),
-            pltpu.VMEM((slab, width), bf16),
+            *scatter_scratch(64, wide_two, 32, 0),
+            pltpu.VMEM((slabs[0], width), bf16),
+            dma,
+            dma,
+            dma,
+            pltpu.VMEM((slabs[0], width), bf16),
+            dma,
             dma((22,)),
             dma((22,)),
+            *expert_scratch(slabs[1], width),
             *total_scratch(16, wide_one // 2),
             *total_scratch(16, wide_two // 2),
             pltpu.VMEM((64, wide_one), bf16),
@@ -1198,11 +1337,11 @@
         cost_estimate=pl.CostEstimate(
             flops=24 * 10**9, bytes_accessed=10**8, transcendentals=10**6
         ),
-    )(lengths, *inputs, mixes, grads.reshape(8, slab, width))
+    )(lengths, *inputs, mixes, grads_in, grads_out.reshape(8, slabs[1], width))
 
 
 def close_kernel(
-    output_any, d_tokens_any, one_any, two_any, expert_any,
+    output_any, d_tokens_any, one_any, two_any, in_any, out_any,
     output_out, d_tokens_out, d_gain_one_out, d_gain_two_out, d_query_out, d_key_out,
     d_value_out, d_output_out, d_router_out, d_in_out, d_out_out,
     output_ref, d_tokens_ref, one_ref, two_ref, expert_ref, query_ref, key_ref, value_ref,
@@ -1218,7 +1357,10 @@
     loads.add(one_any, one_ref)
     loads.add(two_any, two_ref)
     for span in spans:
-        loads.add(expert_any.at[span], expert_ref.at[span])
+        if span.start < width:
+            loads.add(in_any.at[span], expert_ref.at[span])
+        else:
+            loads.add(out_any.at[pl.ds(span.start - width, 256)], expert_ref.at[span])
     loads.add(output_any, output_ref)
     loads.add(d_tokens_any, d_tokens_ref)
     loads.wait(0, 1)
@@ -1249,10 +1391,10 @@
     stores.wait(*range(9 + parts))
 
 
-def close_layer(output, d_tokens, one, two, expert):
+def close_layer(output, d_tokens, one, two, d_in, d_out):
     rows, width = output.shape
     half = KEY_VALUE_HEADS * HEAD_SIZE
-    hidden = expert.shape[0] - width
+    hidden = d_out.shape[0]
     f32 = jnp.float32
     shape = jax.ShapeDtypeStruct
     small = (
@@ -1269,28 +1411,28 @@
             shape(d_tokens.shape, f32),
             *(shape(extent, f32) for extent in outs),
         ),
-        in_specs=[anywhere] * 5,
+        in_specs=[anywhere] * 6,
         out_specs=(anywhere,) * 11,
         scratch_shapes=[
             pltpu.VMEM(output.shape, output.dtype),
             pltpu.VMEM(d_tokens.shape, f32),
             pltpu.VMEM(one.shape, one.dtype),
             pltpu.VMEM(two.shape, two.dtype),
-            pltpu.VMEM(expert.shape, expert.dtype),
+            pltpu.VMEM((width + hidden, width), d_in.dtype),
             pltpu.VMEM(query, f32),
             pltpu.VMEM(key, f32),
             pltpu.VMEM(value, f32),
             pltpu.VMEM(matrix, f32),
-            pltpu.VMEM(expert.shape, f32),
+            pltpu.VMEM((width + hidden, width), f32),
             pltpu.VMEM(router, f32),
             pltpu.VMEM(gain_one, f32),
             pltpu.VMEM(gain_two, f32),
-            dma((4 + expert.shape[0] // 256,)),
-            dma((9 + expert.shape[0] // 256,)),
+            dma((4 + (width + hidden) // 256,)),
+            dma((9 + (width + hidden) // 256,)),
         ],
         compiler_params=pltpu.CompilerParams(vmem_limit_bytes=62 * 1024 * 1024),
         cost_estimate=pl.CostEstimate(flops=0, bytes_accessed=12 * 10**6, transcendentals=0),
-    )(output, d_tokens, one, two, expert)
+    )(output, d_tokens, one, two, d_in, d_out)
 
 
 def local(
@@ -1313,15 +1455,15 @@
         tokens, seq_lengths, routes, attn_gain, ffn_gain,
         w_query, key_projection, value_projection, w_output, w_router, cotangent, 1,
     )
-    back, mixes, expert_grads = expert_layer(payload, all_cotangent, w_in[0], w_out[0], 2)
-    output, d_tokens, one, two, expert_grads = rear_layer(
+    back, mixes, *grads = expert_layer(payload, all_cotangent, w_in[0], w_out[0], 2)
+    output, d_tokens, one, two, d_in, d_out = rear_layer(
         tokens, seq_lengths, cotangent, attn_gain, ffn_gain, (payload, *kept), back, mixes,
-        expert_grads, 3,
+        *grads, 3,
     )
     (
         output, d_tokens, d_attn_gain, d_ffn_gain, d_query, d_key, d_value, d_output, d_router,
         d_in, d_out,
-    ) = close_layer(output, d_tokens, one, two, expert_grads.reshape(-1, width))
+    ) = close_layer(output, d_tokens, one, two, d_in.reshape(-1, width), d_out.reshape(-1, width))
     return (
         output,
         d_tokens,

time: 242 us -> 232 us (0.959)
  Pallas kernels: 241 us -> 230 us
    pallas_call x1, Pallas kernels: 95.5 us -> 82.2 us  [rear_layer(): pl.pallas_call(rear_kernel, out_shape=(shape((rows, width), bf16), shape(...]
    pallas_call x1, Pallas kernels: 82.3 us -> 85.1 us  [expert_layer(): pl.pallas_call(functools.partial(expert_kernel, cut), out_shape=(jax.Shap...]
where the time goes in v5:
time: 232 us; the launch traced here: 230 us
  Pallas kernels  230 us (99%)
    pallas_call x1, Pallas kernels, expert_layer(): pl.pallas_call(functools.partial(expert_kernel, cut), out_shape=(jax.Shap...  85.1 us
    pallas_call x1, Pallas kernels, rear_layer(): pl.pallas_call(rear_kernel, out_shape=(shape((rows, width), bf16), shape(...  82.2 us
    pallas_call x1, Pallas kernels, front_layer(): pl.pallas_call(front_kernel, out_shape=(*kept, shape((16, rows, width), b...  57.8 us

profile of v5, /device:TPU:8, one launch (start us, length us, event | category | flops | bytes accessed | tf_op | source)
XLA Modules:
  0.0 230.5 jit_solution(5110163022633313125)
XLA Ops:
  0.6 57.8 %shard_map.212 = (bf16[208,1024]{1,0:T(8,128)(2,1)}, f32[192,1024]{1,0:T(8,128)}, bf16[192,1024]{1,0:T(8,128)(2,1)}, bf16[192,2048]{1,0:T(8,128)(2,1)}, bf16[192...) custom-call(bf16[192,1024]{1,0:T(8,128)(2,1)} %tokens_any.3, ...), custom_call_target="tpu_custom_call" | custom-call | flops 24000000000 | bytes 100000000 | tf_op jit(solution)/shard_map/pallas_call | solution.py:741
  58.4 85.1 %shard_map.213 = (f32[208,1024]{1,0:T(8,128)}, bf16[16,192,1024]{2,1,0:T(8,128)(2,1)}, bf16[2,128,1024]{2,1,0:T(8,128)(2,1)}, bf16[512,1024]{1,0:T(8,128)(2,1)}) custom-call(bf16[208,1024]{1,0:T(8,128)(2,1)} %get-tuple-element.44.payload_ref.payload_any, bf16[16,192,1024]{2,1,0:T(8,128)(2,1)} %get-tuple-element.55.mix_ref, bf16[1024,1024]{1,0:T(8,128)(2,1)} %bitcast.15, ...), custom_call_target="tpu_custom_call" | custom-call | flops 24000000000 | bytes 100000000 | tf_op jit(solution)/shard_map/pallas_call | solution.py:327
  143.5 82.2 %shard_map.214 = (bf16[192,1024]{1,0:T(8,128)(2,1)}, f32[192,1024]{1,0:T(8,128)}, bf16[64,1280]{1,0:T(8,128)(2,1)}, bf16[64,2304]{1,0:T(8,128)(2,1)}, bf16[8,128...) custom-call(s32[1,2]{1,0:T(1,128)} %lengths_ref.3, bf16[192,1024]{1,0:T(8,128)(2,1)} %tokens_any.3, ...), custom_call_target="tpu_custom_call" | custom-call | flops 24000000000 | bytes 100000000 | tf_op jit(solution)/shard_map/pallas_call | solution.py:1294
  225.7 4.6 %shard_map.215 = (bf16[192,1024]{1,0:T(8,128)(2,1)}, f32[192,1024]{1,0:T(8,128)}, f32[8,128]{1,0:T(8,128)}, f32[8,128]{1,0:T(8,128)}, f32[64,1024]{1,0:T(8,128)}...) custom-call(bf16[192,1024]{1,0:T(8,128)(2,1)} %get-tuple-element.60., ...), custom_call_target="tpu_custom_call" | custom-call | bytes 12000000 | tf_op jit(solution)/shard_map/pallas_call | solution.py:1407
